TPU v7x, 128 devices: a whole 4x4x4 slice. The times are simulated.
128 devices in a mesh: gx: 8 (over z, core), yz: 16 (over x, y).
Axes of the slice: x: 4, y: 4, z: 4, core: 2. Of those that a mesh axis runs over, the one named last changes fastest.
Arguments:
- resid: bfloat16 [512, 16384], P(None, 'gx'), may hold values from -6 to 6
- queries: bfloat16 [512, 8192], P(None, 'yz'), may hold values from -128 to 128
- new_keys: bfloat16 [512, 512], P(None, 'yz'), may hold values from -4.5 to 4.5
- new_values: bfloat16 [512, 512], P(None, 'yz'), may hold values from -5 to 5
- cache_keys: bfloat16 [512, 384, 512], P(('gx', 'yz')), may hold values from -4.5 to 4.5
- cache_values: bfloat16 [512, 384, 512], P(('gx', 'yz')), may hold values from -5 to 5
- lengths: int32 [512], replicated, may hold values from 1 to 384, as said below
- cache_slot: int32 [512], replicated, may hold values from 0 to 511, as said below
- out_weight: bfloat16 [8192, 16384], P('yz', 'gx'), may hold values from -0.0625 to 0.0625
- norm_gain: float32 [16384], P('gx'), may hold values from 0.1 to 1.9
- gate_weight: bfloat16 [16384, 28672], P('gx', 'yz'), may hold values from -0.046875 to 0.046875
- up_weight: bfloat16 [16384, 28672], P('gx', 'yz'), may hold values from -0.046875 to 0.046875
- down_weight: bfloat16 [28672, 16384], P('yz', 'gx'), may hold values from -0.03125 to 0.03125
Outputs:
- layer_out: bfloat16 [512, 16384], P('yz', 'gx')
Inputs may be any that keep to these rules, and one draw needn't show every extreme that they name: `cache_slot`: each slot number appears once; slot s lies on the device of index s // 4 along gx+yz. `lengths`: cache positions at or past a row's length hold entries that are not part of its context.
All inputs are finite; a program needn't handle non-finite values.
Results may differ from a plain program's by a relative error of at most 0.015.
Values may be sent and summed in bfloat16 or wider, within the bound.
No kernel may reach another device: no remote copies, remote signals or barrier semaphores. Data moves between devices by JAX's collectives and lax.ppermute only.
A program may use at most 128 MiB of HBM per device.

v0:
```python
import jax
import jax.numpy as jnp
from jax import lax
from jax.sharding import PartitionSpec as P

HD = 128
RING = 4
CORES = 2
AXES = ("gx", "yz")
BF16 = jnp.bfloat16
F32 = jnp.float32
FAR_FIRST = (2, 1, 3, 0)


def place(device):
    gx, yz = divmod(device, RING * RING)
    z, core = divmod(gx, CORES)
    x, y = divmod(yz, RING)
    return x, y, z, core


def number(x, y, z, core):
    gx = (z % RING) * CORES + core
    return gx * RING * RING + (x % RING) * RING + y % RING


def pairs(move):
    count = RING * RING * RING * CORES
    return [(d, number(*move(*place(d)))) for d in range(count)]


def send_first(value, step):
    def move(x, y, z, core):
        return (x + step, y, z, core) if core == 0 else (x, y + step, z, core)

    return lax.ppermute(value, AXES, pairs(move))


def send_second(value, step):
    def move(x, y, z, core):
        return (x, y + step, z, core) if core == 0 else (x + step, y, z, core)

    return lax.ppermute(value, AXES, pairs(move))


def send_z(value, step):
    return lax.ppermute(value, AXES, pairs(lambda x, y, z, core: (x, y, z + step, core)))


def send_core(value):
    return lax.ppermute(value, AXES, pairs(lambda x, y, z, core: (x, y, z, 1 - core)))


def spread(send, blocks):
    return [send(blocks[j], j) for j in FAR_FIRST if j != 0]


def collect(send, value):
    got = {0: value}
    for j in (2, 1, 3):
        got[j] = send(value, -j)
    return [got[j] for j in range(RING)]


def add_up(own, others):
    total = own.astype(F32)
    for other in others:
        total = total + other.astype(F32)
    return total


def hi_lo(total):
    high = lax.reduce_precision(total, exponent_bits=8, mantissa_bits=7)
    return high.astype(BF16), (total - high).astype(BF16)


def one_hot_rows(index, count):
    return (index[:, None] == jnp.arange(count, dtype=jnp.int32)[None, :]).astype(BF16)


def pick(matrix, values):
    return jnp.dot(matrix, values, preferred_element_type=F32).astype(BF16)


def attend_slots(query_heads, key_rows, value_rows, cache_keys, cache_values, valid):
    slot_count, positions = cache_keys.shape[:2]
    kv_heads, groups = query_heads.shape[1:3]
    scaling = HD ** (-0.5)
    key_heads = cache_keys.reshape(slot_count, positions, kv_heads, HD)
    value_heads = cache_values.reshape(slot_count, positions, kv_heads, HD)
    scores = (
        jnp.einsum("bkgd,bckd->bkgc", query_heads, key_heads, preferred_element_type=F32) * scaling
    )
    new_score = (
        jnp.einsum("bkgd,bkd->bkg", query_heads, key_rows, preferred_element_type=F32) * scaling
    )
    inside = jnp.arange(positions)[None, :] < valid[:, None]
    scores = jnp.where(inside[:, None, None, :], scores, -jnp.inf)
    largest = jnp.maximum(jnp.max(scores, axis=-1), new_score)
    powers = jnp.exp(scores - largest[..., None])
    power_new = jnp.exp(new_score - largest)
    totals = jnp.sum(powers, axis=-1) + power_new
    weights = (powers / totals[..., None]).astype(BF16)
    weight_new = (power_new / totals).astype(BF16)
    context = jnp.einsum("bkgc,bckd->bkgd", weights, value_heads, preferred_element_type=F32)
    context = context + weight_new.astype(F32)[..., None] * value_rows.astype(F32)[:, :, None, :]
    return context.reshape(slot_count, kv_heads * groups * HD).astype(BF16)


def on_device(
    resid,
    queries,
    new_keys,
    new_values,
    cache_keys,
    cache_values,
    lengths,
    cache_slot,
    out_weight,
    norm_gain,
    gate_weight,
    up_weight,
    down_weight,
):
    index_gx = lax.axis_index("gx")
    index_yz = lax.axis_index("yz")
    count_yz = RING * RING
    count_gx = RING * CORES
    z, core = index_gx // CORES, index_gx % CORES
    x, y = index_yz // RING, index_yz % RING
    rows = resid.shape[0]
    width = resid.shape[1]
    hidden_width = gate_weight.shape[1]
    per_device = cache_keys.shape[0]
    group_slots = per_device * count_yz
    block = rows // count_yz
    kv_heads = cache_keys.shape[2] // HD
    head_width = out_weight.shape[0]
    heads_here = head_width // HD
    new_width = new_keys.shape[1]
    positions = jnp.arange(rows, dtype=jnp.int32)

    slot_here = index_gx * group_slots + jnp.arange(group_slots, dtype=jnp.int32)
    routing = cache_slot[None, :] == slot_here[:, None]
    outgoing = pick(
        routing.astype(BF16), jnp.concatenate([queries, new_keys, new_values], axis=1)
    )
    valid = jnp.sum(jnp.where(routing, lengths[None, :], 0), axis=1)
    valid_own = lax.dynamic_slice_in_dim(valid, index_yz * per_device, per_device)
    arrived = lax.all_to_all(outgoing, "yz", split_axis=0, concat_axis=0, tiled=True)
    arrived = arrived.reshape(count_yz, per_device, head_width + 2 * new_width)
    query_heads = (
        arrived[:, :, :head_width]
        .reshape(count_yz, per_device, heads_here, HD)
        .transpose(1, 0, 2, 3)
        .reshape(per_device, kv_heads, count_yz * heads_here // kv_heads, HD)
    )
    key_rows = (
        arrived[:, :, head_width : head_width + new_width]
        .transpose(1, 0, 2)
        .reshape(per_device, kv_heads, HD)
    )
    value_rows = (
        arrived[:, :, head_width + new_width :].transpose(1, 0, 2).reshape(per_device, kv_heads, HD)
    )
    context = attend_slots(query_heads, key_rows, value_rows, cache_keys, cache_values, valid_own)

    outgoing = context.reshape(per_device, count_yz, head_width).transpose(1, 0, 2)
    outgoing = jnp.broadcast_to(outgoing[None], (count_gx,) + outgoing.shape)
    all_columns = lax.all_to_all(
        outgoing.reshape(count_gx * count_yz, per_device, head_width),
        AXES,
        split_axis=0,
        concat_axis=0,
        tiled=True,
    ).reshape(rows, head_width)

    far, near, inner = positions // (RING * block), (positions // block) % RING, positions % block
    row_x = jnp.where(core == 0, x + far, x + near) % RING
    row_y = jnp.where(core == 0, y + near, y + far) % RING
    row_here = (row_x * RING + row_y) * block + inner
    slot_of = jnp.sum(
        jnp.where(row_here[:, None] == positions[None, :], cache_slot[None, :], 0), axis=1
    )
    context_rows = pick(one_hot_rows(slot_of, rows), all_columns)

    def sum_rows(product):
        chunk = RING * block
        parts = {}
        for j in FAR_FIRST:
            part = product(slice(j * chunk, (j + 1) * chunk))
            parts[j] = part if j == 0 else part.astype(BF16)
        total = add_up(parts[0], spread(send_first, parts))
        parts = {k: total[k * block : (k + 1) * block] for k in range(RING)}
        parts = {k: part if k == 0 else part.astype(BF16) for k, part in parts.items()}
        return add_up(parts[0], spread(send_second, parts))

    attended = sum_rows(
        lambda part: jnp.dot(context_rows[part], out_weight, preferred_element_type=F32)
    )
    own_resid = lax.dynamic_slice_in_dim(resid, index_yz * block, block, 0)
    middle = (own_resid.astype(F32) + attended).astype(BF16)
    mid_float = middle.astype(F32)
    scaled = (mid_float * norm_gain[None, :]).astype(BF16)
    high, low = hi_lo(jnp.sum(mid_float * mid_float, axis=1, keepdims=True))
    tail = [jnp.broadcast_to(part, (block, HD // 2)) for part in (high, low)]
    payload = jnp.concatenate([scaled] + tail, axis=1)

    blocks = jnp.concatenate(collect(send_second, payload), axis=0)
    blocks = jnp.concatenate(collect(send_first, blocks), axis=0)

    half = RING * block // CORES
    target = positions[: RING * half] // half
    distance = jnp.zeros_like(target)
    for order_index, j in enumerate(FAR_FIRST):
        distance = jnp.where(target == order_index, j, distance)
    part_x = (z + distance) % RING
    inner_half = positions[: RING * half] % half

    def half_rows(part_core):
        part_y = part_core * (RING // CORES) + inner_half // block
        source = jnp.where(core == 0, part_x * RING + part_y, part_y * RING + part_x)
        matrix = one_hot_rows(source * block + inner_half % block, rows)
        ends = jnp.dot(matrix, blocks[:, width:], preferred_element_type=F32)
        return pick(matrix, blocks[:, :width]), ends[:, : HD // 2] + ends[:, HD // 2 :]

    other_rows, other_squares = half_rows(1 - core)
    own_rows, own_squares = half_rows(core)
    squares = own_squares + send_core(other_squares)
    weights = (gate_weight, up_weight)
    given = [send_core(pick(other_rows, weight)) for weight in weights]
    sums = []
    for weight, gift in zip(weights, given):
        parts = {}
        for pair in range(RING // 2):
            span = slice(pair * 2 * half, (pair + 1) * 2 * half)
            both = jnp.dot(own_rows[span], weight, preferred_element_type=F32)
            both = both + gift[span].astype(F32)
            for i in range(2):
                j = FAR_FIRST[pair * 2 + i]
                part = both[i * half : (i + 1) * half]
                parts[j] = part if j == 0 else part.astype(BF16)
        sums.append(parts)
    square_parts = {j: squares[i * half : (i + 1) * half] for i, j in enumerate(FAR_FIRST)}
    squares = add_up(square_parts[0], spread(send_z, square_parts))
    gate, upper = [add_up(parts[0], spread(send_z, parts)) for parts in sums]
    factor = lax.rsqrt(squares[:, :1] / (width * count_gx) + 1e-05)
    gate = gate * factor
    hidden = (jax.nn.silu(gate) * (upper * factor)).astype(BF16)

    own_hidden = collect(send_z, hidden)
    other_hidden = [send_core(part) for part in own_hidden]
    all_hidden = jnp.concatenate(own_hidden + other_hidden, axis=0)
    place_x = jnp.where(core == 0, far, near)
    place_y = jnp.where(core == 0, near, far)
    place_core = (place_y // (RING // CORES) + core) % CORES
    place_z = (place_x - z) % RING
    place_here = (place_core * RING + place_z) * half + (place_y % (RING // CORES)) * block + inner
    hidden_rows = pick(one_hot_rows(place_here, rows), all_hidden)
    projected = sum_rows(
        lambda part: jnp.dot(hidden_rows[part], down_weight, preferred_element_type=F32)
    )
    return (mid_float + projected).astype(BF16)


def solution(mesh):
    in_specs = (
        P(None, "gx"),
        P(None, "yz"),
        P(None, "yz"),
        P(None, "yz"),
        P(("gx", "yz"), None, None),
        P(("gx", "yz"), None, None),
        P(),
        P(),
        P("yz", "gx"),
        P("gx"),
        P("gx", "yz"),
        P("gx", "yz"),
        P("yz", "gx"),
    )
    out_specs = P("yz", "gx")
    return jax.shard_map(
        on_device, mesh=mesh, in_specs=in_specs, out_specs=out_specs, check_vma=False
    )
```

profile of v0, /device:TPU:6, one launch (start us, length us, event | category | flops | bytes accessed | tf_op | source)
XLA Modules:
  0.0 198.4 jit_solution(18271431025305966279)
XLA Ops:
  0.0 1.0 copy.34
  1.1 0.9 copy.35
  1.9 1.3 convolution_convert_fusion.12
  3.9 7.4 %all-to-all-start = ((bf16[16,4,576]{2,1,0:T(4,128)(2,1)}), bf16[16,4,576]{2,1,0:T(4,128)(2,1)S(1)}, u32[]{:S(2)}, u32[]{:S(2)}) async-start(bf16[16,4,576]{2,1,0:T(4,128)(2,1)} %all_to_all.9), calls=%async_computation | async-start | bytes 163840 | tf_op jit(solution)/shard_map/all_to_all | solution.py:150
  11.7 5.3 %all-to-all-done = bf16[16,4,576]{2,1,0:T(4,128)(2,1)S(1)} async-done(((bf16[16,4,576]{2,1,0:T(4,128)(2,1)}), bf16[16,4,576]{2,1,0:T(4,128)(2,1)S(1)}, u32[]{:S(2)}, u32[]{:S(2)}) %all-to-all-start) | async-done | bytes 73760 | tf_op jit(solution)/shard_map/all_to_all | solution.py:150
  17.5 2.2 %fusion.126 = (f32[4,4,16]{2,1,0:T(4,128)S(1)}, f32[4,4,16,384]{3,2,1,0:T(8,128)S(1)}) fusion(bf16[4,4,16,128]{3,2,1,0:T(8,128)(2,1)S(1)} %bitcast.67, pred[4,384]{1,0:T(4,128)(4,1)S(1)} %iota_compare_fusion.11, bf16[4,384,512]{2,1,0:T(8,128)(2,1)} %param.17), kind=kOutput, calls=%fused_computation.232 | convolution fusion | flops 25460480 | bytes 2034176 | tf_op jit(solution)/shard_map/bkgd,bckd->bkgc/dot_general | solution.py:92
  20.6 1.0 broadcast_in_dim.53
  21.6 8.6 %all-to-all-start.1 = ((bf16[128,4,512]{2,1,0:T(4,128)(2,1)}), bf16[128,4,512]{2,1,0:T(4,128)(2,1)S(1)}, u32[]{:S(2)}, u32[]{:S(2)}) async-start(bf16[128,4,512]{2,1,0:T(4,128)(2,1)} %bitcast.8), calls=%async_computation.1 | async-start | bytes 1048576 | tf_op jit(solution)/shard_map/all_to_all | solution.py:170
  30.5 11.6 %all-to-all-done.1 = bf16[128,4,512]{2,1,0:T(4,128)(2,1)S(1)} async-done(((bf16[128,4,512]{2,1,0:T(4,128)(2,1)}), bf16[128,4,512]{2,1,0:T(4,128)(2,1)S(1)}, u32[]{:S(2)}, u32[]{:S(2)}) %all-to-all-start.1) | async-done | bytes 524320 | tf_op jit(solution)/shard_map/all_to_all | solution.py:170
  43.7 1.2 convolution_convert_fusion.10
  44.9 2.8 %collective-permute-start = (bf16[128,2048]{1,0:T(8,128)(2,1)}, bf16[128,2048]{1,0:T(8,128)(2,1)}, u32[]{:S(2)}, u32[]{:S(2)}) collective-permute-start(bf16[128,2048]{1,0:T(8,128)(2,1)} %convolution_convert_fusion.10), channel_id=1, source_target_pairs={{0,8},{1,9},{2,10},{3,11},{4,12},{5,13},{6,14},{7,15},{8,0},{9,1},... | collective-permute-start | bytes 1572872 | tf_op jit(solution)/shard_map/ppermute | solution.py:36
  48.5 1.1 collective-permute-start.2
  50.3 5.7 %collective-permute-done = bf16[128,2048]{1,0:T(8,128)(2,1)} collective-permute-done((bf16[128,2048]{1,0:T(8,128)(2,1)}, bf16[128,2048]{1,0:T(8,128)(2,1)}, u32[]{:S(2)}, u32[]{:S(2)}) %collective-permute-start) | collective-permute-done | bytes 524320 | tf_op jit(solution)/shard_map/ppermute | solution.py:36
  56.0 5.6 %collective-permute-done.1 = bf16[128,2048]{1,0:T(8,128)(2,1)} collective-permute-done((bf16[128,2048]{1,0:T(8,128)(2,1)S(1)}, bf16[128,2048]{1,0:T(8,128)(2,1)}, u32[]{:S(2)}, u32[]{:S(2)}) %collective-permute-start.1) | collective-permute-done | bytes 524320 | tf_op jit(solution)/shard_map/ppermute | solution.py:36
  61.6 2.0 %fusion.127 = (bf16[128,2048]{1,0:T(8,128)(2,1)S(1)}, f32[128,2048]{1,0:T(8,128)S(1)}) fusion(bf16[128,2048]{1,0:T(8,128)(2,1)} %collective-permute-done.2, bf16[128,2048]{1,0:T(8,128)(2,1)} %collective-permute-done.1, bf16[128,2048]{1,0:T(8,128)(2,1)} %collective-permute-done, bf16[512,2048]{1,0:T(8,128)(2,1)S(1)} %copy-done, bf16[512,512]{1,0:T(8,128)(2,1)} %copy-done.2), kind=kOutput, calls=%fused_computation.233 | convolution fusion | flops 270270464 | bytes 5373952 | tf_op jit(solution)/shard_map/dot_general | solution.py:199
  63.7 1.4 collective-permute-start.3
  65.1 2.0 %collective-permute-start.5 = (bf16[32,2048]{1,0:T(8,128)(2,1)S(1)}, bf16[32,2048]{1,0:T(8,128)(2,1)S(1)}, u32[]{:S(2)}, u32[]{:S(2)}) collective-permute-start(bf16[32,2048]{1,0:T(8,128)(2,1)S(1)} %get-tuple-element.21), channel_id=1, source_target_pairs={{0,3},{1,0},{2,1},{3,2},{4,7},{5,4},{6,5},{7,6},{8,11},{9,8},{10,9... | collective-permute-start | bytes 393224 | tf_op jit(solution)/shard_map/ppermute | solution.py:43
  67.7 2.5 %collective-permute-done.3 = bf16[32,2048]{1,0:T(8,128)(2,1)S(1)} collective-permute-done((bf16[32,2048]{1,0:T(8,128)(2,1)S(1)}, bf16[32,2048]{1,0:T(8,128)(2,1)S(1)}, u32[]{:S(2)}, u32[]{:S(2)}) %collective-permute-start.3) | collective-permute-done | bytes 131104 | tf_op jit(solution)/shard_map/ppermute | solution.py:43
  70.8 2.5 %collective-permute-done.4 = bf16[32,2048]{1,0:T(8,128)(2,1)S(1)} collective-permute-done((bf16[32,2048]{1,0:T(8,128)(2,1)S(1)}, bf16[32,2048]{1,0:T(8,128)(2,1)S(1)}, u32[]{:S(2)}, u32[]{:S(2)}) %collective-permute-start.4) | collective-permute-done | bytes 131104 | tf_op jit(solution)/shard_map/ppermute | solution.py:43
  73.3 1.1 fusion.54
  75.2 0.9 concatenate.17
  76.3 1.6 collective-permute-start.7
  77.9 1.6 collective-permute-start.6
  79.5 4.5 %collective-permute-done.8 = bf16[32,2176]{1,0:T(8,128)(2,1)S(1)} collective-permute-done((bf16[32,2176]{1,0:T(8,128)(2,1)S(1)}, bf16[32,2176]{1,0:T(8,128)(2,1)S(1)}, u32[]{:S(2)}, u32[]{:S(2)}) %collective-permute-start.8) | collective-permute-done | bytes 139296 | tf_op jit(solution)/shard_map/ppermute | solution.py:43
  84.0 0.9 collective-permute-done.6
  85.0 3.1 %collective-permute-start.11 = (bf16[128,2176]{1,0:T(8,128)(2,1)S(1)}, bf16[128,2176]{1,0:T(8,128)(2,1)S(1)}, u32[]{:S(2)}, u32[]{:S(2)}) collective-permute-start(bf16[128,2176]{1,0:T(8,128)(2,1)S(1)} %pad_maximum_fusion), channel_id=1, source_target_pairs={{0,4},{1,5},{2,6},{3,7},{4,8},{5,9},{6,10},{7,11},{8,12},{9,13},{1... | collective-permute-start | bytes 1671176 | tf_op jit(solution)/shard_map/ppermute | solution.py:36
  88.0 1.0 collective-permute-start.10
  89.8 15.2 %collective-permute-done.9 = bf16[128,2176]{1,0:T(8,128)(2,1)S(1)} collective-permute-done((bf16[128,2176]{1,0:T(8,128)(2,1)S(1)}, bf16[128,2176]{1,0:T(8,128)(2,1)S(1)}, u32[]{:S(2)}, u32[]{:S(2)}) %collective-permute-start.9) | collective-permute-done | bytes 557088 | tf_op jit(solution)/shard_map/ppermute | solution.py:36
  107.4 2.1 %convolution_convert_fusion.1 = bf16[256,1792]{1,0:T(8,128)(2,1)S(1)} fusion(bf16[256,2048]{1,0:T(8,128)(2,1)S(1)} %convolution_convert_fusion.3, bf16[2048,1792]{1,0:T(8,128)(2,1)S(1)} %bitcast.65), kind=kOutput, calls=%fused_computation.1 | convolution fusion | flops 1879506944 | bytes 9306112 | tf_op jit(solution)/shard_map/dot_general | solution.py:82
  109.8 2.1 %convolution_convert_fusion.2 = bf16[256,1792]{1,0:T(8,128)(2,1)S(1)} fusion(bf16[256,2048]{1,0:T(8,128)(2,1)S(1)} %convolution_convert_fusion.3, bf16[2048,1792]{1,0:T(8,128)(2,1)S(1)} %bitcast.63), kind=kOutput, calls=%fused_computation.2 | convolution fusion | flops 1879506944 | bytes 9306112 | tf_op jit(solution)/shard_map/dot_general | solution.py:82
  111.9 1.1 fusion.33
  113.0 1.1 fusion.35
  115.6 1.2 collective-permute-done.16
  117.6 1.3 collective-permute-start.18
  119.8 1.2 add_convert_fusion.1
  121.1 2.7 %collective-permute-start.15 = (bf16[64,1792]{1,0:T(8,128)(2,1)S(1)}, bf16[64,1792]{1,0:T(8,128)(2,1)S(1)}, u32[]{:S(2)}, u32[]{:S(2)}) collective-permute-start(bf16[64,1792]{1,0:T(8,128)(2,1)S(1)} %slice.374), channel_id=1, source_target_pairs={{0,96},{1,97},{2,98},{3,99},{4,100},{5,101},{6,102},{7,103},{8,104... | collective-permute-start | bytes 688136 | tf_op jit(solution)/shard_map/ppermute | solution.py:47
  123.8 1.4 collective-permute-start.13
  125.3 1.2 add_convert_fusion
  127.0 3.1 %collective-permute-start.23 = (bf16[64,1792]{1,0:T(8,128)(2,1)S(1)}, bf16[64,1792]{1,0:T(8,128)(2,1)S(1)}, u32[]{:S(2)}, u32[]{:S(2)}) collective-permute-start(bf16[64,1792]{1,0:T(8,128)(2,1)S(1)} %slice.373), channel_id=1, source_target_pairs={{0,96},{1,97},{2,98},{3,99},{4,100},{5,101},{6,102},{7,103},{8,104... | collective-permute-start | bytes 688136 | tf_op jit(solution)/shard_map/ppermute | solution.py:47
  130.1 1.0 collective-permute-start.21
  131.1 1.9 collective-permute-done.15
  133.0 2.0 %collective-permute-start.22 = (bf16[64,1792]{1,0:T(8,128)(2,1)S(1)}, bf16[64,1792]{1,0:T(8,128)(2,1)S(1)}, u32[]{:S(2)}, u32[]{:S(2)}) collective-permute-start(bf16[64,1792]{1,0:T(8,128)(2,1)S(1)} %get-tuple-element.26), channel_id=1, source_target_pairs={{0,32},{1,33},{2,34},{3,35},{4,36},{5,37},{6,38},{7,39},{8,40},{9,... | collective-permute-start | bytes 688136 | tf_op jit(solution)/shard_map/ppermute | solution.py:47
  135.0 6.6 %collective-permute-done.14 = bf16[64,1792]{1,0:T(8,128)(2,1)S(1)} collective-permute-done((bf16[64,1792]{1,0:T(8,128)(2,1)S(1)}, bf16[64,1792]{1,0:T(8,128)(2,1)S(1)}, u32[]{:S(2)}, u32[]{:S(2)}) %collective-permute-start.14) | collective-permute-done | bytes 229408 | tf_op jit(solution)/shard_map/ppermute | solution.py:47
  141.6 1.3 collective-permute-done.23
  142.9 0.9 collective-permute-done.21
  143.8 2.9 %collective-permute-done.22 = bf16[64,1792]{1,0:T(8,128)(2,1)S(1)} collective-permute-done((bf16[64,1792]{1,0:T(8,128)(2,1)S(1)}, bf16[64,1792]{1,0:T(8,128)(2,1)S(1)}, u32[]{:S(2)}, u32[]{:S(2)}) %collective-permute-start.22) | collective-permute-done | bytes 229408 | tf_op jit(solution)/shard_map/ppermute | solution.py:47
  147.1 2.0 %collective-permute-start.25 = (bf16[64,1792]{1,0:T(8,128)(2,1)S(1)}, bf16[64,1792]{1,0:T(8,128)(2,1)S(1)}, u32[]{:S(2)}, u32[]{:S(2)}) collective-permute-start(bf16[64,1792]{1,0:T(8,128)(2,1)S(1)} %get-tuple-element.6), channel_id=1, source_target_pairs={{0,64},{1,65},{2,66},{3,67},{4,68},{5,69},{6,70},{7,71},{8,72},{9,... | collective-permute-start | bytes 688136 | tf_op jit(solution)/shard_map/ppermute | solution.py:47
  149.1 1.9 collective-permute-start.24
  151.2 8.7 %collective-permute-done.26 = bf16[64,1792]{1,0:T(8,128)(2,1)S(1)} collective-permute-done((bf16[64,1792]{1,0:T(8,128)(2,1)S(1)}, bf16[64,1792]{1,0:T(8,128)(2,1)S(1)}, u32[]{:S(2)}, u32[]{:S(2)}) %collective-permute-start.26) | collective-permute-done | bytes 229408 | tf_op jit(solution)/shard_map/ppermute | solution.py:47
  160.7 1.4 collective-permute-done.28
  162.2 1.2 convolution_convert_fusion
  164.1 1.1 convolution_convert_fusion.5
  165.2 1.1 convolution_convert_fusion.6
  166.3 1.1 convolution_convert_fusion.7
  167.4 1.1 collective-permute-start.31
  168.5 1.2 collective-permute-start.32
  170.5 7.8 %collective-permute-done.31 = bf16[128,2048]{1,0:T(8,128)(2,1)S(1)} collective-permute-done((bf16[128,2048]{1,0:T(8,128)(2,1)S(1)}, bf16[128,2048]{1,0:T(8,128)(2,1)S(1)}, u32[]{:S(2)}, u32[]{:S(2)}) %collective-permute-start.31) | collective-permute-done | bytes 524320 | tf_op jit(solution)/shard_map/ppermute | solution.py:36
  178.3 3.5 %collective-permute-done.32 = bf16[128,2048]{1,0:T(8,128)(2,1)S(1)} collective-permute-done((bf16[128,2048]{1,0:T(8,128)(2,1)S(1)}, bf16[128,2048]{1,0:T(8,128)(2,1)S(1)}, u32[]{:S(2)}, u32[]{:S(2)}) %collective-permute-start.32) | collective-permute-done | bytes 524320 | tf_op jit(solution)/shard_map/ppermute | solution.py:36
  181.8 2.0 %collective-permute-done.33 = bf16[128,2048]{1,0:T(8,128)(2,1)S(1)} collective-permute-done((bf16[128,2048]{1,0:T(8,128)(2,1)S(1)}, bf16[128,2048]{1,0:T(8,128)(2,1)S(1)}, u32[]{:S(2)}, u32[]{:S(2)}) %collective-permute-start.33) | collective-permute-done | bytes 524320 | tf_op jit(solution)/shard_map/ppermute | solution.py:36
  183.8 1.6 fusion.128
  185.4 3.6 %collective-permute-start.34 = (bf16[32,2048]{1,0:T(8,128)(2,1)S(1)}, bf16[32,2048]{1,0:T(8,128)(2,1)S(1)}, u32[]{:S(2)}, u32[]{:S(2)}) collective-permute-start(bf16[32,2048]{1,0:T(8,128)(2,1)S(1)} %get-tuple-element.17), channel_id=1, source_target_pairs={{0,2},{1,3},{2,0},{3,1},{4,6},{5,7},{6,4},{7,5},{8,10},{9,11},{10,... | collective-permute-start | bytes 393224 | tf_op jit(solution)/shard_map/ppermute | solution.py:43
  189.1 2.5 %collective-permute-start.36 = (bf16[32,2048]{1,0:T(8,128)(2,1)S(1)}, bf16[32,2048]{1,0:T(8,128)(2,1)S(1)}, u32[]{:S(2)}, u32[]{:S(2)}) collective-permute-start(bf16[32,2048]{1,0:T(8,128)(2,1)S(1)} %get-tuple-element.18), channel_id=1, source_target_pairs={{0,3},{1,0},{2,1},{3,2},{4,7},{5,4},{6,5},{7,6},{8,11},{9,8},{10,9... | collective-permute-start | bytes 393224 | tf_op jit(solution)/shard_map/ppermute | solution.py:43
  192.0 2.0 %collective-permute-done.36 = bf16[32,2048]{1,0:T(8,128)(2,1)S(1)} collective-permute-done((bf16[32,2048]{1,0:T(8,128)(2,1)S(1)}, bf16[32,2048]{1,0:T(8,128)(2,1)S(1)}, u32[]{:S(2)}, u32[]{:S(2)}) %collective-permute-start.36) | collective-permute-done | bytes 131104 | tf_op jit(solution)/shard_map/ppermute | solution.py:43
  194.0 3.7 %collective-permute-done.35 = bf16[32,2048]{1,0:T(8,128)(2,1)S(1)} collective-permute-done((bf16[32,2048]{1,0:T(8,128)(2,1)S(1)}, bf16[32,2048]{1,0:T(8,128)(2,1)S(1)}, u32[]{:S(2)}, u32[]{:S(2)}) %collective-permute-start.35) | collective-permute-done | bytes 131104 | tf_op jit(solution)/shard_map/ppermute | solution.py:43
  (132 shorter events, 18.7 us)
Async XLA Ops:
  0.0 42.7 %copy-start = (bf16[512,2048]{1,0:T(8,128)(2,1)S(1)}, bf16[512,2048]{1,0:T(8,128)(2,1)}, u32[]{:S(2)}) copy-start(bf16[512,2048]{1,0:T(8,128)(2,1)} %param.21) | copy-start | bytes 6291460
  0.0 11.4 %copy-start.4 = (s32[512]{0:T(512)S(1)}, s32[512]{0:T(512)}, u32[]{:S(2)}) copy-start(s32[512]{0:T(512)} %param.20) | copy-start | bytes 6148
  0.0 11.4 %copy-start.5 = (s32[512]{0:T(512)S(1)}, s32[512]{0:T(512)}, u32[]{:S(2)}) copy-start(s32[512]{0:T(512)} %param.19) | copy-start | bytes 6148
  3.9 13.1 %all-to-all-start = ((bf16[16,4,576]{2,1,0:T(4,128)(2,1)}), bf16[16,4,576]{2,1,0:T(4,128)(2,1)S(1)}, u32[]{:S(2)}, u32[]{:S(2)}) async-start(bf16[16,4,576]{2,1,0:T(4,128)(2,1)} %all_to_all.9), calls=%async_computation | async-start | bytes 163840 | tf_op jit(solution)/shard_map/all_to_all | solution.py:150
  17.4 2.7 %copy-start.8 = (bf16[4,384,512]{2,1,0:T(8,128)(2,1)S(1)}, bf16[4,384,512]{2,1,0:T(8,128)(2,1)}, u32[]{:S(2)}) copy-start(bf16[4,384,512]{2,1,0:T(8,128)(2,1)} %param.18) | copy-start | bytes 4718596
  21.6 20.5 %all-to-all-start.1 = ((bf16[128,4,512]{2,1,0:T(4,128)(2,1)}), bf16[128,4,512]{2,1,0:T(4,128)(2,1)S(1)}, u32[]{:S(2)}, u32[]{:S(2)}) async-start(bf16[128,4,512]{2,1,0:T(4,128)(2,1)} %bitcast.8), calls=%async_computation.1 | async-start | bytes 1048576 | tf_op jit(solution)/shard_map/all_to_all | solution.py:170
  42.7 5.8 %copy-start.2 = (bf16[512,512]{1,0:T(8,128)(2,1)}, bf16[512,512]{1,0:T(8,128)(2,1)S(1)}, u32[]{:S(2)}) copy-start(bf16[512,512]{1,0:T(8,128)(2,1)S(1)} %convolution_convert_fusion.11) | copy-start | bytes 1572868
  44.9 11.1 %collective-permute-start = (bf16[128,2048]{1,0:T(8,128)(2,1)}, bf16[128,2048]{1,0:T(8,128)(2,1)}, u32[]{:S(2)}, u32[]{:S(2)}) collective-permute-start(bf16[128,2048]{1,0:T(8,128)(2,1)} %convolution_convert_fusion.10), channel_id=1, source_target_pairs={{0,8},{1,9},{2,10},{3,11},{4,12},{5,13},{6,14},{7,15},{8,0},{9,1},... | collective-permute-start | bytes 1572872 | tf_op jit(solution)/shard_map/ppermute | solution.py:36
  47.7 14.0 %collective-permute-start.1 = (bf16[128,2048]{1,0:T(8,128)(2,1)S(1)}, bf16[128,2048]{1,0:T(8,128)(2,1)}, u32[]{:S(2)}, u32[]{:S(2)}) collective-permute-start(bf16[128,2048]{1,0:T(8,128)(2,1)S(1)} %convolution_convert_fusion.9), channel_id=1, source_target_pairs={{0,4},{1,5},{2,6},{3,7},{4,8},{5,9},{6,10},{7,11},{8,12},{9,13},{1... | collective-permute-start | bytes 1572872 | tf_op jit(solution)/shard_map/ppermute | solution.py:36
  48.5 13.1 %collective-permute-start.2 = (bf16[128,2048]{1,0:T(8,128)(2,1)S(1)}, bf16[128,2048]{1,0:T(8,128)(2,1)}, u32[]{:S(2)}, u32[]{:S(2)}) collective-permute-start(bf16[128,2048]{1,0:T(8,128)(2,1)S(1)} %convolution_convert_fusion.8), channel_id=1, source_target_pairs={{0,12},{1,13},{2,14},{3,15},{4,0},{5,1},{6,2},{7,3},{8,4},{9,5},{1... | collective-permute-start | bytes 1572872 | tf_op jit(solution)/shard_map/ppermute | solution.py:36
  50.3 24.1 %copy-start.3 = (f32[2048]{0:T(1024)S(1)}, f32[2048]{0:T(1024)}, u32[]{:S(2)}) copy-start(f32[2048]{0:T(1024)} %param.22) | copy-start | bytes 24580
  63.7 6.6 %collective-permute-start.3 = (bf16[32,2048]{1,0:T(8,128)(2,1)S(1)}, bf16[32,2048]{1,0:T(8,128)(2,1)S(1)}, u32[]{:S(2)}, u32[]{:S(2)}) collective-permute-start(bf16[32,2048]{1,0:T(8,128)(2,1)S(1)} %get-tuple-element.20), channel_id=1, source_target_pairs={{0,2},{1,3},{2,0},{3,1},{4,6},{5,7},{6,4},{7,5},{8,10},{9,11},{10,... | collective-permute-start | bytes 393224 | tf_op jit(solution)/shard_map/ppermute | solution.py:43
  65.1 5.7 %collective-permute-start.5 = (bf16[32,2048]{1,0:T(8,128)(2,1)S(1)}, bf16[32,2048]{1,0:T(8,128)(2,1)S(1)}, u32[]{:S(2)}, u32[]{:S(2)}) collective-permute-start(bf16[32,2048]{1,0:T(8,128)(2,1)S(1)} %get-tuple-element.21), channel_id=1, source_target_pairs={{0,3},{1,0},{2,1},{3,2},{4,7},{5,4},{6,5},{7,6},{8,11},{9,8},{10,9... | collective-permute-start | bytes 393224 | tf_op jit(solution)/shard_map/ppermute | solution.py:43
  67.1 6.2 %collective-permute-start.4 = (bf16[32,2048]{1,0:T(8,128)(2,1)S(1)}, bf16[32,2048]{1,0:T(8,128)(2,1)S(1)}, u32[]{:S(2)}, u32[]{:S(2)}) collective-permute-start(bf16[32,2048]{1,0:T(8,128)(2,1)S(1)} %get-tuple-element.22), channel_id=1, source_target_pairs={{0,1},{1,2},{2,3},{3,0},{4,5},{5,6},{6,7},{7,4},{8,9},{9,10},{10,1... | collective-permute-start | bytes 393224 | tf_op jit(solution)/shard_map/ppermute | solution.py:43
  75.2 31.6 %slice-start.4 = ((s8[7340032]{0:T(1024)(128)(4,1)}), s8[3145728]{0:T(1024)(128)(4,1)S(1)}, s32[]{:S(2)}) async-start(s8[7340032]{0:T(1024)(128)(4,1)} %bitcast.64), calls=%async_computation.6 | async-start | bytes 6291456
  76.2 7.8 %collective-permute-start.8 = (bf16[32,2176]{1,0:T(8,128)(2,1)S(1)}, bf16[32,2176]{1,0:T(8,128)(2,1)S(1)}, u32[]{:S(2)}, u32[]{:S(2)}) collective-permute-start(bf16[32,2176]{1,0:T(8,128)(2,1)S(1)} %concatenate.17), channel_id=1, source_target_pairs={{0,1},{1,2},{2,3},{3,0},{4,5},{5,6},{6,7},{7,4},{8,9},{9,10},{10,1... | collective-permute-start | bytes 417800 | tf_op jit(solution)/shard_map/ppermute | solution.py:43
  76.3 7.7 %collective-permute-start.7 = (bf16[32,2176]{1,0:T(8,128)(2,1)S(1)}, bf16[32,2176]{1,0:T(8,128)(2,1)S(1)}, u32[]{:S(2)}, u32[]{:S(2)}) collective-permute-start(bf16[32,2176]{1,0:T(8,128)(2,1)S(1)} %concatenate.17), channel_id=1, source_target_pairs={{0,2},{1,3},{2,0},{3,1},{4,6},{5,7},{6,4},{7,5},{8,10},{9,11},{10,... | collective-permute-start | bytes 417800 | tf_op jit(solution)/shard_map/ppermute | solution.py:43
  77.9 7.0 %collective-permute-start.6 = (bf16[32,2176]{1,0:T(8,128)(2,1)S(1)}, bf16[32,2176]{1,0:T(8,128)(2,1)S(1)}, u32[]{:S(2)}, u32[]{:S(2)}) collective-permute-start(bf16[32,2176]{1,0:T(8,128)(2,1)S(1)} %concatenate.17), channel_id=1, source_target_pairs={{0,3},{1,0},{2,1},{3,2},{4,7},{5,4},{6,5},{7,6},{8,11},{9,8},{10,9... | collective-permute-start | bytes 417800 | tf_op jit(solution)/shard_map/ppermute | solution.py:43
  84.9 20.3 %copy-start.6 = (s32[256]{0:T(256)S(1)}, s32[256]{0:T(256)}, u32[]{:S(2)}) copy-start(s32[256]{0:T(256)} %multiply_add_fusion.1) | copy-start | bytes 3076
  85.0 20.2 %collective-permute-start.11 = (bf16[128,2176]{1,0:T(8,128)(2,1)S(1)}, bf16[128,2176]{1,0:T(8,128)(2,1)S(1)}, u32[]{:S(2)}, u32[]{:S(2)}) collective-permute-start(bf16[128,2176]{1,0:T(8,128)(2,1)S(1)} %pad_maximum_fusion), channel_id=1, source_target_pairs={{0,4},{1,5},{2,6},{3,7},{4,8},{5,9},{6,10},{7,11},{8,12},{9,13},{1... | collective-permute-start | bytes 1671176 | tf_op jit(solution)/shard_map/ppermute | solution.py:36
  88.0 17.1 %collective-permute-start.10 = (bf16[128,2176]{1,0:T(8,128)(2,1)S(1)}, bf16[128,2176]{1,0:T(8,128)(2,1)S(1)}, u32[]{:S(2)}, u32[]{:S(2)}) collective-permute-start(bf16[128,2176]{1,0:T(8,128)(2,1)S(1)} %pad_maximum_fusion), channel_id=1, source_target_pairs={{0,8},{1,9},{2,10},{3,11},{4,12},{5,13},{6,14},{7,15},{8,0},{9,1},... | collective-permute-start | bytes 1671176 | tf_op jit(solution)/shard_map/ppermute | solution.py:36
  89.0 16.0 %collective-permute-start.9 = (bf16[128,2176]{1,0:T(8,128)(2,1)S(1)}, bf16[128,2176]{1,0:T(8,128)(2,1)S(1)}, u32[]{:S(2)}, u32[]{:S(2)}) collective-permute-start(bf16[128,2176]{1,0:T(8,128)(2,1)S(1)} %pad_maximum_fusion), channel_id=1, source_target_pairs={{0,12},{1,13},{2,14},{3,15},{4,0},{5,1},{6,2},{7,3},{8,4},{9,5},{1... | collective-permute-start | bytes 1671176 | tf_op jit(solution)/shard_map/ppermute | solution.py:36
  105.2 0.9 copy-start.7
  105.2 2.2 %slice-start.5 = ((s8[7340032]{0:T(1024)(128)(4,1)}), s8[4194304]{0:T(1024)(128)(4,1)S(1)}, s32[]{:S(2)}) async-start(s8[7340032]{0:T(1024)(128)(4,1)} %bitcast.64), calls=%async_computation.7 | async-start | bytes 8388608
  106.0 3.5 %slice-start.2 = ((s8[7340032]{0:T(1024)(128)(4,1)}), s8[4194304]{0:T(1024)(128)(4,1)S(1)}, s32[]{:S(2)}) async-start(s8[7340032]{0:T(1024)(128)(4,1)} %bitcast.62), calls=%async_computation.4 | async-start | bytes 8388608
  107.4 2.3 %slice-start.3 = ((s8[7340032]{0:T(1024)(128)(4,1)}), s8[3145728]{0:T(1024)(128)(4,1)S(1)}, s32[]{:S(2)}) async-start(s8[7340032]{0:T(1024)(128)(4,1)} %bitcast.62), calls=%async_computation.5 | async-start | bytes 6291456
  114.2 5.7 %collective-permute-start.12 = (bf16[256,1792]{1,0:T(8,128)(2,1)S(1)}, bf16[256,1792]{1,0:T(8,128)(2,1)S(1)}, u32[]{:S(2)}, u32[]{:S(2)}) collective-permute-start(bf16[256,1792]{1,0:T(8,128)(2,1)S(1)} %convolution_convert_fusion.2), channel_id=1, source_target_pairs={{0,16},{1,17},{2,18},{3,19},{4,20},{5,21},{6,22},{7,23},{8,24},{9,... | collective-permute-start | bytes 2752520 | tf_op jit(solution)/shard_map/ppermute | solution.py:51
  114.6 2.2 %collective-permute-start.16 = (f32[256,64]{0,1:T(8,128)S(1)}, f32[256,64]{0,1:T(8,128)S(1)}, u32[]{:S(2)}, u32[]{:S(2)}) collective-permute-start(f32[256,64]{0,1:T(8,128)S(1)} %slice_add_fusion.4), channel_id=1, source_target_pairs={{0,16},{1,17},{2,18},{3,19},{4,20},{5,21},{6,22},{7,23},{8,24},{9,... | collective-permute-start | bytes 196616 | tf_op jit(solution)/shard_map/ppermute | solution.py:51
  115.5 8.4 %collective-permute-start.20 = (bf16[256,1792]{1,0:T(8,128)(2,1)S(1)}, bf16[256,1792]{1,0:T(8,128)(2,1)S(1)}, u32[]{:S(2)}, u32[]{:S(2)}) collective-permute-start(bf16[256,1792]{1,0:T(8,128)(2,1)S(1)} %convolution_convert_fusion.1), channel_id=1, source_target_pairs={{0,16},{1,17},{2,18},{3,19},{4,20},{5,21},{6,22},{7,23},{8,24},{9,... | collective-permute-start | bytes 2752520 | tf_op jit(solution)/shard_map/ppermute | solution.py:51
  116.9 9.7 %collective-permute-start.19 = (f32[64,64]{0,1:T(8,128)S(1)}, f32[64,64]{0,1:T(8,128)S(1)}, u32[]{:S(2)}, u32[]{:S(2)}) collective-permute-start(f32[64,64]{0,1:T(8,128)S(1)} %get-tuple-element.30), channel_id=1, source_target_pairs={{0,96},{1,97},{2,98},{3,99},{4,100},{5,101},{6,102},{7,103},{8,104... | collective-permute-start | bytes 49160 | tf_op jit(solution)/shard_map/ppermute | solution.py:47
  117.6 9.3 %collective-permute-start.18 = (f32[64,64]{0,1:T(8,128)S(1)}, f32[64,64]{0,1:T(8,128)S(1)}, u32[]{:S(2)}, u32[]{:S(2)}) collective-permute-start(f32[64,64]{0,1:T(8,128)S(1)} %get-tuple-element.31), channel_id=1, source_target_pairs={{0,32},{1,33},{2,34},{3,35},{4,36},{5,37},{6,38},{7,39},{8,40},{9,... | collective-permute-start | bytes 49160 | tf_op jit(solution)/shard_map/ppermute | solution.py:47
  119.0 11.1 %collective-permute-start.17 = (f32[64,64]{0,1:T(8,128)S(1)}, f32[64,64]{0,1:T(8,128)S(1)}, u32[]{:S(2)}, u32[]{:S(2)}) collective-permute-start(f32[64,64]{0,1:T(8,128)S(1)} %get-tuple-element.32), channel_id=1, source_target_pairs={{0,64},{1,65},{2,66},{3,67},{4,68},{5,69},{6,70},{7,71},{8,72},{9,... | collective-permute-start | bytes 49160 | tf_op jit(solution)/shard_map/ppermute | solution.py:47
  121.1 11.9 %collective-permute-start.15 = (bf16[64,1792]{1,0:T(8,128)(2,1)S(1)}, bf16[64,1792]{1,0:T(8,128)(2,1)S(1)}, u32[]{:S(2)}, u32[]{:S(2)}) collective-permute-start(bf16[64,1792]{1,0:T(8,128)(2,1)S(1)} %slice.374), channel_id=1, source_target_pairs={{0,96},{1,97},{2,98},{3,99},{4,100},{5,101},{6,102},{7,103},{8,104... | collective-permute-start | bytes 688136 | tf_op jit(solution)/shard_map/ppermute | solution.py:47
  123.8 11.1 %collective-permute-start.13 = (bf16[64,1792]{1,0:T(8,128)(2,1)S(1)}, bf16[64,1792]{1,0:T(8,128)(2,1)S(1)}, u32[]{:S(2)}, u32[]{:S(2)}) collective-permute-start(bf16[64,1792]{1,0:T(8,128)(2,1)S(1)} %get-tuple-element.23), channel_id=1, source_target_pairs={{0,64},{1,65},{2,66},{3,67},{4,68},{5,69},{6,70},{7,71},{8,72},{9,... | collective-permute-start | bytes 688136 | tf_op jit(solution)/shard_map/ppermute | solution.py:47
  126.6 15.0 %collective-permute-start.14 = (bf16[64,1792]{1,0:T(8,128)(2,1)S(1)}, bf16[64,1792]{1,0:T(8,128)(2,1)S(1)}, u32[]{:S(2)}, u32[]{:S(2)}) collective-permute-start(bf16[64,1792]{1,0:T(8,128)(2,1)S(1)} %get-tuple-element.24), channel_id=1, source_target_pairs={{0,32},{1,33},{2,34},{3,35},{4,36},{5,37},{6,38},{7,39},{8,40},{9,... | collective-permute-start | bytes 688136 | tf_op jit(solution)/shard_map/ppermute | solution.py:47
  127.0 15.9 %collective-permute-start.23 = (bf16[64,1792]{1,0:T(8,128)(2,1)S(1)}, bf16[64,1792]{1,0:T(8,128)(2,1)S(1)}, u32[]{:S(2)}, u32[]{:S(2)}) collective-permute-start(bf16[64,1792]{1,0:T(8,128)(2,1)S(1)} %slice.373), channel_id=1, source_target_pairs={{0,96},{1,97},{2,98},{3,99},{4,100},{5,101},{6,102},{7,103},{8,104... | collective-permute-start | bytes 688136 | tf_op jit(solution)/shard_map/ppermute | solution.py:47
  130.1 13.7 %collective-permute-start.21 = (bf16[64,1792]{1,0:T(8,128)(2,1)S(1)}, bf16[64,1792]{1,0:T(8,128)(2,1)S(1)}, u32[]{:S(2)}, u32[]{:S(2)}) collective-permute-start(bf16[64,1792]{1,0:T(8,128)(2,1)S(1)} %get-tuple-element.25), channel_id=1, source_target_pairs={{0,64},{1,65},{2,66},{3,67},{4,68},{5,69},{6,70},{7,71},{8,72},{9,... | collective-permute-start | bytes 688136 | tf_op jit(solution)/shard_map/ppermute | solution.py:47
  133.0 13.7 %collective-permute-start.22 = (bf16[64,1792]{1,0:T(8,128)(2,1)S(1)}, bf16[64,1792]{1,0:T(8,128)(2,1)S(1)}, u32[]{:S(2)}, u32[]{:S(2)}) collective-permute-start(bf16[64,1792]{1,0:T(8,128)(2,1)S(1)} %get-tuple-element.26), channel_id=1, source_target_pairs={{0,32},{1,33},{2,34},{3,35},{4,36},{5,37},{6,38},{7,39},{8,40},{9,... | collective-permute-start | bytes 688136 | tf_op jit(solution)/shard_map/ppermute | solution.py:47
  146.7 16.7 %slice-start = ((s8[7340032]{0:T(1024)(128)(4,1)}), s8[4194304]{0:T(1024)(128)(4,1)S(1)}, s32[]{:S(2)}) async-start(s8[7340032]{0:T(1024)(128)(4,1)} %bitcast.60), calls=%async_computation.2 | async-start | bytes 8388608
  147.0 12.9 %collective-permute-start.26 = (bf16[64,1792]{1,0:T(8,128)(2,1)S(1)}, bf16[64,1792]{1,0:T(8,128)(2,1)S(1)}, u32[]{:S(2)}, u32[]{:S(2)}) collective-permute-start(bf16[64,1792]{1,0:T(8,128)(2,1)S(1)} %get-tuple-element.6), channel_id=1, source_target_pairs={{0,32},{1,33},{2,34},{3,35},{4,36},{5,37},{6,38},{7,39},{8,40},{9,... | collective-permute-start | bytes 688136 | tf_op jit(solution)/shard_map/ppermute | solution.py:47
  147.1 12.8 %collective-permute-start.25 = (bf16[64,1792]{1,0:T(8,128)(2,1)S(1)}, bf16[64,1792]{1,0:T(8,128)(2,1)S(1)}, u32[]{:S(2)}, u32[]{:S(2)}) collective-permute-start(bf16[64,1792]{1,0:T(8,128)(2,1)S(1)} %get-tuple-element.6), channel_id=1, source_target_pairs={{0,64},{1,65},{2,66},{3,67},{4,68},{5,69},{6,70},{7,71},{8,72},{9,... | collective-permute-start | bytes 688136 | tf_op jit(solution)/shard_map/ppermute | solution.py:47
  149.1 11.4 %collective-permute-start.24 = (bf16[64,1792]{1,0:T(8,128)(2,1)S(1)}, bf16[64,1792]{1,0:T(8,128)(2,1)S(1)}, u32[]{:S(2)}, u32[]{:S(2)}) collective-permute-start(bf16[64,1792]{1,0:T(8,128)(2,1)S(1)} %get-tuple-element.6), channel_id=1, source_target_pairs={{0,96},{1,97},{2,98},{3,99},{4,100},{5,101},{6,102},{7,103},{8,104... | collective-permute-start | bytes 688136 | tf_op jit(solution)/shard_map/ppermute | solution.py:47
  151.1 9.5 %collective-permute-start.27 = (bf16[64,1792]{1,0:T(8,128)(2,1)S(1)}, bf16[64,1792]{1,0:T(8,128)(2,1)S(1)}, u32[]{:S(2)}, u32[]{:S(2)}) collective-permute-start(bf16[64,1792]{1,0:T(8,128)(2,1)S(1)} %get-tuple-element.6), channel_id=1, source_target_pairs={{0,16},{1,17},{2,18},{3,19},{4,20},{5,21},{6,22},{7,23},{8,24},{9,... | collective-permute-start | bytes 688136 | tf_op jit(solution)/shard_map/ppermute | solution.py:51
  159.9 2.2 %collective-permute-start.30 = (bf16[64,1792]{1,0:T(8,128)(2,1)S(1)}, bf16[64,1792]{1,0:T(8,128)(2,1)S(1)}, u32[]{:S(2)}, u32[]{:S(2)}) collective-permute-start(bf16[64,1792]{1,0:T(8,128)(2,1)S(1)} %collective-permute-done.26), channel_id=1, source_target_pairs={{0,16},{1,17},{2,18},{3,19},{4,20},{5,21},{6,22},{7,23},{8,24},{9,... | collective-permute-start | bytes 688136 | tf_op jit(solution)/shard_map/ppermute | solution.py:51
  159.9 2.2 %collective-permute-start.29 = (bf16[64,1792]{1,0:T(8,128)(2,1)S(1)}, bf16[64,1792]{1,0:T(8,128)(2,1)S(1)}, u32[]{:S(2)}, u32[]{:S(2)}) collective-permute-start(bf16[64,1792]{1,0:T(8,128)(2,1)S(1)} %collective-permute-done.25), channel_id=1, source_target_pairs={{0,16},{1,17},{2,18},{3,19},{4,20},{5,21},{6,22},{7,23},{8,24},{9,... | collective-permute-start | bytes 688136 | tf_op jit(solution)/shard_map/ppermute | solution.py:51
  160.5 1.5 collective-permute-start.28
  162.2 1.9 slice-start.1
  167.4 10.9 %collective-permute-start.31 = (bf16[128,2048]{1,0:T(8,128)(2,1)S(1)}, bf16[128,2048]{1,0:T(8,128)(2,1)S(1)}, u32[]{:S(2)}, u32[]{:S(2)}) collective-permute-start(bf16[128,2048]{1,0:T(8,128)(2,1)S(1)} %convolution_convert_fusion.7), channel_id=1, source_target_pairs={{0,8},{1,9},{2,10},{3,11},{4,12},{5,13},{6,14},{7,15},{8,0},{9,1},... | collective-permute-start | bytes 1572872 | tf_op jit(solution)/shard_map/ppermute | solution.py:36
  168.5 13.3 %collective-permute-start.32 = (bf16[128,2048]{1,0:T(8,128)(2,1)S(1)}, bf16[128,2048]{1,0:T(8,128)(2,1)S(1)}, u32[]{:S(2)}, u32[]{:S(2)}) collective-permute-start(bf16[128,2048]{1,0:T(8,128)(2,1)S(1)} %convolution_convert_fusion.6), channel_id=1, source_target_pairs={{0,4},{1,5},{2,6},{3,7},{4,8},{5,9},{6,10},{7,11},{8,12},{9,13},{1... | collective-permute-start | bytes 1572872 | tf_op jit(solution)/shard_map/ppermute | solution.py:36
  169.7 14.1 %collective-permute-start.33 = (bf16[128,2048]{1,0:T(8,128)(2,1)S(1)}, bf16[128,2048]{1,0:T(8,128)(2,1)S(1)}, u32[]{:S(2)}, u32[]{:S(2)}) collective-permute-start(bf16[128,2048]{1,0:T(8,128)(2,1)S(1)} %convolution_convert_fusion.5), channel_id=1, source_target_pairs={{0,12},{1,13},{2,14},{3,15},{4,0},{5,1},{6,2},{7,3},{8,4},{9,5},{1... | collective-permute-start | bytes 1572872 | tf_op jit(solution)/shard_map/ppermute | solution.py:36
  183.8 14.6 %copy-start.1 = (bf16[512,2048]{1,0:T(8,128)(2,1)S(1)}, bf16[512,2048]{1,0:T(8,128)(2,1)}, u32[]{:S(2)}) copy-start(bf16[512,2048]{1,0:T(8,128)(2,1)} %param.21) | copy-start | bytes 6291460
  185.4 6.6 %collective-permute-start.34 = (bf16[32,2048]{1,0:T(8,128)(2,1)S(1)}, bf16[32,2048]{1,0:T(8,128)(2,1)S(1)}, u32[]{:S(2)}, u32[]{:S(2)}) collective-permute-start(bf16[32,2048]{1,0:T(8,128)(2,1)S(1)} %get-tuple-element.17), channel_id=1, source_target_pairs={{0,2},{1,3},{2,0},{3,1},{4,6},{5,7},{6,4},{7,5},{8,10},{9,11},{10,... | collective-permute-start | bytes 393224 | tf_op jit(solution)/shard_map/ppermute | solution.py:43
  189.1 5.0 %collective-permute-start.36 = (bf16[32,2048]{1,0:T(8,128)(2,1)S(1)}, bf16[32,2048]{1,0:T(8,128)(2,1)S(1)}, u32[]{:S(2)}, u32[]{:S(2)}) collective-permute-start(bf16[32,2048]{1,0:T(8,128)(2,1)S(1)} %get-tuple-element.18), channel_id=1, source_target_pairs={{0,3},{1,0},{2,1},{3,2},{4,7},{5,4},{6,5},{7,6},{8,11},{9,8},{10,9... | collective-permute-start | bytes 393224 | tf_op jit(solution)/shard_map/ppermute | solution.py:43
  191.5 6.2 %collective-permute-start.35 = (bf16[32,2048]{1,0:T(8,128)(2,1)S(1)}, bf16[32,2048]{1,0:T(8,128)(2,1)S(1)}, u32[]{:S(2)}, u32[]{:S(2)}) collective-permute-start(bf16[32,2048]{1,0:T(8,128)(2,1)S(1)} %get-tuple-element.19), channel_id=1, source_target_pairs={{0,1},{1,2},{2,3},{3,0},{4,5},{5,6},{6,7},{7,4},{8,9},{9,10},{10,1... | collective-permute-start | bytes 393224 | tf_op jit(solution)/shard_map/ppermute | solution.py:43
where the time goes:
time: 200 us; the launch traced here: 198 us
  waiting for transfers between devices  99 us (50%)
  starting transfers between devices  60.4 us (30%)
  matrix products  25.9 us (13%)
  local copies, waits for them, and re-layouts  8 us (4%)
  other arithmetic  4.41 us (2%)
    ppermute x9, waiting for transfers between devices, send_first(): return lax.ppermute(value, AXES, pairs(move))  39.8 us
    ppermute x12, waiting for transfers between devices, send_z(): lax.ppermute(value, AXES, pairs(lambda x, y, z, core: (x, y, z + step, co...  22.5 us
    ppermute x12, starting transfers between devices, send_z(): lax.ppermute(value, AXES, pairs(lambda x, y, z, core: (x, y, z + step, co...  17.6 us
    ppermute x9, waiting for transfers between devices, send_second(): return lax.ppermute(value, AXES, pairs(move))  17.2 us
    ppermute x9, starting transfers between devices, send_second(): return lax.ppermute(value, AXES, pairs(move))  12.8 us
    ppermute x9, starting transfers between devices, send_first(): return lax.ppermute(value, AXES, pairs(move))  12.7 us
    all_to_all x1, waiting for transfers between devices, on_device(): lax.all_to_all(outgoing.reshape(count_gx * count_yz, per_device, head_wid...  11.6 us
    dot_general x7, matrix products, pick(): return jnp.dot(matrix, values, preferred_element_type=F32).astype(BF16)  8.69 us
  transfers between devices with their start and end apart: 39, of which 25 were waited for; matrix products, arithmetic and copies ran while one was open for 3% of the time, Pallas kernels for 0%

commit v1 on v0

v1 whole, which is shorter than its diff:
```python
import functools

import jax
import jax.numpy as jnp
from jax import lax
from jax.experimental import pallas as pl
from jax.experimental.pallas import tpu as pltpu
from jax.sharding import PartitionSpec as P

HD = 128
RING = 4
CORES = 2
AXES = ("gx", "yz")
BF16 = jnp.bfloat16
F32 = jnp.float32
FAR_FIRST = (2, 1, 3, 0)
TURNS = 2


def place(device):
    gx, yz = divmod(device, RING * RING)
    z, core = divmod(gx, CORES)
    x, y = divmod(yz, RING)
    return x, y, z, core


def number(x, y, z, core):
    gx = (z % RING) * CORES + core
    return gx * RING * RING + (x % RING) * RING + y % RING


def pairs(move):
    count = RING * RING * RING * CORES
    return [(d, number(*move(*place(d)))) for d in range(count)]


def send_first(value, step):
    def move(x, y, z, core):
        return (x + step, y, z, core) if core == 0 else (x, y + step, z, core)

    return lax.ppermute(value, AXES, pairs(move))


def send_second(value, step):
    def move(x, y, z, core):
        return (x, y + step, z, core) if core == 0 else (x + step, y, z, core)

    return lax.ppermute(value, AXES, pairs(move))


def send_z(value, step):
    return lax.ppermute(value, AXES, pairs(lambda x, y, z, core: (x, y, z + step, core)))


def send_core(value):
    return lax.ppermute(value, AXES, pairs(lambda x, y, z, core: (x, y, z, 1 - core)))


def spread(send, blocks):
    return [send(blocks[j], j) for j in FAR_FIRST if j != 0]


def collect(send, value):
    got = {0: value}
    for j in (2, 1, 3):
        got[j] = send(value, -j)
    return [got[j] for j in range(RING)]


def add_up(own, others):
    total = own.astype(F32)
    for other in others:
        total = total + other.astype(F32)
    return total


def one_hot_rows(index, count):
    return (index[:, None] == jnp.arange(count, dtype=jnp.int32)[None, :]).astype(BF16)


def pick(matrix, values):
    return jnp.dot(matrix, values, preferred_element_type=F32).astype(BF16)


def local_kernel(body, shapes, *values):
    whole = pl.BlockSpec(memory_space=pltpu.VMEM)
    size = sum(v.size * v.dtype.itemsize for v in values)
    return pl.pallas_call(
        body,
        out_shape=shapes,
        in_specs=[whole] * len(values),
        out_specs=[whole] * len(shapes),
        compiler_params=pltpu.CompilerParams(vmem_limit_bytes=24 * 2**20),
        cost_estimate=pl.CostEstimate(flops=size, bytes_accessed=2 * size, transcendentals=0),
    )(*values)


def ends_of(total):
    high = total.astype(BF16).astype(F32)
    lane = lax.broadcasted_iota(jnp.int32, (total.shape[0], HD), 1)
    return jnp.where(lane < HD // 2, high, total - high).astype(BF16)


def middle_kernel(part, far_one, far_two, far_three, resid, gain, payload, middle):
    chunk, width = part.shape
    piece = chunk // RING
    for k in range(RING):
        here = pl.ds(k * piece, piece)
        total = part[here, :] + resid[here, :].astype(F32)
        for d, other in enumerate((far_one, far_two, far_three)):
            total = total + other[pl.ds((k - d - 1) % RING * piece, piece), :].astype(F32)
        rounded = total.astype(BF16)
        if k == 0:
            middle[...] = rounded
        total = rounded.astype(F32)
        payload[here, :width] = (total * gain[...]).astype(BF16)
        payload[here, width:] = ends_of(jnp.sum(total * total, axis=1, keepdims=True))


def pair_kernel(gate, upper, ends, gate_other, upper_other, ends_other, *payloads):
    half = gate.shape[0] // RING
    width = gate.shape[1]
    for i, payload in enumerate(payloads):
        here = pl.ds(i * half, half)
        payload[:, :width] = (gate[here, :] + gate_other[here, :].astype(F32)).astype(BF16)
        payload[:, width : 2 * width] = (
            upper[here, :] + upper_other[here, :].astype(F32)
        ).astype(BF16)
        both = ends[here, :] + ends_other[here, :]
        payload[:, 2 * width :] = ends_of(both[:, :1] + both[:, HD // 2 : HD // 2 + 1])


def hidden_kernel(model_width, own, one, two, three, hidden):
    width = hidden.shape[1]

    def total(span):
        values = [ref[:, span].astype(F32) for ref in (own, one, two, three)]
        return values[0] + values[1] + values[2] + values[3]

    ends = total(pl.ds(2 * width, HD))
    squares = ends[:, :1] + ends[:, HD // 2 : HD // 2 + 1]
    factor = lax.rsqrt(squares / model_width + 1e-05)
    gate = total(pl.ds(0, width)) * factor
    upper = total(pl.ds(width, width)) * factor
    hidden[...] = (gate / (1.0 + jnp.exp(-gate)) * upper).astype(BF16)


def attend_slots(query_heads, key_rows, value_rows, cache_keys, cache_values, valid):
    slot_count, positions = cache_keys.shape[:2]
    kv_heads, groups = query_heads.shape[1:3]
    scaling = HD ** (-0.5)
    key_heads = cache_keys.reshape(slot_count, positions, kv_heads, HD)
    value_heads = cache_values.reshape(slot_count, positions, kv_heads, HD)
    scores = (
        jnp.einsum("bkgd,bckd->bkgc", query_heads, key_heads, preferred_element_type=F32) * scaling
    )
    new_score = (
        jnp.einsum("bkgd,bkd->bkg", query_heads, key_rows, preferred_element_type=F32) * scaling
    )
    inside = jnp.arange(positions)[None, :] < valid[:, None]
    scores = jnp.where(inside[:, None, None, :], scores, -jnp.inf)
    largest = jnp.maximum(jnp.max(scores, axis=-1), new_score)
    powers = jnp.exp(scores - largest[..., None])
    power_new = jnp.exp(new_score - largest)
    totals = jnp.sum(powers, axis=-1) + power_new
    weights = (powers / totals[..., None]).astype(BF16)
    weight_new = (power_new / totals).astype(BF16)
    context = jnp.einsum("bkgc,bckd->bkgd", weights, value_heads, preferred_element_type=F32)
    context = context + weight_new.astype(F32)[..., None] * value_rows.astype(F32)[:, :, None, :]
    return context.reshape(slot_count, kv_heads * groups * HD).astype(BF16)


def on_device(
    resid,
    queries,
    new_keys,
    new_values,
    cache_keys,
    cache_values,
    lengths,
    cache_slot,
    out_weight,
    norm_gain,
    gate_weight,
    up_weight,
    down_weight,
):
    index_gx = lax.axis_index("gx")
    index_yz = lax.axis_index("yz")
    count_yz = RING * RING
    count_gx = RING * CORES
    z, core = index_gx // CORES, index_gx % CORES
    x, y = index_yz // RING, index_yz % RING
    rows = resid.shape[0]
    width = resid.shape[1]
    per_device = cache_keys.shape[0]
    group_slots = per_device * count_yz
    block = rows // count_yz
    kv_heads = cache_keys.shape[2] // HD
    head_width = out_weight.shape[0]
    heads_here = head_width // HD
    new_width = new_keys.shape[1]

    slot_here = index_gx * group_slots + jnp.arange(group_slots, dtype=jnp.int32)
    routing = cache_slot[None, :] == slot_here[:, None]
    outgoing = pick(
        routing.astype(BF16), jnp.concatenate([queries, new_keys, new_values], axis=1)
    )
    valid = jnp.sum(jnp.where(routing, lengths[None, :], 0), axis=1)
    valid_own = lax.dynamic_slice_in_dim(valid, index_yz * per_device, per_device)
    arrived = lax.all_to_all(outgoing, "yz", split_axis=0, concat_axis=0, tiled=True)
    arrived = arrived.reshape(count_yz, per_device, head_width + 2 * new_width)
    query_heads = (
        arrived[:, :, :head_width]
        .reshape(count_yz, per_device, heads_here, HD)
        .transpose(1, 0, 2, 3)
        .reshape(per_device, kv_heads, count_yz * heads_here // kv_heads, HD)
    )
    key_rows = (
        arrived[:, :, head_width : head_width + new_width]
        .transpose(1, 0, 2)
        .reshape(per_device, kv_heads, HD)
    )
    value_rows = (
        arrived[:, :, head_width + new_width :].transpose(1, 0, 2).reshape(per_device, kv_heads, HD)
    )
    context = attend_slots(query_heads, key_rows, value_rows, cache_keys, cache_values, valid_own)

    outgoing = context.reshape(per_device, count_yz, head_width).transpose(1, 0, 2)
    outgoing = jnp.broadcast_to(outgoing[None], (count_gx,) + outgoing.shape)
    all_columns = lax.all_to_all(
        outgoing.reshape(count_gx * count_yz, per_device, head_width),
        AXES,
        split_axis=0,
        concat_axis=0,
        tiled=True,
    ).reshape(rows, head_width)

    def turn(number):
        positions = jnp.arange(rows // TURNS, dtype=jnp.int32)
        piece = block // TURNS
        chunk = RING * piece

        far, near, inner = positions // chunk, (positions // piece) % RING, positions % piece
        row_x = jnp.where(core == 0, x + far, x + near) % RING
        row_y = jnp.where(core == 0, y + near, y + far) % RING
        row_here = (row_x * RING + row_y) * block + number * piece + inner
        slot_of = jnp.sum(
            jnp.where(row_here[:, None] == jnp.arange(rows)[None, :], cache_slot[None, :], 0), axis=1
        )
        context_rows = pick(one_hot_rows(slot_of, rows), all_columns)

        def sum_first(values, weight):
            parts = {}
            for j in FAR_FIRST:
                part = jnp.dot(
                    values[j * chunk : (j + 1) * chunk], weight, preferred_element_type=F32
                )
                parts[j] = part if j == 0 else part.astype(BF16)
            return add_up(parts[0], spread(send_first, parts))

        part = sum_first(context_rows, out_weight)
        others = collect(send_second, part.astype(BF16))[1:]
        resid_rows = pick(one_hot_rows(row_here[:chunk], rows), resid)
        payload, middle = local_kernel(
            middle_kernel,
            [
                jax.ShapeDtypeStruct((chunk, width + HD), BF16),
                jax.ShapeDtypeStruct((piece, width), BF16),
            ],
            part,
            *others,
            resid_rows,
            norm_gain[None, :],
        )
        blocks = jnp.concatenate(collect(send_first, payload), axis=0)

        half = chunk // CORES
        target = positions[: RING * half] // half
        distance = jnp.zeros_like(target)
        for order_index, j in enumerate(FAR_FIRST):
            distance = jnp.where(target == order_index, j, distance)
        part_x = (z + distance) % RING
        inner_half = positions[: RING * half] % half

        def half_rows(part_core):
            part_y = part_core * (RING // CORES) + inner_half // piece
            source = jnp.where(core == 0, part_x * RING + part_y, part_y * RING + part_x)
            matrix = one_hot_rows(source * piece + inner_half % piece, rows // TURNS)
            ends = jnp.dot(matrix, blocks[:, width:], preferred_element_type=F32)
            return pick(matrix, blocks[:, :width]), ends

        other_rows, other_ends = half_rows(1 - core)
        own_rows, own_ends = half_rows(core)
        other_ends = send_core(other_ends)
        other_gate = send_core(pick(other_rows, gate_weight))
        other_upper = send_core(pick(other_rows, up_weight))
        hidden_width = gate_weight.shape[1]
        payloads = local_kernel(
            pair_kernel,
            [jax.ShapeDtypeStruct((half, 2 * hidden_width + HD), BF16)] * RING,
            jnp.dot(own_rows, gate_weight, preferred_element_type=F32),
            jnp.dot(own_rows, up_weight, preferred_element_type=F32),
            own_ends,
            other_gate,
            other_upper,
            other_ends,
        )
        parts = dict(zip(FAR_FIRST, payloads))
        (hidden,) = local_kernel(
            functools.partial(hidden_kernel, width * count_gx),
            [jax.ShapeDtypeStruct((half, hidden_width), BF16)],
            parts[0],
            *spread(send_z, parts),
        )

        own_hidden = jnp.concatenate(collect(send_z, hidden), axis=0)
        all_hidden = jnp.concatenate([own_hidden, send_core(own_hidden)], axis=0)
        place_x = jnp.where(core == 0, far, near)
        place_y = jnp.where(core == 0, near, far)
        place_core = (place_y // (RING // CORES) + core) % CORES
        place_z = (place_x - z) % RING
        place_here = (
            (place_core * RING + place_z) * half + (place_y % (RING // CORES)) * piece + inner
        )
        hidden_rows = pick(one_hot_rows(place_here, rows // TURNS), all_hidden)
        part = sum_first(hidden_rows, down_weight)
        parts = {k: part[k * piece : (k + 1) * piece] for k in range(RING)}
        parts = {k: part if k == 0 else part.astype(BF16) for k, part in parts.items()}
        projected = add_up(parts[0], spread(send_second, parts))
        return (middle.astype(F32) + projected).astype(BF16)

    return jnp.concatenate([turn(number) for number in range(TURNS)], axis=0)


def solution(mesh):
    in_specs = (
        P(None, "gx"),
        P(None, "yz"),
        P(None, "yz"),
        P(None, "yz"),
        P(("gx", "yz"), None, None),
        P(("gx", "yz"), None, None),
        P(),
        P(),
        P("yz", "gx"),
        P("gx"),
        P("gx", "yz"),
        P("gx", "yz"),
        P("yz", "gx"),
    )
    out_specs = P("yz", "gx")
    return jax.shard_map(
        on_device, mesh=mesh, in_specs=in_specs, out_specs=out_specs, check_vma=False
    )
```

time: 200 us -> 195 us (0.975)
  waiting for transfers between devices: 99 us -> 48.3 us
  starting transfers between devices: 60.4 us -> 93.6 us
  matrix products: 25.9 us -> 39.1 us
  other arithmetic: 4.41 us -> 1.76 us
    ppermute x9 -> x18, waiting for transfers between devices: 39.8 us -> 8.43 us  [send_first(): return lax.ppermute(value, AXES, pairs(move))]
    ppermute x9 -> x18, starting transfers between devices: 12.7 us -> 27.6 us  [send_first(): return lax.ppermute(value, AXES, pairs(move))]
    ppermute x7 -> x8, starting transfers between devices: 1.35 us -> 15.9 us  [send_core(): lax.ppermute(value, AXES, pairs(lambda x, y, z, core: (x, y, z, 1 - core)))]
    ppermute x12, waiting for transfers between devices: 22.5 us -> 16.2 us  [send_z(): lax.ppermute(value, AXES, pairs(lambda x, y, z, core: (x, y, z + step, co...]
    dot_general x12 -> x20, matrix products: 13.8 us -> 20 us  [the longest x16 15.5 us: sum_first(): jnp.dot(values[j * chunk:(j + 1) * chunk], weight, preferred_element_type...]
    ppermute x9 -> x12, waiting for transfers between devices: 17.2 us -> 11 us  [send_second(): return lax.ppermute(value, AXES, pairs(move))]
    dot_general x7 -> x15, matrix products: 8.69 us -> 14.1 us  [pick(): return jnp.dot(matrix, values, preferred_element_type=F32).astype(BF16)]
    ppermute x9 -> x12, starting transfers between devices: 12.8 us -> 17.5 us  [send_second(): return lax.ppermute(value, AXES, pairs(move))]
  transfers between devices with their start and end apart: 39 -> 52, of which waited for: 25 -> 20; matrix products, arithmetic and copies ran while one was open for 3% -> 13% of each run, Pallas kernels for 0% -> 1%
where the time goes in v1:
time: 195 us; the launch traced here: 193 us
  starting transfers between devices  93.6 us (48%)
  waiting for transfers between devices  48.3 us (25%)
  matrix products  39.1 us (20%)
  local copies, waits for them, and re-layouts  7.15 us (4%)
    ppermute x18, starting transfers between devices, send_first(): return lax.ppermute(value, AXES, pairs(move))  27.6 us
    ppermute x12, starting transfers between devices, send_second(): return lax.ppermute(value, AXES, pairs(move))  17.5 us
    ppermute x12, starting transfers between devices, send_z(): lax.ppermute(value, AXES, pairs(lambda x, y, z, core: (x, y, z + step, co...  16.6 us
    ppermute x12, waiting for transfers between devices, send_z(): lax.ppermute(value, AXES, pairs(lambda x, y, z, core: (x, y, z + step, co...  16.2 us
    ppermute x8, starting transfers between devices, send_core(): lax.ppermute(value, AXES, pairs(lambda x, y, z, core: (x, y, z, 1 - core)))  15.9 us
    dot_general x16, matrix products, sum_first(): jnp.dot(values[j * chunk:(j + 1) * chunk], weight, preferred_element_type...  15.5 us
    dot_general x15, matrix products, pick(): return jnp.dot(matrix, values, preferred_element_type=F32).astype(BF16)  14.1 us
    ppermute x12, waiting for transfers between devices, send_second(): return lax.ppermute(value, AXES, pairs(move))  11 us
  transfers between devices with their start and end apart: 52, of which 20 were waited for; matrix products, arithmetic and copies ran while one was open for 13% of the time, Pallas kernels for 1%

profile of v1, /device:TPU:6, one launch (start us, length us, event | category | flops | bytes accessed | tf_op | source)
XLA Modules:
  0.0 192.9 jit_solution(4680167325031445927)
XLA Ops:
  1.9 1.3 convolution_convert_fusion.26
  3.9 7.4 %all-to-all-start = ((bf16[16,4,576]{2,1,0:T(4,128)(2,1)}), bf16[16,4,576]{2,1,0:T(4,128)(2,1)S(1)}, u32[]{:S(2)}, u32[]{:S(2)}) async-start(bf16[16,4,576]{2,1,0:T(4,128)(2,1)} %all_to_all.9), calls=%async_computation | async-start | bytes 163840 | tf_op jit(solution)/shard_map/all_to_all | solution.py:211
  11.7 2.1 %convolution_convert_fusion.20.resid = bf16[64,2048]{1,0:T(8,128)(2,1)S(1)} fusion(bf16[512,2048]{1,0:T(8,128)(2,1)} %param.13, s32[64]{0:T(128)S(1)} %slice.130), kind=kOutput, calls=%fused_computation.20 | convolution fusion | flops 134381568 | bytes 2359552 | tf_op jit(solution)/shard_map/dot_general | solution.py:82
  14.0 3.1 %all-to-all-done = bf16[16,4,576]{2,1,0:T(4,128)(2,1)S(1)} async-done(((bf16[16,4,576]{2,1,0:T(4,128)(2,1)}), bf16[16,4,576]{2,1,0:T(4,128)(2,1)S(1)}, u32[]{:S(2)}, u32[]{:S(2)}) %all-to-all-start) | async-done | bytes 73760 | tf_op jit(solution)/shard_map/all_to_all | solution.py:211
  17.5 2.1 %fusion.119 = (f32[4,4,16]{2,1,0:T(4,128)S(1)}, f32[4,4,16,384]{3,2,1,0:T(8,128)S(1)}) fusion(bf16[4,4,16,128]{3,2,1,0:T(8,128)(2,1)S(1)} %bitcast.89, pred[4,384]{1,0:T(4,128)(4,1)S(1)} %iota_compare_fusion.23, bf16[4,384,512]{2,1,0:T(8,128)(2,1)} %param.17), kind=kOutput, calls=%fused_computation.227 | convolution fusion | flops 25460480 | bytes 2034176 | tf_op jit(solution)/shard_map/bkgd,bckd->bkgc/dot_general | solution.py:155
  20.0 1.8 fusion.15
  22.9 8.6 %all-to-all-start.1 = ((bf16[128,4,512]{2,1,0:T(4,128)(2,1)}), bf16[128,4,512]{2,1,0:T(4,128)(2,1)S(1)}, u32[]{:S(2)}, u32[]{:S(2)}) async-start(bf16[128,4,512]{2,1,0:T(4,128)(2,1)} %bitcast.87), calls=%async_computation.1 | async-start | bytes 1048576 | tf_op jit(solution)/shard_map/all_to_all | solution.py:231
  31.8 2.1 %convolution_convert_fusion.13.resid = bf16[64,2048]{1,0:T(8,128)(2,1)S(1)} fusion(bf16[512,2048]{1,0:T(8,128)(2,1)} %param.13, s32[64]{0:T(128)S(1)} %slice.146), kind=kOutput, calls=%fused_computation.13 | convolution fusion | flops 134381568 | bytes 2359552 | tf_op jit(solution)/shard_map/dot_general | solution.py:82
  33.9 9.5 %all-to-all-done.1 = bf16[128,4,512]{2,1,0:T(4,128)(2,1)S(1)} async-done(((bf16[128,4,512]{2,1,0:T(4,128)(2,1)}), bf16[128,4,512]{2,1,0:T(4,128)(2,1)S(1)}, u32[]{:S(2)}, u32[]{:S(2)}) %all-to-all-start.1) | async-done | bytes 524320 | tf_op jit(solution)/shard_map/all_to_all | solution.py:231
  44.4 1.4 convolution_convert_fusion.25
  48.6 2.8 %collective-permute-start = (bf16[64,2048]{1,0:T(8,128)(2,1)S(1)}, bf16[64,2048]{1,0:T(8,128)(2,1)S(1)}, u32[]{:S(2)}, u32[]{:S(2)}) collective-permute-start(bf16[64,2048]{1,0:T(8,128)(2,1)S(1)} %convolution_convert_fusion.23), channel_id=1, source_target_pairs={{0,8},{1,9},{2,10},{3,11},{4,12},{5,13},{6,14},{7,15},{8,0},{9,1},... | collective-permute-start | bytes 786440 | tf_op jit(solution)/shard_map/ppermute | solution.py:41
  52.4 1.1 collective-permute-start.2
  54.4 2.6 %collective-permute-start.26 = (bf16[64,2048]{1,0:T(8,128)(2,1)S(1)}, bf16[64,2048]{1,0:T(8,128)(2,1)S(1)}, u32[]{:S(2)}, u32[]{:S(2)}) collective-permute-start(bf16[64,2048]{1,0:T(8,128)(2,1)S(1)} %convolution_convert_fusion.15), channel_id=1, source_target_pairs={{0,4},{1,5},{2,6},{3,7},{4,8},{5,9},{6,10},{7,11},{8,12},{9,13},{1... | collective-permute-start | bytes 786440 | tf_op jit(solution)/shard_map/ppermute | solution.py:41
  57.7 1.8 collective-permute-done.1
  59.5 3.2 %collective-permute-done.2 = bf16[64,2048]{1,0:T(8,128)(2,1)S(1)} collective-permute-done((bf16[64,2048]{1,0:T(8,128)(2,1)S(1)}, bf16[64,2048]{1,0:T(8,128)(2,1)S(1)}, u32[]{:S(2)}, u32[]{:S(2)}) %collective-permute-start.2) | collective-permute-done | bytes 262176 | tf_op jit(solution)/shard_map/ppermute | solution.py:41
  63.4 2.7 %collective-permute-start.4 = (bf16[64,2048]{1,0:T(8,128)(2,1)S(1)}, bf16[64,2048]{1,0:T(8,128)(2,1)S(1)}, u32[]{:S(2)}, u32[]{:S(2)}) collective-permute-start(bf16[64,2048]{1,0:T(8,128)(2,1)S(1)} %get-tuple-element.47), channel_id=1, source_target_pairs={{0,2},{1,3},{2,0},{3,1},{4,6},{5,7},{6,4},{7,5},{8,10},{9,11},{10,... | collective-permute-start | bytes 786440 | tf_op jit(solution)/shard_map/ppermute | solution.py:48
  66.1 1.4 collective-permute-done.26
  68.2 2.0 %collective-permute-start.28 = (bf16[64,2048]{1,0:T(8,128)(2,1)S(1)}, bf16[64,2048]{1,0:T(8,128)(2,1)S(1)}, u32[]{:S(2)}, u32[]{:S(2)}) collective-permute-start(bf16[64,2048]{1,0:T(8,128)(2,1)S(1)} %get-tuple-element.51), channel_id=1, source_target_pairs={{0,3},{1,0},{2,1},{3,2},{4,7},{5,4},{6,5},{7,6},{8,11},{9,8},{10,9... | collective-permute-start | bytes 786440 | tf_op jit(solution)/shard_map/ppermute | solution.py:48
  71.6 2.6 %collective-permute-done.5.far_three = bf16[64,2048]{1,0:T(8,128)(2,1)S(1)} collective-permute-done((bf16[64,2048]{1,0:T(8,128)(2,1)S(1)}, bf16[64,2048]{1,0:T(8,128)(2,1)S(1)}, u32[]{:S(2)}, u32[]{:S(2)}) %collective-permute-start.5) | collective-permute-done | bytes 262176 | tf_op jit(solution)/shard_map/ppermute | solution.py:48
  74.5 2.2 %collective-permute-start.7 = (bf16[64,2176]{1,0:T(8,128)(2,1)S(1)}, bf16[64,2176]{1,0:T(8,128)(2,1)S(1)}, u32[]{:S(2)}, u32[]{:S(2)}) collective-permute-start(bf16[64,2176]{1,0:T(8,128)(2,1)S(1)} %get-tuple-element.18), channel_id=1, source_target_pairs={{0,8},{1,9},{2,10},{3,11},{4,12},{5,13},{6,14},{7,15},{8,0},{9,1},... | collective-permute-start | bytes 835592 | tf_op jit(solution)/shard_map/ppermute | solution.py:41
  76.8 3.5 %collective-permute-start.8 = (bf16[64,2176]{1,0:T(8,128)(2,1)S(1)}, bf16[64,2176]{1,0:T(8,128)(2,1)S(1)}, u32[]{:S(2)}, u32[]{:S(2)}) collective-permute-start(bf16[64,2176]{1,0:T(8,128)(2,1)S(1)} %get-tuple-element.18), channel_id=1, source_target_pairs={{0,4},{1,5},{2,6},{3,7},{4,8},{5,9},{6,10},{7,11},{8,12},{9,13},{1... | collective-permute-start | bytes 835592 | tf_op jit(solution)/shard_map/ppermute | solution.py:41
  80.2 5.5 %collective-permute-done.30.far_three = bf16[64,2048]{1,0:T(8,128)(2,1)S(1)} collective-permute-done((bf16[64,2048]{1,0:T(8,128)(2,1)S(1)}, bf16[64,2048]{1,0:T(8,128)(2,1)S(1)}, u32[]{:S(2)}, u32[]{:S(2)}) %collective-permute-start.30) | collective-permute-done | bytes 262176 | tf_op jit(solution)/shard_map/ppermute | solution.py:48
  86.1 1.8 collective-permute-start.31
  87.8 2.5 %collective-permute-start.32 = (bf16[64,2176]{1,0:T(8,128)(2,1)S(1)}, bf16[64,2176]{1,0:T(8,128)(2,1)S(1)}, u32[]{:S(2)}, u32[]{:S(2)}) collective-permute-start(bf16[64,2176]{1,0:T(8,128)(2,1)S(1)} %get-tuple-element.24), channel_id=1, source_target_pairs={{0,8},{1,9},{2,10},{3,11},{4,12},{5,13},{6,14},{7,15},{8,0},{9,1},... | collective-permute-start | bytes 835592 | tf_op jit(solution)/shard_map/ppermute | solution.py:41
  90.3 1.5 collective-permute-start.33
  92.4 1.1 convolution_convert_fusion.6
  95.2 1.1 convolution_convert_fusion.7
  96.7 1.1 fusion.125.gate
  97.9 1.1 fusion.126.upper
  99.7 1.1 convolution_convert_fusion.3
  100.8 1.1 convolution_convert_fusion.2
  103.5 1.1 fusion.127.gate
  105.1 14.5 %collective-permute-start.36 = (f32[128,128]{1,0:T(8,128)S(1)}, f32[128,128]{1,0:T(8,128)S(1)}, u32[]{:S(2)}, u32[]{:S(2)}) collective-permute-start(f32[128,128]{1,0:T(8,128)S(1)} %fusion.56), channel_id=1, source_target_pairs={{0,16},{1,17},{2,18},{3,19},{4,20},{5,21},{6,22},{7,23},{8,24},{9,... | collective-permute-start | bytes 196616 | tf_op jit(solution)/shard_map/ppermute | solution.py:56
  119.9 1.4 collective-permute-start.12
  121.3 1.1 fusion.128.upper
  123.1 2.6 %collective-permute-start.14 = (bf16[32,3712]{1,0:T(8,128)(2,1)S(1)}, bf16[32,3712]{1,0:T(8,128)(2,1)S(1)}, u32[]{:S(2)}, u32[]{:S(2)}) collective-permute-start(bf16[32,3712]{1,0:T(8,128)(2,1)S(1)} %get-tuple-element.22), channel_id=1, source_target_pairs={{0,96},{1,97},{2,98},{3,99},{4,100},{5,101},{6,102},{7,103},{8,104... | collective-permute-start | bytes 712712 | tf_op jit(solution)/shard_map/ppermute | solution.py:52
  126.3 1.1 collective-permute-start.37
  127.4 1.2 collective-permute-start.38
  128.6 1.6 collective-permute-done.12.one
  131.2 4.1 %collective-permute-done.13.two = bf16[32,3712]{1,0:T(8,128)(2,1)S(1)} collective-permute-done((bf16[32,3712]{1,0:T(8,128)(2,1)S(1)}, bf16[32,3712]{1,0:T(8,128)(2,1)S(1)}, u32[]{:S(2)}, u32[]{:S(2)}) %collective-permute-start.13) | collective-permute-done | bytes 237600 | tf_op jit(solution)/shard_map/ppermute | solution.py:52
  135.4 1.2 collective-permute-done.14.three
  136.9 4.3 %collective-permute-start.15 = (bf16[32,1792]{1,0:T(8,128)(2,1)S(1)}, bf16[32,1792]{1,0:T(8,128)(2,1)S(1)}, u32[]{:S(2)}, u32[]{:S(2)}) collective-permute-start(bf16[32,1792]{1,0:T(8,128)(2,1)S(1)} %shard_map.129), channel_id=1, source_target_pairs={{0,96},{1,97},{2,98},{3,99},{4,100},{5,101},{6,102},{7,103},{8,104... | collective-permute-start | bytes 344072 | tf_op jit(solution)/shard_map/ppermute | solution.py:52
  142.2 3.3 %collective-permute-done.38.two = bf16[32,3712]{1,0:T(8,128)(2,1)S(1)} collective-permute-done((bf16[32,3712]{1,0:T(8,128)(2,1)S(1)}, bf16[32,3712]{1,0:T(8,128)(2,1)S(1)}, u32[]{:S(2)}, u32[]{:S(2)}) %collective-permute-start.38) | collective-permute-done | bytes 237600 | tf_op jit(solution)/shard_map/ppermute | solution.py:52
  146.6 1.7 collective-permute-start.41
  149.6 2.3 %collective-permute-done.40 = bf16[32,1792]{1,0:T(8,128)(2,1)S(1)} collective-permute-done((bf16[32,1792]{1,0:T(8,128)(2,1)S(1)}, bf16[32,1792]{1,0:T(8,128)(2,1)S(1)}, u32[]{:S(2)}, u32[]{:S(2)}) %collective-permute-start.40) | collective-permute-done | bytes 114720 | tf_op jit(solution)/shard_map/ppermute | solution.py:52
  151.9 1.9 collective-permute-done.41
  153.9 1.4 collective-permute-done.42
  156.0 1.4 convolution_convert_fusion.19
  157.5 1.4 convolution_convert_fusion.18
  158.9 1.4 convolution_convert_fusion.17
  160.9 1.4 convolution_convert_fusion.12
  162.3 1.4 convolution_convert_fusion.11
  163.8 1.5 collective-permute-start.19
  165.3 1.6 collective-permute-start.20
  167.3 2.1 %collective-permute-start.44 = (bf16[64,2048]{1,0:T(8,128)(2,1)S(1)}, bf16[64,2048]{1,0:T(8,128)(2,1)S(1)}, u32[]{:S(2)}, u32[]{:S(2)}) collective-permute-start(bf16[64,2048]{1,0:T(8,128)(2,1)S(1)} %convolution_convert_fusion.12), channel_id=1, source_target_pairs={{0,8},{1,9},{2,10},{3,11},{4,12},{5,13},{6,14},{7,15},{8,0},{9,1},... | collective-permute-start | bytes 786440 | tf_op jit(solution)/shard_map/ppermute | solution.py:41
  170.2 1.4 convolution_convert_fusion.10
  171.7 1.2 collective-permute-start.46
  172.9 1.6 collective-permute-done.21
  174.5 1.5 fusion.121
  176.0 4.8 %collective-permute-start.22 = (bf16[16,2048]{1,0:T(8,128)(2,1)S(1)}, bf16[16,2048]{1,0:T(8,128)(2,1)S(1)}, u32[]{:S(2)}, u32[]{:S(2)}) collective-permute-start(bf16[16,2048]{1,0:T(8,128)(2,1)S(1)} %get-tuple-element.35), channel_id=1, source_target_pairs={{0,2},{1,3},{2,0},{3,1},{4,6},{5,7},{6,4},{7,5},{8,10},{9,11},{10,... | collective-permute-start | bytes 196616 | tf_op jit(solution)/shard_map/ppermute | solution.py:48
  180.8 3.2 %collective-permute-start.24 = (bf16[16,2048]{1,0:T(8,128)(2,1)S(1)}, bf16[16,2048]{1,0:T(8,128)(2,1)S(1)}, u32[]{:S(2)}, u32[]{:S(2)}) collective-permute-start(bf16[16,2048]{1,0:T(8,128)(2,1)S(1)} %get-tuple-element.36), channel_id=1, source_target_pairs={{0,3},{1,0},{2,1},{3,2},{4,7},{5,4},{6,5},{7,6},{8,11},{9,8},{10,9... | collective-permute-start | bytes 196616 | tf_op jit(solution)/shard_map/ppermute | solution.py:48
  184.1 1.5 fusion.123
  186.7 2.3 %collective-permute-start.49 = (bf16[16,2048]{1,0:T(8,128)(2,1)S(1)}, bf16[16,2048]{1,0:T(8,128)(2,1)S(1)}, u32[]{:S(2)}, u32[]{:S(2)}) collective-permute-start(bf16[16,2048]{1,0:T(8,128)(2,1)S(1)} %get-tuple-element.39), channel_id=1, source_target_pairs={{0,3},{1,0},{2,1},{3,2},{4,7},{5,4},{6,5},{7,6},{8,11},{9,8},{10,9... | collective-permute-start | bytes 196616 | tf_op jit(solution)/shard_map/ppermute | solution.py:48
  189.1 2.5 %collective-permute-done.47 = bf16[16,2048]{1,0:T(8,128)(2,1)S(1)} collective-permute-done((bf16[16,2048]{1,0:T(8,128)(2,1)S(1)}, bf16[16,2048]{1,0:T(8,128)(2,1)S(1)}, u32[]{:S(2)}, u32[]{:S(2)}) %collective-permute-start.47) | collective-permute-done | bytes 65568 | tf_op jit(solution)/shard_map/ppermute | solution.py:48
  (170 shorter events, 30.7 us)
Async XLA Ops:
  0.0 45.8 %copy-start = (bf16[512,2048]{1,0:T(8,128)(2,1)S(1)}, bf16[512,2048]{1,0:T(8,128)(2,1)}, u32[]{:S(2)}) copy-start(bf16[512,2048]{1,0:T(8,128)(2,1)} %param.21) | copy-start | bytes 6291460
  0.0 11.4 %copy-start.4 = (s32[512]{0:T(512)S(1)}, s32[512]{0:T(512)}, u32[]{:S(2)}) copy-start(s32[512]{0:T(512)} %param.20) | copy-start | bytes 6148
  0.0 11.4 %copy-start.5 = (s32[512]{0:T(512)S(1)}, s32[512]{0:T(512)}, u32[]{:S(2)}) copy-start(s32[512]{0:T(512)} %param.19) | copy-start | bytes 6148
  3.9 13.1 %all-to-all-start = ((bf16[16,4,576]{2,1,0:T(4,128)(2,1)}), bf16[16,4,576]{2,1,0:T(4,128)(2,1)S(1)}, u32[]{:S(2)}, u32[]{:S(2)}) async-start(bf16[16,4,576]{2,1,0:T(4,128)(2,1)} %all_to_all.9), calls=%async_computation | async-start | bytes 163840 | tf_op jit(solution)/shard_map/all_to_all | solution.py:211
  22.9 20.5 %all-to-all-start.1 = ((bf16[128,4,512]{2,1,0:T(4,128)(2,1)}), bf16[128,4,512]{2,1,0:T(4,128)(2,1)S(1)}, u32[]{:S(2)}, u32[]{:S(2)}) async-start(bf16[128,4,512]{2,1,0:T(4,128)(2,1)} %bitcast.87), calls=%async_computation.1 | async-start | bytes 1048576 | tf_op jit(solution)/shard_map/all_to_all | solution.py:231
  46.3 1.0 copy-start.3
  48.6 8.9 %collective-permute-start = (bf16[64,2048]{1,0:T(8,128)(2,1)S(1)}, bf16[64,2048]{1,0:T(8,128)(2,1)S(1)}, u32[]{:S(2)}, u32[]{:S(2)}) collective-permute-start(bf16[64,2048]{1,0:T(8,128)(2,1)S(1)} %convolution_convert_fusion.23), channel_id=1, source_target_pairs={{0,8},{1,9},{2,10},{3,11},{4,12},{5,13},{6,14},{7,15},{8,0},{9,1},... | collective-permute-start | bytes 786440 | tf_op jit(solution)/shard_map/ppermute | solution.py:41
  51.5 8.0 %collective-permute-start.1 = (bf16[64,2048]{1,0:T(8,128)(2,1)S(1)}, bf16[64,2048]{1,0:T(8,128)(2,1)S(1)}, u32[]{:S(2)}, u32[]{:S(2)}) collective-permute-start(bf16[64,2048]{1,0:T(8,128)(2,1)S(1)} %convolution_convert_fusion.22), channel_id=1, source_target_pairs={{0,4},{1,5},{2,6},{3,7},{4,8},{5,9},{6,10},{7,11},{8,12},{9,13},{1... | collective-permute-start | bytes 786440 | tf_op jit(solution)/shard_map/ppermute | solution.py:41
  52.4 10.4 %collective-permute-start.2 = (bf16[64,2048]{1,0:T(8,128)(2,1)S(1)}, bf16[64,2048]{1,0:T(8,128)(2,1)S(1)}, u32[]{:S(2)}, u32[]{:S(2)}) collective-permute-start(bf16[64,2048]{1,0:T(8,128)(2,1)S(1)} %convolution_convert_fusion.21), channel_id=1, source_target_pairs={{0,12},{1,13},{2,14},{3,15},{4,0},{5,1},{6,2},{7,3},{8,4},{9,5},{1... | collective-permute-start | bytes 786440 | tf_op jit(solution)/shard_map/ppermute | solution.py:41
  53.5 12.6 %collective-permute-start.25 = (bf16[64,2048]{1,0:T(8,128)(2,1)S(1)}, bf16[64,2048]{1,0:T(8,128)(2,1)S(1)}, u32[]{:S(2)}, u32[]{:S(2)}) collective-permute-start(bf16[64,2048]{1,0:T(8,128)(2,1)S(1)} %convolution_convert_fusion.16), channel_id=1, source_target_pairs={{0,8},{1,9},{2,10},{3,11},{4,12},{5,13},{6,14},{7,15},{8,0},{9,1},... | collective-permute-start | bytes 786440 | tf_op jit(solution)/shard_map/ppermute | solution.py:41
  54.4 13.1 %collective-permute-start.26 = (bf16[64,2048]{1,0:T(8,128)(2,1)S(1)}, bf16[64,2048]{1,0:T(8,128)(2,1)S(1)}, u32[]{:S(2)}, u32[]{:S(2)}) collective-permute-start(bf16[64,2048]{1,0:T(8,128)(2,1)S(1)} %convolution_convert_fusion.15), channel_id=1, source_target_pairs={{0,4},{1,5},{2,6},{3,7},{4,8},{5,9},{6,10},{7,11},{8,12},{9,13},{1... | collective-permute-start | bytes 786440 | tf_op jit(solution)/shard_map/ppermute | solution.py:41
  57.0 35.3 %slice-start.4 = ((s8[7340032]{0:T(1024)(128)(4,1)}), s8[4194304]{0:T(1024)(128)(4,1)S(1)}, s32[]{:S(2)}) async-start(s8[7340032]{0:T(1024)(128)(4,1)} %bitcast.85), calls=%async_computation.6 | async-start | bytes 8388608
  57.5 10.2 %collective-permute-start.27 = (bf16[64,2048]{1,0:T(8,128)(2,1)S(1)}, bf16[64,2048]{1,0:T(8,128)(2,1)S(1)}, u32[]{:S(2)}, u32[]{:S(2)}) collective-permute-start(bf16[64,2048]{1,0:T(8,128)(2,1)S(1)} %convolution_convert_fusion.14), channel_id=1, source_target_pairs={{0,12},{1,13},{2,14},{3,15},{4,0},{5,1},{6,2},{7,3},{8,4},{9,5},{1... | collective-permute-start | bytes 786440 | tf_op jit(solution)/shard_map/ppermute | solution.py:41
  63.3 10.9 %copy-start.2 = (f32[2048]{0:T(1024)S(1)}, f32[2048]{0:T(1024)}, u32[]{:S(2)}) copy-start(f32[2048]{0:T(1024)} %param.22) | copy-start | bytes 24580
  63.3 29.1 %slice-start.5 = ((s8[7340032]{0:T(1024)(128)(4,1)}), s8[3145728]{0:T(1024)(128)(4,1)S(1)}, s32[]{:S(2)}) async-start(s8[7340032]{0:T(1024)(128)(4,1)} %bitcast.85), calls=%async_computation.7 | async-start | bytes 6291456
  63.3 7.5 %collective-permute-start.3 = (bf16[64,2048]{1,0:T(8,128)(2,1)S(1)}, bf16[64,2048]{1,0:T(8,128)(2,1)S(1)}, u32[]{:S(2)}, u32[]{:S(2)}) collective-permute-start(bf16[64,2048]{1,0:T(8,128)(2,1)S(1)} %get-tuple-element.47), channel_id=1, source_target_pairs={{0,3},{1,0},{2,1},{3,2},{4,7},{5,4},{6,5},{7,6},{8,11},{9,8},{10,9... | collective-permute-start | bytes 786440 | tf_op jit(solution)/shard_map/ppermute | solution.py:48
  63.4 8.2 %collective-permute-start.4 = (bf16[64,2048]{1,0:T(8,128)(2,1)S(1)}, bf16[64,2048]{1,0:T(8,128)(2,1)S(1)}, u32[]{:S(2)}, u32[]{:S(2)}) collective-permute-start(bf16[64,2048]{1,0:T(8,128)(2,1)S(1)} %get-tuple-element.47), channel_id=1, source_target_pairs={{0,2},{1,3},{2,0},{3,1},{4,6},{5,7},{6,4},{7,5},{8,10},{9,11},{10,... | collective-permute-start | bytes 786440 | tf_op jit(solution)/shard_map/ppermute | solution.py:48
  66.1 8.1 %collective-permute-start.5 = (bf16[64,2048]{1,0:T(8,128)(2,1)S(1)}, bf16[64,2048]{1,0:T(8,128)(2,1)S(1)}, u32[]{:S(2)}, u32[]{:S(2)}) collective-permute-start(bf16[64,2048]{1,0:T(8,128)(2,1)S(1)} %get-tuple-element.47), channel_id=1, source_target_pairs={{0,1},{1,2},{2,3},{3,0},{4,5},{5,6},{6,7},{7,4},{8,9},{9,10},{10,1... | collective-permute-start | bytes 786440 | tf_op jit(solution)/shard_map/ppermute | solution.py:48
  68.2 8.5 %collective-permute-start.28 = (bf16[64,2048]{1,0:T(8,128)(2,1)S(1)}, bf16[64,2048]{1,0:T(8,128)(2,1)S(1)}, u32[]{:S(2)}, u32[]{:S(2)}) collective-permute-start(bf16[64,2048]{1,0:T(8,128)(2,1)S(1)} %get-tuple-element.51), channel_id=1, source_target_pairs={{0,3},{1,0},{2,1},{3,2},{4,7},{5,4},{6,5},{7,6},{8,11},{9,8},{10,9... | collective-permute-start | bytes 786440 | tf_op jit(solution)/shard_map/ppermute | solution.py:48
  70.2 10.0 %collective-permute-start.29 = (bf16[64,2048]{1,0:T(8,128)(2,1)S(1)}, bf16[64,2048]{1,0:T(8,128)(2,1)S(1)}, u32[]{:S(2)}, u32[]{:S(2)}) collective-permute-start(bf16[64,2048]{1,0:T(8,128)(2,1)S(1)} %get-tuple-element.51), channel_id=1, source_target_pairs={{0,2},{1,3},{2,0},{3,1},{4,6},{5,7},{6,4},{7,5},{8,10},{9,11},{10,... | collective-permute-start | bytes 786440 | tf_op jit(solution)/shard_map/ppermute | solution.py:48
  70.8 14.9 %collective-permute-start.30 = (bf16[64,2048]{1,0:T(8,128)(2,1)S(1)}, bf16[64,2048]{1,0:T(8,128)(2,1)S(1)}, u32[]{:S(2)}, u32[]{:S(2)}) collective-permute-start(bf16[64,2048]{1,0:T(8,128)(2,1)S(1)} %get-tuple-element.51), channel_id=1, source_target_pairs={{0,1},{1,2},{2,3},{3,0},{4,5},{5,6},{6,7},{7,4},{8,9},{9,10},{10,1... | collective-permute-start | bytes 786440 | tf_op jit(solution)/shard_map/ppermute | solution.py:48
  74.4 15.9 %collective-permute-start.6 = (bf16[64,2176]{1,0:T(8,128)(2,1)S(1)}, bf16[64,2176]{1,0:T(8,128)(2,1)S(1)}, u32[]{:S(2)}, u32[]{:S(2)}) collective-permute-start(bf16[64,2176]{1,0:T(8,128)(2,1)S(1)} %get-tuple-element.18), channel_id=1, source_target_pairs={{0,12},{1,13},{2,14},{3,15},{4,0},{5,1},{6,2},{7,3},{8,4},{9,5},{1... | collective-permute-start | bytes 835592 | tf_op jit(solution)/shard_map/ppermute | solution.py:41
  74.5 17.4 %collective-permute-start.7 = (bf16[64,2176]{1,0:T(8,128)(2,1)S(1)}, bf16[64,2176]{1,0:T(8,128)(2,1)S(1)}, u32[]{:S(2)}, u32[]{:S(2)}) collective-permute-start(bf16[64,2176]{1,0:T(8,128)(2,1)S(1)} %get-tuple-element.18), channel_id=1, source_target_pairs={{0,8},{1,9},{2,10},{3,11},{4,12},{5,13},{6,14},{7,15},{8,0},{9,1},... | collective-permute-start | bytes 835592 | tf_op jit(solution)/shard_map/ppermute | solution.py:41
  76.8 15.2 %collective-permute-start.8 = (bf16[64,2176]{1,0:T(8,128)(2,1)S(1)}, bf16[64,2176]{1,0:T(8,128)(2,1)S(1)}, u32[]{:S(2)}, u32[]{:S(2)}) collective-permute-start(bf16[64,2176]{1,0:T(8,128)(2,1)S(1)} %get-tuple-element.18), channel_id=1, source_target_pairs={{0,4},{1,5},{2,6},{3,7},{4,8},{5,9},{6,10},{7,11},{8,12},{9,13},{1... | collective-permute-start | bytes 835592 | tf_op jit(solution)/shard_map/ppermute | solution.py:41
  86.1 12.9 %collective-permute-start.31 = (bf16[64,2176]{1,0:T(8,128)(2,1)S(1)}, bf16[64,2176]{1,0:T(8,128)(2,1)S(1)}, u32[]{:S(2)}, u32[]{:S(2)}) collective-permute-start(bf16[64,2176]{1,0:T(8,128)(2,1)S(1)} %get-tuple-element.24), channel_id=1, source_target_pairs={{0,12},{1,13},{2,14},{3,15},{4,0},{5,1},{6,2},{7,3},{8,4},{9,5},{1... | collective-permute-start | bytes 835592 | tf_op jit(solution)/shard_map/ppermute | solution.py:41
  87.8 11.2 %collective-permute-start.32 = (bf16[64,2176]{1,0:T(8,128)(2,1)S(1)}, bf16[64,2176]{1,0:T(8,128)(2,1)S(1)}, u32[]{:S(2)}, u32[]{:S(2)}) collective-permute-start(bf16[64,2176]{1,0:T(8,128)(2,1)S(1)} %get-tuple-element.24), channel_id=1, source_target_pairs={{0,8},{1,9},{2,10},{3,11},{4,12},{5,13},{6,14},{7,15},{8,0},{9,1},... | collective-permute-start | bytes 835592 | tf_op jit(solution)/shard_map/ppermute | solution.py:41
  90.3 9.0 %collective-permute-start.33 = (bf16[64,2176]{1,0:T(8,128)(2,1)S(1)}, bf16[64,2176]{1,0:T(8,128)(2,1)S(1)}, u32[]{:S(2)}, u32[]{:S(2)}) collective-permute-start(bf16[64,2176]{1,0:T(8,128)(2,1)S(1)} %get-tuple-element.24), channel_id=1, source_target_pairs={{0,4},{1,5},{2,6},{3,7},{4,8},{5,9},{6,10},{7,11},{8,12},{9,13},{1... | collective-permute-start | bytes 835592 | tf_op jit(solution)/shard_map/ppermute | solution.py:41
  92.0 2.2 %slice-start.2 = ((s8[7340032]{0:T(1024)(128)(4,1)}), s8[4194304]{0:T(1024)(128)(4,1)S(1)}, s32[]{:S(2)}) async-start(s8[7340032]{0:T(1024)(128)(4,1)} %bitcast.83), calls=%async_computation.4 | async-start | bytes 8388608
  92.4 2.9 %slice-start.3 = ((s8[7340032]{0:T(1024)(128)(4,1)}), s8[3145728]{0:T(1024)(128)(4,1)S(1)}, s32[]{:S(2)}) async-start(s8[7340032]{0:T(1024)(128)(4,1)} %bitcast.83), calls=%async_computation.5 | async-start | bytes 6291456
  102.3 17.3 %collective-permute-start.10 = (bf16[128,1792]{1,0:T(8,128)(2,1)S(1)}, bf16[128,1792]{1,0:T(8,128)(2,1)S(1)}, u32[]{:S(2)}, u32[]{:S(2)}) collective-permute-start(bf16[128,1792]{1,0:T(8,128)(2,1)S(1)} %convolution_convert_fusion.6), channel_id=1, source_target_pairs={{0,16},{1,17},{2,18},{3,19},{4,20},{5,21},{6,22},{7,23},{8,24},{9,... | collective-permute-start | bytes 1376264 | tf_op jit(solution)/shard_map/ppermute | solution.py:56
  102.4 17.2 %collective-permute-start.9 = (bf16[128,1792]{1,0:T(8,128)(2,1)S(1)}, bf16[128,1792]{1,0:T(8,128)(2,1)S(1)}, u32[]{:S(2)}, u32[]{:S(2)}) collective-permute-start(bf16[128,1792]{1,0:T(8,128)(2,1)S(1)} %convolution_convert_fusion.7), channel_id=1, source_target_pairs={{0,16},{1,17},{2,18},{3,19},{4,20},{5,21},{6,22},{7,23},{8,24},{9,... | collective-permute-start | bytes 1376264 | tf_op jit(solution)/shard_map/ppermute | solution.py:56
  102.9 2.2 %collective-permute-start.11 = (f32[128,128]{1,0:T(8,128)S(1)}, f32[128,128]{1,0:T(8,128)S(1)}, u32[]{:S(2)}, u32[]{:S(2)}) collective-permute-start(f32[128,128]{1,0:T(8,128)S(1)} %fusion.57), channel_id=1, source_target_pairs={{0,16},{1,17},{2,18},{3,19},{4,20},{5,21},{6,22},{7,23},{8,24},{9,... | collective-permute-start | bytes 196616 | tf_op jit(solution)/shard_map/ppermute | solution.py:56
  103.0 23.0 %collective-permute-start.34 = (bf16[128,1792]{1,0:T(8,128)(2,1)S(1)}, bf16[128,1792]{1,0:T(8,128)(2,1)S(1)}, u32[]{:S(2)}, u32[]{:S(2)}) collective-permute-start(bf16[128,1792]{1,0:T(8,128)(2,1)S(1)} %convolution_convert_fusion.3), channel_id=1, source_target_pairs={{0,16},{1,17},{2,18},{3,19},{4,20},{5,21},{6,22},{7,23},{8,24},{9,... | collective-permute-start | bytes 1376264 | tf_op jit(solution)/shard_map/ppermute | solution.py:56
  103.4 22.6 %collective-permute-start.35 = (bf16[128,1792]{1,0:T(8,128)(2,1)S(1)}, bf16[128,1792]{1,0:T(8,128)(2,1)S(1)}, u32[]{:S(2)}, u32[]{:S(2)}) collective-permute-start(bf16[128,1792]{1,0:T(8,128)(2,1)S(1)} %convolution_convert_fusion.2), channel_id=1, source_target_pairs={{0,16},{1,17},{2,18},{3,19},{4,20},{5,21},{6,22},{7,23},{8,24},{9,... | collective-permute-start | bytes 1376264 | tf_op jit(solution)/shard_map/ppermute | solution.py:56
  105.1 18.1 %collective-permute-start.36 = (f32[128,128]{1,0:T(8,128)S(1)}, f32[128,128]{1,0:T(8,128)S(1)}, u32[]{:S(2)}, u32[]{:S(2)}) collective-permute-start(f32[128,128]{1,0:T(8,128)S(1)} %fusion.56), channel_id=1, source_target_pairs={{0,16},{1,17},{2,18},{3,19},{4,20},{5,21},{6,22},{7,23},{8,24},{9,... | collective-permute-start | bytes 196616 | tf_op jit(solution)/shard_map/ppermute | solution.py:56
  119.6 36.4 %slice-start = ((s8[7340032]{0:T(1024)(128)(4,1)}), s8[4194304]{0:T(1024)(128)(4,1)S(1)}, s32[]{:S(2)}) async-start(s8[7340032]{0:T(1024)(128)(4,1)} %bitcast.81), calls=%async_computation.2 | async-start | bytes 8388608
  119.9 36.1 %slice-start.1 = ((s8[7340032]{0:T(1024)(128)(4,1)}), s8[3145728]{0:T(1024)(128)(4,1)S(1)}, s32[]{:S(2)}) async-start(s8[7340032]{0:T(1024)(128)(4,1)} %bitcast.81), calls=%async_computation.3 | async-start | bytes 6291456
  119.9 10.3 %collective-permute-start.12 = (bf16[32,3712]{1,0:T(8,128)(2,1)S(1)}, bf16[32,3712]{1,0:T(8,128)(2,1)S(1)}, u32[]{:S(2)}, u32[]{:S(2)}) collective-permute-start(bf16[32,3712]{1,0:T(8,128)(2,1)S(1)} %get-tuple-element.20), channel_id=1, source_target_pairs={{0,64},{1,65},{2,66},{3,67},{4,68},{5,69},{6,70},{7,71},{8,72},{9,... | collective-permute-start | bytes 712712 | tf_op jit(solution)/shard_map/ppermute | solution.py:52
  122.5 12.9 %collective-permute-start.13 = (bf16[32,3712]{1,0:T(8,128)(2,1)S(1)}, bf16[32,3712]{1,0:T(8,128)(2,1)S(1)}, u32[]{:S(2)}, u32[]{:S(2)}) collective-permute-start(bf16[32,3712]{1,0:T(8,128)(2,1)S(1)} %get-tuple-element.21), channel_id=1, source_target_pairs={{0,32},{1,33},{2,34},{3,35},{4,36},{5,37},{6,38},{7,39},{8,40},{9,... | collective-permute-start | bytes 712712 | tf_op jit(solution)/shard_map/ppermute | solution.py:52
  123.1 13.5 %collective-permute-start.14 = (bf16[32,3712]{1,0:T(8,128)(2,1)S(1)}, bf16[32,3712]{1,0:T(8,128)(2,1)S(1)}, u32[]{:S(2)}, u32[]{:S(2)}) collective-permute-start(bf16[32,3712]{1,0:T(8,128)(2,1)S(1)} %get-tuple-element.22), channel_id=1, source_target_pairs={{0,96},{1,97},{2,98},{3,99},{4,100},{5,101},{6,102},{7,103},{8,104... | collective-permute-start | bytes 712712 | tf_op jit(solution)/shard_map/ppermute | solution.py:52
  126.3 14.9 %collective-permute-start.37 = (bf16[32,3712]{1,0:T(8,128)(2,1)S(1)}, bf16[32,3712]{1,0:T(8,128)(2,1)S(1)}, u32[]{:S(2)}, u32[]{:S(2)}) collective-permute-start(bf16[32,3712]{1,0:T(8,128)(2,1)S(1)} %get-tuple-element.26), channel_id=1, source_target_pairs={{0,64},{1,65},{2,66},{3,67},{4,68},{5,69},{6,70},{7,71},{8,72},{9,... | collective-permute-start | bytes 712712 | tf_op jit(solution)/shard_map/ppermute | solution.py:52
  127.4 18.1 %collective-permute-start.38 = (bf16[32,3712]{1,0:T(8,128)(2,1)S(1)}, bf16[32,3712]{1,0:T(8,128)(2,1)S(1)}, u32[]{:S(2)}, u32[]{:S(2)}) collective-permute-start(bf16[32,3712]{1,0:T(8,128)(2,1)S(1)} %get-tuple-element.27), channel_id=1, source_target_pairs={{0,32},{1,33},{2,34},{3,35},{4,36},{5,37},{6,38},{7,39},{8,40},{9,... | collective-permute-start | bytes 712712 | tf_op jit(solution)/shard_map/ppermute | solution.py:52
  130.2 15.3 %collective-permute-start.39 = (bf16[32,3712]{1,0:T(8,128)(2,1)S(1)}, bf16[32,3712]{1,0:T(8,128)(2,1)S(1)}, u32[]{:S(2)}, u32[]{:S(2)}) collective-permute-start(bf16[32,3712]{1,0:T(8,128)(2,1)S(1)} %get-tuple-element.28), channel_id=1, source_target_pairs={{0,96},{1,97},{2,98},{3,99},{4,100},{5,101},{6,102},{7,103},{8,104... | collective-permute-start | bytes 712712 | tf_op jit(solution)/shard_map/ppermute | solution.py:52
  136.9 11.4 %collective-permute-start.15 = (bf16[32,1792]{1,0:T(8,128)(2,1)S(1)}, bf16[32,1792]{1,0:T(8,128)(2,1)S(1)}, u32[]{:S(2)}, u32[]{:S(2)}) collective-permute-start(bf16[32,1792]{1,0:T(8,128)(2,1)S(1)} %shard_map.129), channel_id=1, source_target_pairs={{0,96},{1,97},{2,98},{3,99},{4,100},{5,101},{6,102},{7,103},{8,104... | collective-permute-start | bytes 344072 | tf_op jit(solution)/shard_map/ppermute | solution.py:52
  141.2 8.1 %collective-permute-start.16 = (bf16[32,1792]{1,0:T(8,128)(2,1)S(1)}, bf16[32,1792]{1,0:T(8,128)(2,1)S(1)}, u32[]{:S(2)}, u32[]{:S(2)}) collective-permute-start(bf16[32,1792]{1,0:T(8,128)(2,1)S(1)} %shard_map.129), channel_id=1, source_target_pairs={{0,64},{1,65},{2,66},{3,67},{4,68},{5,69},{6,70},{7,71},{8,72},{9,... | collective-permute-start | bytes 344072 | tf_op jit(solution)/shard_map/ppermute | solution.py:52
  141.2 8.3 %collective-permute-start.17 = (bf16[32,1792]{1,0:T(8,128)(2,1)S(1)}, bf16[32,1792]{1,0:T(8,128)(2,1)S(1)}, u32[]{:S(2)}, u32[]{:S(2)}) collective-permute-start(bf16[32,1792]{1,0:T(8,128)(2,1)S(1)} %shard_map.129), channel_id=1, source_target_pairs={{0,32},{1,33},{2,34},{3,35},{4,36},{5,37},{6,38},{7,39},{8,40},{9,... | collective-permute-start | bytes 344072 | tf_op jit(solution)/shard_map/ppermute | solution.py:52
  145.9 6.1 %collective-permute-start.40 = (bf16[32,1792]{1,0:T(8,128)(2,1)S(1)}, bf16[32,1792]{1,0:T(8,128)(2,1)S(1)}, u32[]{:S(2)}, u32[]{:S(2)}) collective-permute-start(bf16[32,1792]{1,0:T(8,128)(2,1)S(1)} %shard_map.132), channel_id=1, source_target_pairs={{0,96},{1,97},{2,98},{3,99},{4,100},{5,101},{6,102},{7,103},{8,104... | collective-permute-start | bytes 344072 | tf_op jit(solution)/shard_map/ppermute | solution.py:52
  146.6 7.3 %collective-permute-start.41 = (bf16[32,1792]{1,0:T(8,128)(2,1)S(1)}, bf16[32,1792]{1,0:T(8,128)(2,1)S(1)}, u32[]{:S(2)}, u32[]{:S(2)}) collective-permute-start(bf16[32,1792]{1,0:T(8,128)(2,1)S(1)} %shard_map.132), channel_id=1, source_target_pairs={{0,64},{1,65},{2,66},{3,67},{4,68},{5,69},{6,70},{7,71},{8,72},{9,... | collective-permute-start | bytes 344072 | tf_op jit(solution)/shard_map/ppermute | solution.py:52
  148.4 6.9 %collective-permute-start.42 = (bf16[32,1792]{1,0:T(8,128)(2,1)S(1)}, bf16[32,1792]{1,0:T(8,128)(2,1)S(1)}, u32[]{:S(2)}, u32[]{:S(2)}) collective-permute-start(bf16[32,1792]{1,0:T(8,128)(2,1)S(1)} %shard_map.132), channel_id=1, source_target_pairs={{0,32},{1,33},{2,34},{3,35},{4,36},{5,37},{6,38},{7,39},{8,40},{9,... | collective-permute-start | bytes 344072 | tf_op jit(solution)/shard_map/ppermute | solution.py:52
  149.5 6.0 %collective-permute-start.18 = (bf16[128,1792]{1,0:T(8,128)(2,1)S(1)}, bf16[128,1792]{1,0:T(8,128)(2,1)S(1)}, u32[]{:S(2)}, u32[]{:S(2)}) collective-permute-start(bf16[128,1792]{1,0:T(8,128)(2,1)S(1)} %pad_maximum_fusion), channel_id=1, source_target_pairs={{0,16},{1,17},{2,18},{3,19},{4,20},{5,21},{6,22},{7,23},{8,24},{9,... | collective-permute-start | bytes 1376264 | tf_op jit(solution)/shard_map/ppermute | solution.py:56
  155.3 5.1 %collective-permute-start.43 = (bf16[128,1792]{1,0:T(8,128)(2,1)S(1)}, bf16[128,1792]{1,0:T(8,128)(2,1)S(1)}, u32[]{:S(2)}, u32[]{:S(2)}) collective-permute-start(bf16[128,1792]{1,0:T(8,128)(2,1)S(1)} %pad_maximum_fusion.1), channel_id=1, source_target_pairs={{0,16},{1,17},{2,18},{3,19},{4,20},{5,21},{6,22},{7,23},{8,24},{9,... | collective-permute-start | bytes 1376264 | tf_op jit(solution)/shard_map/ppermute | solution.py:56
  163.8 8.0 %collective-permute-start.19 = (bf16[64,2048]{1,0:T(8,128)(2,1)S(1)}, bf16[64,2048]{1,0:T(8,128)(2,1)S(1)}, u32[]{:S(2)}, u32[]{:S(2)}) collective-permute-start(bf16[64,2048]{1,0:T(8,128)(2,1)S(1)} %convolution_convert_fusion.19), channel_id=1, source_target_pairs={{0,8},{1,9},{2,10},{3,11},{4,12},{5,13},{6,14},{7,15},{8,0},{9,1},... | collective-permute-start | bytes 786440 | tf_op jit(solution)/shard_map/ppermute | solution.py:41
  165.3 7.7 %collective-permute-start.20 = (bf16[64,2048]{1,0:T(8,128)(2,1)S(1)}, bf16[64,2048]{1,0:T(8,128)(2,1)S(1)}, u32[]{:S(2)}, u32[]{:S(2)}) collective-permute-start(bf16[64,2048]{1,0:T(8,128)(2,1)S(1)} %convolution_convert_fusion.18), channel_id=1, source_target_pairs={{0,4},{1,5},{2,6},{3,7},{4,8},{5,9},{6,10},{7,11},{8,12},{9,13},{1... | collective-permute-start | bytes 786440 | tf_op jit(solution)/shard_map/ppermute | solution.py:41
  166.9 7.6 %collective-permute-start.21 = (bf16[64,2048]{1,0:T(8,128)(2,1)S(1)}, bf16[64,2048]{1,0:T(8,128)(2,1)S(1)}, u32[]{:S(2)}, u32[]{:S(2)}) collective-permute-start(bf16[64,2048]{1,0:T(8,128)(2,1)S(1)} %convolution_convert_fusion.17), channel_id=1, source_target_pairs={{0,12},{1,13},{2,14},{3,15},{4,0},{5,1},{6,2},{7,3},{8,4},{9,5},{1... | collective-permute-start | bytes 786440 | tf_op jit(solution)/shard_map/ppermute | solution.py:41
  167.3 13.5 %collective-permute-start.44 = (bf16[64,2048]{1,0:T(8,128)(2,1)S(1)}, bf16[64,2048]{1,0:T(8,128)(2,1)S(1)}, u32[]{:S(2)}, u32[]{:S(2)}) collective-permute-start(bf16[64,2048]{1,0:T(8,128)(2,1)S(1)} %convolution_convert_fusion.12), channel_id=1, source_target_pairs={{0,8},{1,9},{2,10},{3,11},{4,12},{5,13},{6,14},{7,15},{8,0},{9,1},... | collective-permute-start | bytes 786440 | tf_op jit(solution)/shard_map/ppermute | solution.py:41
  169.4 14.7 %collective-permute-start.45 = (bf16[64,2048]{1,0:T(8,128)(2,1)S(1)}, bf16[64,2048]{1,0:T(8,128)(2,1)S(1)}, u32[]{:S(2)}, u32[]{:S(2)}) collective-permute-start(bf16[64,2048]{1,0:T(8,128)(2,1)S(1)} %convolution_convert_fusion.11), channel_id=1, source_target_pairs={{0,4},{1,5},{2,6},{3,7},{4,8},{5,9},{6,10},{7,11},{8,12},{9,13},{1... | collective-permute-start | bytes 786440 | tf_op jit(solution)/shard_map/ppermute | solution.py:41
  171.7 12.4 %collective-permute-start.46 = (bf16[64,2048]{1,0:T(8,128)(2,1)S(1)}, bf16[64,2048]{1,0:T(8,128)(2,1)S(1)}, u32[]{:S(2)}, u32[]{:S(2)}) collective-permute-start(bf16[64,2048]{1,0:T(8,128)(2,1)S(1)} %convolution_convert_fusion.10), channel_id=1, source_target_pairs={{0,12},{1,13},{2,14},{3,15},{4,0},{5,1},{6,2},{7,3},{8,4},{9,5},{1... | collective-permute-start | bytes 786440 | tf_op jit(solution)/shard_map/ppermute | solution.py:41
  176.0 10.6 %collective-permute-start.22 = (bf16[16,2048]{1,0:T(8,128)(2,1)S(1)}, bf16[16,2048]{1,0:T(8,128)(2,1)S(1)}, u32[]{:S(2)}, u32[]{:S(2)}) collective-permute-start(bf16[16,2048]{1,0:T(8,128)(2,1)S(1)} %get-tuple-element.35), channel_id=1, source_target_pairs={{0,2},{1,3},{2,0},{3,1},{4,6},{5,7},{6,4},{7,5},{8,10},{9,11},{10,... | collective-permute-start | bytes 196616 | tf_op jit(solution)/shard_map/ppermute | solution.py:48
  180.8 8.2 %collective-permute-start.23 = (bf16[16,2048]{1,0:T(8,128)(2,1)S(1)}, bf16[16,2048]{1,0:T(8,128)(2,1)S(1)}, u32[]{:S(2)}, u32[]{:S(2)}) collective-permute-start(bf16[16,2048]{1,0:T(8,128)(2,1)S(1)} %get-tuple-element.37), channel_id=1, source_target_pairs={{0,1},{1,2},{2,3},{3,0},{4,5},{5,6},{6,7},{7,4},{8,9},{9,10},{10,1... | collective-permute-start | bytes 196616 | tf_op jit(solution)/shard_map/ppermute | solution.py:48
  180.8 8.2 %collective-permute-start.24 = (bf16[16,2048]{1,0:T(8,128)(2,1)S(1)}, bf16[16,2048]{1,0:T(8,128)(2,1)S(1)}, u32[]{:S(2)}, u32[]{:S(2)}) collective-permute-start(bf16[16,2048]{1,0:T(8,128)(2,1)S(1)} %get-tuple-element.36), channel_id=1, source_target_pairs={{0,3},{1,0},{2,1},{3,2},{4,7},{5,4},{6,5},{7,6},{8,11},{9,8},{10,9... | collective-permute-start | bytes 196616 | tf_op jit(solution)/shard_map/ppermute | solution.py:48
  184.1 8.6 %copy-start.1 = (bf16[512,2048]{1,0:T(8,128)(2,1)S(1)}, bf16[512,2048]{1,0:T(8,128)(2,1)}, u32[]{:S(2)}) copy-start(bf16[512,2048]{1,0:T(8,128)(2,1)} %param.21) | copy-start | bytes 6291460
  185.6 6.0 %collective-permute-start.47 = (bf16[16,2048]{1,0:T(8,128)(2,1)S(1)}, bf16[16,2048]{1,0:T(8,128)(2,1)S(1)}, u32[]{:S(2)}, u32[]{:S(2)}) collective-permute-start(bf16[16,2048]{1,0:T(8,128)(2,1)S(1)} %get-tuple-element.38), channel_id=1, source_target_pairs={{0,2},{1,3},{2,0},{3,1},{4,6},{5,7},{6,4},{7,5},{8,10},{9,11},{10,... | collective-permute-start | bytes 196616 | tf_op jit(solution)/shard_map/ppermute | solution.py:48
  185.7 6.2 %collective-permute-start.48 = (bf16[16,2048]{1,0:T(8,128)(2,1)S(1)}, bf16[16,2048]{1,0:T(8,128)(2,1)S(1)}, u32[]{:S(2)}, u32[]{:S(2)}) collective-permute-start(bf16[16,2048]{1,0:T(8,128)(2,1)S(1)} %get-tuple-element.40), channel_id=1, source_target_pairs={{0,1},{1,2},{2,3},{3,0},{4,5},{5,6},{6,7},{7,4},{8,9},{9,10},{10,1... | collective-permute-start | bytes 196616 | tf_op jit(solution)/shard_map/ppermute | solution.py:48
  186.7 5.3 %collective-permute-start.49 = (bf16[16,2048]{1,0:T(8,128)(2,1)S(1)}, bf16[16,2048]{1,0:T(8,128)(2,1)S(1)}, u32[]{:S(2)}, u32[]{:S(2)}) collective-permute-start(bf16[16,2048]{1,0:T(8,128)(2,1)S(1)} %get-tuple-element.39), channel_id=1, source_target_pairs={{0,3},{1,0},{2,1},{3,2},{4,7},{5,4},{6,5},{7,6},{8,11},{9,8},{10,9... | collective-permute-start | bytes 196616 | tf_op jit(solution)/shard_map/ppermute | solution.py:48

commit v2 on v1

--- a/solution.py
+++ b/solution.py
@@ -76,6 +76,10 @@
 
 def one_hot_rows(index, count):
     return (index[:, None] == jnp.arange(count, dtype=jnp.int32)[None, :]).astype(BF16)
+
+
+def after(value, earlier):
+    return lax.optimization_barrier((value, earlier))[0]
 
 
 def pick(matrix, values):
@@ -117,16 +121,23 @@
         payload[here, width:] = ends_of(jnp.sum(total * total, axis=1, keepdims=True))
 
 
-def pair_kernel(gate, upper, ends, gate_other, upper_other, ends_other, *payloads):
+def gift_kernel(gate, upper, ends, gift):
+    width = gate.shape[1]
+    gift[:, :width] = gate[...]
+    gift[:, width : 2 * width] = upper[...]
+    gift[:, 2 * width :] = ends[...]
+
+
+def pair_kernel(gate, upper, ends, other, *payloads):
     half = gate.shape[0] // RING
     width = gate.shape[1]
     for i, payload in enumerate(payloads):
         here = pl.ds(i * half, half)
-        payload[:, :width] = (gate[here, :] + gate_other[here, :].astype(F32)).astype(BF16)
+        payload[:, :width] = (gate[here, :] + other[here, :width].astype(F32)).astype(BF16)
         payload[:, width : 2 * width] = (
-            upper[here, :] + upper_other[here, :].astype(F32)
+            upper[here, :] + other[here, width : 2 * width].astype(F32)
         ).astype(BF16)
-        both = ends[here, :] + ends_other[here, :]
+        both = ends[here, :].astype(F32) + other[here, 2 * width :].astype(F32)
         payload[:, 2 * width :] = ends_of(both[:, :1] + both[:, HD // 2 : HD // 2 + 1])
 
 
@@ -203,8 +214,8 @@
 
     slot_here = index_gx * group_slots + jnp.arange(group_slots, dtype=jnp.int32)
     routing = cache_slot[None, :] == slot_here[:, None]
-    outgoing = pick(
-        routing.astype(BF16), jnp.concatenate([queries, new_keys, new_values], axis=1)
+    outgoing = jnp.concatenate(
+        [pick(routing.astype(BF16), values) for values in (queries, new_keys, new_values)], axis=1
     )
     valid = jnp.sum(jnp.where(routing, lengths[None, :], 0), axis=1)
     valid_own = lax.dynamic_slice_in_dim(valid, index_yz * per_device, per_device)
@@ -236,12 +247,21 @@
         tiled=True,
     ).reshape(rows, head_width)
 
-    def turn(number):
-        positions = jnp.arange(rows // TURNS, dtype=jnp.int32)
-        piece = block // TURNS
-        chunk = RING * piece
-
-        far, near, inner = positions // chunk, (positions // piece) % RING, positions % piece
+    positions = jnp.arange(rows // TURNS, dtype=jnp.int32)
+    piece = block // TURNS
+    chunk = RING * piece
+    half = chunk // CORES
+    hidden_width = gate_weight.shape[1]
+    far, near, inner = positions // chunk, (positions // piece) % RING, positions % piece
+
+    def sum_first(values, weight):
+        parts = {}
+        for j in FAR_FIRST:
+            part = jnp.dot(values[j * chunk : (j + 1) * chunk], weight, preferred_element_type=F32)
+            parts[j] = part if j == 0 else part.astype(BF16)
+        return add_up(parts[0], spread(send_first, parts))
+
+    def project(number):
         row_x = jnp.where(core == 0, x + far, x + near) % RING
         row_y = jnp.where(core == 0, y + near, y + far) % RING
         row_here = (row_x * RING + row_y) * block + number * piece + inner
@@ -249,16 +269,6 @@
             jnp.where(row_here[:, None] == jnp.arange(rows)[None, :], cache_slot[None, :], 0), axis=1
         )
         context_rows = pick(one_hot_rows(slot_of, rows), all_columns)
-
-        def sum_first(values, weight):
-            parts = {}
-            for j in FAR_FIRST:
-                part = jnp.dot(
-                    values[j * chunk : (j + 1) * chunk], weight, preferred_element_type=F32
-                )
-                parts[j] = part if j == 0 else part.astype(BF16)
-            return add_up(parts[0], spread(send_first, parts))
-
         part = sum_first(context_rows, out_weight)
         others = collect(send_second, part.astype(BF16))[1:]
         resid_rows = pick(one_hot_rows(row_here[:chunk], rows), resid)
@@ -273,9 +283,9 @@
             resid_rows,
             norm_gain[None, :],
         )
-        blocks = jnp.concatenate(collect(send_first, payload), axis=0)
-
-        half = chunk // CORES
+        return middle, jnp.concatenate(collect(send_first, payload), axis=0)
+
+    def gate_and_up(blocks):
         target = positions[: RING * half] // half
         distance = jnp.zeros_like(target)
         for order_index, j in enumerate(FAR_FIRST):
@@ -287,35 +297,39 @@
             part_y = part_core * (RING // CORES) + inner_half // piece
             source = jnp.where(core == 0, part_x * RING + part_y, part_y * RING + part_x)
             matrix = one_hot_rows(source * piece + inner_half % piece, rows // TURNS)
-            ends = jnp.dot(matrix, blocks[:, width:], preferred_element_type=F32)
-            return pick(matrix, blocks[:, :width]), ends
+            return pick(matrix, blocks[:, :width]), pick(matrix, blocks[:, width:])
 
         other_rows, other_ends = half_rows(1 - core)
         own_rows, own_ends = half_rows(core)
-        other_ends = send_core(other_ends)
-        other_gate = send_core(pick(other_rows, gate_weight))
-        other_upper = send_core(pick(other_rows, up_weight))
-        hidden_width = gate_weight.shape[1]
+        sums_width = 2 * hidden_width + HD
+        (gift,) = local_kernel(
+            gift_kernel,
+            [jax.ShapeDtypeStruct((RING * half, sums_width), BF16)],
+            pick(other_rows, gate_weight),
+            pick(other_rows, up_weight),
+            other_ends,
+        )
         payloads = local_kernel(
             pair_kernel,
-            [jax.ShapeDtypeStruct((half, 2 * hidden_width + HD), BF16)] * RING,
+            [jax.ShapeDtypeStruct((half, sums_width), BF16)] * RING,
             jnp.dot(own_rows, gate_weight, preferred_element_type=F32),
             jnp.dot(own_rows, up_weight, preferred_element_type=F32),
             own_ends,
-            other_gate,
-            other_upper,
-            other_ends,
-        )
-        parts = dict(zip(FAR_FIRST, payloads))
+            send_core(gift),
+        )
+        return dict(zip(FAR_FIRST, payloads))
+
+    def activate(own, others):
         (hidden,) = local_kernel(
             functools.partial(hidden_kernel, width * count_gx),
             [jax.ShapeDtypeStruct((half, hidden_width), BF16)],
-            parts[0],
-            *spread(send_z, parts),
-        )
-
+            own,
+            *others,
+        )
         own_hidden = jnp.concatenate(collect(send_z, hidden), axis=0)
-        all_hidden = jnp.concatenate([own_hidden, send_core(own_hidden)], axis=0)
+        return hidden, jnp.concatenate([own_hidden, send_core(own_hidden)], axis=0)
+
+    def finish(middle, all_hidden):
         place_x = jnp.where(core == 0, far, near)
         place_y = jnp.where(core == 0, near, far)
         place_core = (place_y // (RING // CORES) + core) % CORES
@@ -330,7 +344,16 @@
         projected = add_up(parts[0], spread(send_second, parts))
         return (middle.astype(F32) + projected).astype(BF16)
 
-    return jnp.concatenate([turn(number) for number in range(TURNS)], axis=0)
+    middles, blocks = zip(*[project(number) for number in range(TURNS)])
+    parts = [gate_and_up(blocks[0])]
+    for number in range(1, TURNS):
+        parts.append(gate_and_up(blocks[number]))
+    results = []
+    for number in range(TURNS):
+        own = parts[number][0]
+        hidden, all_hidden = activate(own, spread(send_z, parts[number]))
+        results.append(finish(middles[number], all_hidden))
+    return jnp.concatenate(results, axis=0)
 
 
 def solution(mesh):

time: 195 us -> 195 us (level)
  matrix products: 39.1 us -> 41.3 us
    ppermute x8 -> x4, starting transfers between devices: 15.9 us -> 0.83 us  [send_core(): lax.ppermute(value, AXES, pairs(lambda x, y, z, core: (x, y, z, 1 - core)))]
    ppermute x12, starting transfers between devices: 16.6 us -> 30.3 us  [send_z(): lax.ppermute(value, AXES, pairs(lambda x, y, z, core: (x, y, z + step, co...]
    dot_general x15 -> x21, matrix products: 14.1 us -> 17 us  [pick(): return jnp.dot(matrix, values, preferred_element_type=F32).astype(BF16)]
    unnamed x40 -> x36, local copies, waits for them, and re-layouts: 3.97 us -> 2.06 us
    dot_general x8 -> x4, matrix products: 5.34 us -> 4.55 us  [the longest x2 2.27 us: gate_and_up(): jnp.dot(own_rows, gate_weight, preferred_element_type=F32)]
  transfers between devices with their start and end apart: 52 -> 48, of which waited for: 20 -> 21; matrix products, arithmetic and copies ran while one was open for 13% -> 13% of each run, Pallas kernels for 1% -> 1%
where the time goes in v2:
time: 195 us; the launch traced here: 192 us
  starting transfers between devices  92.2 us (47%)
  waiting for transfers between devices  47.7 us (24%)
  matrix products  41.3 us (21%)
  local copies, waits for them, and re-layouts  5.42 us (3%)
  other arithmetic  2.55 us (1%)
  Pallas kernels  2.04 us (1%)
    ppermute x12, starting transfers between devices, send_z(): lax.ppermute(value, AXES, pairs(lambda x, y, z, core: (x, y, z + step, co...  30.3 us
    ppermute x18, starting transfers between devices, send_first(): return lax.ppermute(value, AXES, pairs(move))  27.6 us
    ppermute x12, starting transfers between devices, send_second(): return lax.ppermute(value, AXES, pairs(move))  17.5 us
    dot_general x21, matrix products, pick(): return jnp.dot(matrix, values, preferred_element_type=F32).astype(BF16)  17 us
    ppermute x12, waiting for transfers between devices, send_z(): lax.ppermute(value, AXES, pairs(lambda x, y, z, core: (x, y, z + step, co...  16.2 us
    dot_general x16, matrix products, sum_first(): jnp.dot(values[j * chunk:(j + 1) * chunk], weight, preferred_element_type...  15.6 us
    ppermute x12, waiting for transfers between devices, send_second(): return lax.ppermute(value, AXES, pairs(move))  11 us
    all_to_all x1, waiting for transfers between devices, on_device(): lax.all_to_all(outgoing.reshape(count_gx * count_yz, per_device, head_wid...  9.52 us
  transfers between devices with their start and end apart: 48, of which 21 were waited for; matrix products, arithmetic and copies ran while one was open for 13% of the time, Pallas kernels for 1%

profile of v2, /device:TPU:6, one launch (start us, length us, event | category | flops | bytes accessed | tf_op | source)
XLA Modules:
  0.0 192.3 jit_solution(2637578614538628559)
XLA Ops:
  0.0 1.4 convolution_convert_fusion.26
  4.4 7.4 %all-to-all-start = ((bf16[16,4,576]{2,1,0:T(4,128)(2,1)}), bf16[16,4,576]{2,1,0:T(4,128)(2,1)S(1)}, u32[]{:S(2)}, u32[]{:S(2)}) async-start(bf16[16,4,576]{2,1,0:T(4,128)(2,1)} %all_to_all.9), calls=%async_computation | async-start | bytes 163840 | tf_op jit(solution)/shard_map/all_to_all | solution.py:222
  12.9 2.1 %convolution_convert_fusion.20.resid = bf16[64,2048]{1,0:T(8,128)(2,1)S(1)} fusion(bf16[512,2048]{1,0:T(8,128)(2,1)} %param.13, s32[64]{0:T(128)S(1)} %slice.130), kind=kOutput, calls=%fused_computation.20 | convolution fusion | flops 134381568 | bytes 2359552 | tf_op jit(solution)/shard_map/dot_general | solution.py:86
  15.1 2.4 %all-to-all-done = bf16[16,4,576]{2,1,0:T(4,128)(2,1)S(1)} async-done(((bf16[16,4,576]{2,1,0:T(4,128)(2,1)}), bf16[16,4,576]{2,1,0:T(4,128)(2,1)S(1)}, u32[]{:S(2)}, u32[]{:S(2)}) %all-to-all-start) | async-done | bytes 73760 | tf_op jit(solution)/shard_map/all_to_all | solution.py:222
  17.9 2.1 %fusion.115 = (f32[4,4,16]{2,1,0:T(4,128)S(1)}, f32[4,4,16,384]{3,2,1,0:T(8,128)S(1)}) fusion(bf16[4,4,16,128]{3,2,1,0:T(8,128)(2,1)S(1)} %bitcast.92, pred[4,384]{1,0:T(4,128)(4,1)S(1)} %iota_compare_fusion.23, bf16[4,384,512]{2,1,0:T(8,128)(2,1)} %param.17), kind=kOutput, calls=%fused_computation.230 | convolution fusion | flops 25460480 | bytes 2034176 | tf_op jit(solution)/shard_map/bkgd,bckd->bkgc/dot_general | solution.py:166
  20.4 1.9 fusion.15
  23.4 8.6 %all-to-all-start.1 = ((bf16[128,4,512]{2,1,0:T(4,128)(2,1)}), bf16[128,4,512]{2,1,0:T(4,128)(2,1)S(1)}, u32[]{:S(2)}, u32[]{:S(2)}) async-start(bf16[128,4,512]{2,1,0:T(4,128)(2,1)} %bitcast.90), calls=%async_computation.1 | async-start | bytes 1048576 | tf_op jit(solution)/shard_map/all_to_all | solution.py:242
  32.3 2.1 %convolution_convert_fusion.13.resid = bf16[64,2048]{1,0:T(8,128)(2,1)S(1)} fusion(bf16[512,2048]{1,0:T(8,128)(2,1)} %param.13, s32[64]{0:T(128)S(1)} %slice.146), kind=kOutput, calls=%fused_computation.13 | convolution fusion | flops 134381568 | bytes 2359552 | tf_op jit(solution)/shard_map/dot_general | solution.py:86
  34.4 9.5 %all-to-all-done.1 = bf16[128,4,512]{2,1,0:T(4,128)(2,1)S(1)} async-done(((bf16[128,4,512]{2,1,0:T(4,128)(2,1)}), bf16[128,4,512]{2,1,0:T(4,128)(2,1)S(1)}, u32[]{:S(2)}, u32[]{:S(2)}) %all-to-all-start.1) | async-done | bytes 524320 | tf_op jit(solution)/shard_map/all_to_all | solution.py:242
  44.8 1.4 convolution_convert_fusion.25
  49.1 2.8 %collective-permute-start = (bf16[64,2048]{1,0:T(8,128)(2,1)S(1)}, bf16[64,2048]{1,0:T(8,128)(2,1)S(1)}, u32[]{:S(2)}, u32[]{:S(2)}) collective-permute-start(bf16[64,2048]{1,0:T(8,128)(2,1)S(1)} %convolution_convert_fusion.23), channel_id=1, source_target_pairs={{0,8},{1,9},{2,10},{3,11},{4,12},{5,13},{6,14},{7,15},{8,0},{9,1},... | collective-permute-start | bytes 786440 | tf_op jit(solution)/shard_map/ppermute | solution.py:41
  52.8 1.1 collective-permute-start.2
  54.8 2.6 %collective-permute-start.24 = (bf16[64,2048]{1,0:T(8,128)(2,1)S(1)}, bf16[64,2048]{1,0:T(8,128)(2,1)S(1)}, u32[]{:S(2)}, u32[]{:S(2)}) collective-permute-start(bf16[64,2048]{1,0:T(8,128)(2,1)S(1)} %convolution_convert_fusion.15), channel_id=1, source_target_pairs={{0,4},{1,5},{2,6},{3,7},{4,8},{5,9},{6,10},{7,11},{8,12},{9,13},{1... | collective-permute-start | bytes 786440 | tf_op jit(solution)/shard_map/ppermute | solution.py:41
  58.1 1.8 collective-permute-done.1
  60.0 3.2 %collective-permute-done.2 = bf16[64,2048]{1,0:T(8,128)(2,1)S(1)} collective-permute-done((bf16[64,2048]{1,0:T(8,128)(2,1)S(1)}, bf16[64,2048]{1,0:T(8,128)(2,1)S(1)}, u32[]{:S(2)}, u32[]{:S(2)}) %collective-permute-start.2) | collective-permute-done | bytes 262176 | tf_op jit(solution)/shard_map/ppermute | solution.py:41
  63.9 2.7 %collective-permute-start.4 = (bf16[64,2048]{1,0:T(8,128)(2,1)S(1)}, bf16[64,2048]{1,0:T(8,128)(2,1)S(1)}, u32[]{:S(2)}, u32[]{:S(2)}) collective-permute-start(bf16[64,2048]{1,0:T(8,128)(2,1)S(1)} %get-tuple-element.47), channel_id=1, source_target_pairs={{0,2},{1,3},{2,0},{3,1},{4,6},{5,7},{6,4},{7,5},{8,10},{9,11},{10,... | collective-permute-start | bytes 786440 | tf_op jit(solution)/shard_map/ppermute | solution.py:48
  66.5 1.4 collective-permute-done.24
  68.7 2.0 %collective-permute-start.26 = (bf16[64,2048]{1,0:T(8,128)(2,1)S(1)}, bf16[64,2048]{1,0:T(8,128)(2,1)S(1)}, u32[]{:S(2)}, u32[]{:S(2)}) collective-permute-start(bf16[64,2048]{1,0:T(8,128)(2,1)S(1)} %get-tuple-element.51), channel_id=1, source_target_pairs={{0,3},{1,0},{2,1},{3,2},{4,7},{5,4},{6,5},{7,6},{8,11},{9,8},{10,9... | collective-permute-start | bytes 786440 | tf_op jit(solution)/shard_map/ppermute | solution.py:48
  72.0 2.6 %collective-permute-done.5.far_three = bf16[64,2048]{1,0:T(8,128)(2,1)S(1)} collective-permute-done((bf16[64,2048]{1,0:T(8,128)(2,1)S(1)}, bf16[64,2048]{1,0:T(8,128)(2,1)S(1)}, u32[]{:S(2)}, u32[]{:S(2)}) %collective-permute-start.5) | collective-permute-done | bytes 262176 | tf_op jit(solution)/shard_map/ppermute | solution.py:48
  75.0 2.2 %collective-permute-start.7 = (bf16[64,2176]{1,0:T(8,128)(2,1)S(1)}, bf16[64,2176]{1,0:T(8,128)(2,1)S(1)}, u32[]{:S(2)}, u32[]{:S(2)}) collective-permute-start(bf16[64,2176]{1,0:T(8,128)(2,1)S(1)} %get-tuple-element.18), channel_id=1, source_target_pairs={{0,8},{1,9},{2,10},{3,11},{4,12},{5,13},{6,14},{7,15},{8,0},{9,1},... | collective-permute-start | bytes 835592 | tf_op jit(solution)/shard_map/ppermute | solution.py:41
  77.2 3.4 %collective-permute-start.8 = (bf16[64,2176]{1,0:T(8,128)(2,1)S(1)}, bf16[64,2176]{1,0:T(8,128)(2,1)S(1)}, u32[]{:S(2)}, u32[]{:S(2)}) collective-permute-start(bf16[64,2176]{1,0:T(8,128)(2,1)S(1)} %get-tuple-element.18), channel_id=1, source_target_pairs={{0,4},{1,5},{2,6},{3,7},{4,8},{5,9},{6,10},{7,11},{8,12},{9,13},{1... | collective-permute-start | bytes 835592 | tf_op jit(solution)/shard_map/ppermute | solution.py:41
  80.7 5.6 %collective-permute-done.28.far_three = bf16[64,2048]{1,0:T(8,128)(2,1)S(1)} collective-permute-done((bf16[64,2048]{1,0:T(8,128)(2,1)S(1)}, bf16[64,2048]{1,0:T(8,128)(2,1)S(1)}, u32[]{:S(2)}, u32[]{:S(2)}) %collective-permute-start.28) | collective-permute-done | bytes 262176 | tf_op jit(solution)/shard_map/ppermute | solution.py:48
  86.5 1.8 collective-permute-start.29
  88.3 2.5 %collective-permute-start.30 = (bf16[64,2176]{1,0:T(8,128)(2,1)S(1)}, bf16[64,2176]{1,0:T(8,128)(2,1)S(1)}, u32[]{:S(2)}, u32[]{:S(2)}) collective-permute-start(bf16[64,2176]{1,0:T(8,128)(2,1)S(1)} %get-tuple-element.24), channel_id=1, source_target_pairs={{0,8},{1,9},{2,10},{3,11},{4,12},{5,13},{6,14},{7,15},{8,0},{9,1},... | collective-permute-start | bytes 835592 | tf_op jit(solution)/shard_map/ppermute | solution.py:41
  90.8 1.5 collective-permute-start.31
  92.8 1.1 convolution_convert_fusion.6.upper
  94.6 1.1 slice-done.3
  95.7 1.1 convolution_convert_fusion.7.gate
  97.2 1.1 fusion.121.gate
  98.3 1.1 fusion.122.upper
  100.2 1.1 convolution_convert_fusion.2.upper
  101.3 1.1 convolution_convert_fusion.3.gate
  103.9 1.1 fusion.123.gate
  105.7 15.0 %collective-permute-start.10 = (bf16[32,3712]{1,0:T(8,128)(2,1)S(1)}, bf16[32,3712]{1,0:T(8,128)(2,1)S(1)}, u32[]{:S(2)}, u32[]{:S(2)}) collective-permute-start(bf16[32,3712]{1,0:T(8,128)(2,1)S(1)} %get-tuple-element.20), channel_id=1, source_target_pairs={{0,64},{1,65},{2,66},{3,67},{4,68},{5,69},{6,70},{7,71},{8,72},{9,... | collective-permute-start | bytes 712712 | tf_op jit(solution)/shard_map/ppermute | solution.py:52
  120.7 1.1 fusion.124.upper
  122.6 2.6 %collective-permute-start.12 = (bf16[32,3712]{1,0:T(8,128)(2,1)S(1)}, bf16[32,3712]{1,0:T(8,128)(2,1)S(1)}, u32[]{:S(2)}, u32[]{:S(2)}) collective-permute-start(bf16[32,3712]{1,0:T(8,128)(2,1)S(1)} %get-tuple-element.22), channel_id=1, source_target_pairs={{0,96},{1,97},{2,98},{3,99},{4,100},{5,101},{6,102},{7,103},{8,104... | collective-permute-start | bytes 712712 | tf_op jit(solution)/shard_map/ppermute | solution.py:52
  125.8 1.1 collective-permute-start.33
  126.9 1.2 collective-permute-start.34
  128.1 1.5 collective-permute-done.10.one
  130.7 4.1 %collective-permute-done.11.two = bf16[32,3712]{1,0:T(8,128)(2,1)S(1)} collective-permute-done((bf16[32,3712]{1,0:T(8,128)(2,1)S(1)}, bf16[32,3712]{1,0:T(8,128)(2,1)S(1)}, u32[]{:S(2)}, u32[]{:S(2)}) %collective-permute-start.11) | collective-permute-done | bytes 237600 | tf_op jit(solution)/shard_map/ppermute | solution.py:52
  134.8 1.2 collective-permute-done.12.three
  136.3 4.3 %collective-permute-start.13 = (bf16[32,1792]{1,0:T(8,128)(2,1)S(1)}, bf16[32,1792]{1,0:T(8,128)(2,1)S(1)}, u32[]{:S(2)}, u32[]{:S(2)}) collective-permute-start(bf16[32,1792]{1,0:T(8,128)(2,1)S(1)} %shard_map.130), channel_id=1, source_target_pairs={{0,96},{1,97},{2,98},{3,99},{4,100},{5,101},{6,102},{7,103},{8,104... | collective-permute-start | bytes 344072 | tf_op jit(solution)/shard_map/ppermute | solution.py:52
  141.6 3.3 %collective-permute-done.34.two = bf16[32,3712]{1,0:T(8,128)(2,1)S(1)} collective-permute-done((bf16[32,3712]{1,0:T(8,128)(2,1)S(1)}, bf16[32,3712]{1,0:T(8,128)(2,1)S(1)}, u32[]{:S(2)}, u32[]{:S(2)}) %collective-permute-start.34) | collective-permute-done | bytes 237600 | tf_op jit(solution)/shard_map/ppermute | solution.py:52
  146.0 1.8 collective-permute-start.37
  149.1 2.3 %collective-permute-done.36 = bf16[32,1792]{1,0:T(8,128)(2,1)S(1)} collective-permute-done((bf16[32,1792]{1,0:T(8,128)(2,1)S(1)}, bf16[32,1792]{1,0:T(8,128)(2,1)S(1)}, u32[]{:S(2)}, u32[]{:S(2)}) %collective-permute-start.36) | collective-permute-done | bytes 114720 | tf_op jit(solution)/shard_map/ppermute | solution.py:52
  151.3 1.9 %collective-permute-done.37 = bf16[32,1792]{1,0:T(8,128)(2,1)S(1)} collective-permute-done((bf16[32,1792]{1,0:T(8,128)(2,1)S(1)}, bf16[32,1792]{1,0:T(8,128)(2,1)S(1)}, u32[]{:S(2)}, u32[]{:S(2)}) %collective-permute-start.37) | collective-permute-done | bytes 114720 | tf_op jit(solution)/shard_map/ppermute | solution.py:52
  153.3 1.5 collective-permute-done.38
  155.5 1.4 convolution_convert_fusion.19
  157.0 1.4 convolution_convert_fusion.18
  158.4 1.4 convolution_convert_fusion.17
  160.3 1.4 convolution_convert_fusion.12
  161.8 1.4 convolution_convert_fusion.11
  163.2 1.5 collective-permute-start.17
  164.7 1.6 collective-permute-start.18
  166.8 2.1 %collective-permute-start.40 = (bf16[64,2048]{1,0:T(8,128)(2,1)S(1)}, bf16[64,2048]{1,0:T(8,128)(2,1)S(1)}, u32[]{:S(2)}, u32[]{:S(2)}) collective-permute-start(bf16[64,2048]{1,0:T(8,128)(2,1)S(1)} %convolution_convert_fusion.12), channel_id=1, source_target_pairs={{0,8},{1,9},{2,10},{3,11},{4,12},{5,13},{6,14},{7,15},{8,0},{9,1},... | collective-permute-start | bytes 786440 | tf_op jit(solution)/shard_map/ppermute | solution.py:41
  169.6 1.4 convolution_convert_fusion.10
  171.2 1.2 collective-permute-start.42
  172.4 1.6 collective-permute-done.19
  174.0 1.5 fusion.117
  175.5 4.8 %collective-permute-start.20 = (bf16[16,2048]{1,0:T(8,128)(2,1)S(1)}, bf16[16,2048]{1,0:T(8,128)(2,1)S(1)}, u32[]{:S(2)}, u32[]{:S(2)}) collective-permute-start(bf16[16,2048]{1,0:T(8,128)(2,1)S(1)} %get-tuple-element.35), channel_id=1, source_target_pairs={{0,2},{1,3},{2,0},{3,1},{4,6},{5,7},{6,4},{7,5},{8,10},{9,11},{10,... | collective-permute-start | bytes 196616 | tf_op jit(solution)/shard_map/ppermute | solution.py:48
  180.3 3.2 %collective-permute-start.22 = (bf16[16,2048]{1,0:T(8,128)(2,1)S(1)}, bf16[16,2048]{1,0:T(8,128)(2,1)S(1)}, u32[]{:S(2)}, u32[]{:S(2)}) collective-permute-start(bf16[16,2048]{1,0:T(8,128)(2,1)S(1)} %get-tuple-element.36), channel_id=1, source_target_pairs={{0,3},{1,0},{2,1},{3,2},{4,7},{5,4},{6,5},{7,6},{8,11},{9,8},{10,9... | collective-permute-start | bytes 196616 | tf_op jit(solution)/shard_map/ppermute | solution.py:48
  183.5 1.5 fusion.119
  186.1 2.4 %collective-permute-start.45 = (bf16[16,2048]{1,0:T(8,128)(2,1)S(1)}, bf16[16,2048]{1,0:T(8,128)(2,1)S(1)}, u32[]{:S(2)}, u32[]{:S(2)}) collective-permute-start(bf16[16,2048]{1,0:T(8,128)(2,1)S(1)} %get-tuple-element.39), channel_id=1, source_target_pairs={{0,3},{1,0},{2,1},{3,2},{4,7},{5,4},{6,5},{7,6},{8,11},{9,8},{10,9... | collective-permute-start | bytes 196616 | tf_op jit(solution)/shard_map/ppermute | solution.py:48
  188.5 2.5 %collective-permute-done.43 = bf16[16,2048]{1,0:T(8,128)(2,1)S(1)} collective-permute-done((bf16[16,2048]{1,0:T(8,128)(2,1)S(1)}, bf16[16,2048]{1,0:T(8,128)(2,1)S(1)}, u32[]{:S(2)}, u32[]{:S(2)}) %collective-permute-start.43) | collective-permute-done | bytes 65568 | tf_op jit(solution)/shard_map/ppermute | solution.py:48
  (165 shorter events, 30.4 us)
Async XLA Ops:
  0.0 46.2 %copy-start = (bf16[512,2048]{1,0:T(8,128)(2,1)S(1)}, bf16[512,2048]{1,0:T(8,128)(2,1)}, u32[]{:S(2)}) copy-start(bf16[512,2048]{1,0:T(8,128)(2,1)} %param.21) | copy-start | bytes 6291460
  4.4 13.1 %all-to-all-start = ((bf16[16,4,576]{2,1,0:T(4,128)(2,1)}), bf16[16,4,576]{2,1,0:T(4,128)(2,1)S(1)}, u32[]{:S(2)}, u32[]{:S(2)}) async-start(bf16[16,4,576]{2,1,0:T(4,128)(2,1)} %all_to_all.9), calls=%async_computation | async-start | bytes 163840 | tf_op jit(solution)/shard_map/all_to_all | solution.py:222
  20.4 11.5 %copy-start.4 = (s32[512]{0:T(512)S(1)}, s32[512]{0:T(512)}, u32[]{:S(2)}) copy-start(s32[512]{0:T(512)} %param.20) | copy-start | bytes 6148
  23.4 20.5 %all-to-all-start.1 = ((bf16[128,4,512]{2,1,0:T(4,128)(2,1)}), bf16[128,4,512]{2,1,0:T(4,128)(2,1)S(1)}, u32[]{:S(2)}, u32[]{:S(2)}) async-start(bf16[128,4,512]{2,1,0:T(4,128)(2,1)} %bitcast.90), calls=%async_computation.1 | async-start | bytes 1048576 | tf_op jit(solution)/shard_map/all_to_all | solution.py:242
  46.7 1.0 copy-start.3
  49.1 8.9 %collective-permute-start = (bf16[64,2048]{1,0:T(8,128)(2,1)S(1)}, bf16[64,2048]{1,0:T(8,128)(2,1)S(1)}, u32[]{:S(2)}, u32[]{:S(2)}) collective-permute-start(bf16[64,2048]{1,0:T(8,128)(2,1)S(1)} %convolution_convert_fusion.23), channel_id=1, source_target_pairs={{0,8},{1,9},{2,10},{3,11},{4,12},{5,13},{6,14},{7,15},{8,0},{9,1},... | collective-permute-start | bytes 786440 | tf_op jit(solution)/shard_map/ppermute | solution.py:41
  51.9 8.0 %collective-permute-start.1 = (bf16[64,2048]{1,0:T(8,128)(2,1)S(1)}, bf16[64,2048]{1,0:T(8,128)(2,1)S(1)}, u32[]{:S(2)}, u32[]{:S(2)}) collective-permute-start(bf16[64,2048]{1,0:T(8,128)(2,1)S(1)} %convolution_convert_fusion.22), channel_id=1, source_target_pairs={{0,4},{1,5},{2,6},{3,7},{4,8},{5,9},{6,10},{7,11},{8,12},{9,13},{1... | collective-permute-start | bytes 786440 | tf_op jit(solution)/shard_map/ppermute | solution.py:41
  52.8 10.4 %collective-permute-start.2 = (bf16[64,2048]{1,0:T(8,128)(2,1)S(1)}, bf16[64,2048]{1,0:T(8,128)(2,1)S(1)}, u32[]{:S(2)}, u32[]{:S(2)}) collective-permute-start(bf16[64,2048]{1,0:T(8,128)(2,1)S(1)} %convolution_convert_fusion.21), channel_id=1, source_target_pairs={{0,12},{1,13},{2,14},{3,15},{4,0},{5,1},{6,2},{7,3},{8,4},{9,5},{1... | collective-permute-start | bytes 786440 | tf_op jit(solution)/shard_map/ppermute | solution.py:41
  54.0 12.6 %collective-permute-start.23 = (bf16[64,2048]{1,0:T(8,128)(2,1)S(1)}, bf16[64,2048]{1,0:T(8,128)(2,1)S(1)}, u32[]{:S(2)}, u32[]{:S(2)}) collective-permute-start(bf16[64,2048]{1,0:T(8,128)(2,1)S(1)} %convolution_convert_fusion.16), channel_id=1, source_target_pairs={{0,8},{1,9},{2,10},{3,11},{4,12},{5,13},{6,14},{7,15},{8,0},{9,1},... | collective-permute-start | bytes 786440 | tf_op jit(solution)/shard_map/ppermute | solution.py:41
  54.8 13.1 %collective-permute-start.24 = (bf16[64,2048]{1,0:T(8,128)(2,1)S(1)}, bf16[64,2048]{1,0:T(8,128)(2,1)S(1)}, u32[]{:S(2)}, u32[]{:S(2)}) collective-permute-start(bf16[64,2048]{1,0:T(8,128)(2,1)S(1)} %convolution_convert_fusion.15), channel_id=1, source_target_pairs={{0,4},{1,5},{2,6},{3,7},{4,8},{5,9},{6,10},{7,11},{8,12},{9,13},{1... | collective-permute-start | bytes 786440 | tf_op jit(solution)/shard_map/ppermute | solution.py:41
  57.5 35.3 %slice-start.4 = ((s8[7340032]{0:T(1024)(128)(4,1)}), s8[4194304]{0:T(1024)(128)(4,1)S(1)}, s32[]{:S(2)}) async-start(s8[7340032]{0:T(1024)(128)(4,1)} %bitcast.88), calls=%async_computation.6 | async-start | bytes 8388608
  58.0 10.2 %collective-permute-start.25 = (bf16[64,2048]{1,0:T(8,128)(2,1)S(1)}, bf16[64,2048]{1,0:T(8,128)(2,1)S(1)}, u32[]{:S(2)}, u32[]{:S(2)}) collective-permute-start(bf16[64,2048]{1,0:T(8,128)(2,1)S(1)} %convolution_convert_fusion.14), channel_id=1, source_target_pairs={{0,12},{1,13},{2,14},{3,15},{4,0},{5,1},{6,2},{7,3},{8,4},{9,5},{1... | collective-permute-start | bytes 786440 | tf_op jit(solution)/shard_map/ppermute | solution.py:41
  63.7 10.9 %copy-start.2 = (f32[2048]{0:T(1024)S(1)}, f32[2048]{0:T(1024)}, u32[]{:S(2)}) copy-start(f32[2048]{0:T(1024)} %param.22) | copy-start | bytes 24580
  63.8 29.1 %slice-start.5 = ((s8[7340032]{0:T(1024)(128)(4,1)}), s8[3145728]{0:T(1024)(128)(4,1)S(1)}, s32[]{:S(2)}) async-start(s8[7340032]{0:T(1024)(128)(4,1)} %bitcast.88), calls=%async_computation.7 | async-start | bytes 6291456
  63.8 7.5 %collective-permute-start.3 = (bf16[64,2048]{1,0:T(8,128)(2,1)S(1)}, bf16[64,2048]{1,0:T(8,128)(2,1)S(1)}, u32[]{:S(2)}, u32[]{:S(2)}) collective-permute-start(bf16[64,2048]{1,0:T(8,128)(2,1)S(1)} %get-tuple-element.47), channel_id=1, source_target_pairs={{0,3},{1,0},{2,1},{3,2},{4,7},{5,4},{6,5},{7,6},{8,11},{9,8},{10,9... | collective-permute-start | bytes 786440 | tf_op jit(solution)/shard_map/ppermute | solution.py:48
  63.9 8.2 %collective-permute-start.4 = (bf16[64,2048]{1,0:T(8,128)(2,1)S(1)}, bf16[64,2048]{1,0:T(8,128)(2,1)S(1)}, u32[]{:S(2)}, u32[]{:S(2)}) collective-permute-start(bf16[64,2048]{1,0:T(8,128)(2,1)S(1)} %get-tuple-element.47), channel_id=1, source_target_pairs={{0,2},{1,3},{2,0},{3,1},{4,6},{5,7},{6,4},{7,5},{8,10},{9,11},{10,... | collective-permute-start | bytes 786440 | tf_op jit(solution)/shard_map/ppermute | solution.py:48
  66.5 8.1 %collective-permute-start.5 = (bf16[64,2048]{1,0:T(8,128)(2,1)S(1)}, bf16[64,2048]{1,0:T(8,128)(2,1)S(1)}, u32[]{:S(2)}, u32[]{:S(2)}) collective-permute-start(bf16[64,2048]{1,0:T(8,128)(2,1)S(1)} %get-tuple-element.47), channel_id=1, source_target_pairs={{0,1},{1,2},{2,3},{3,0},{4,5},{5,6},{6,7},{7,4},{8,9},{9,10},{10,1... | collective-permute-start | bytes 786440 | tf_op jit(solution)/shard_map/ppermute | solution.py:48
  68.7 8.5 %collective-permute-start.26 = (bf16[64,2048]{1,0:T(8,128)(2,1)S(1)}, bf16[64,2048]{1,0:T(8,128)(2,1)S(1)}, u32[]{:S(2)}, u32[]{:S(2)}) collective-permute-start(bf16[64,2048]{1,0:T(8,128)(2,1)S(1)} %get-tuple-element.51), channel_id=1, source_target_pairs={{0,3},{1,0},{2,1},{3,2},{4,7},{5,4},{6,5},{7,6},{8,11},{9,8},{10,9... | collective-permute-start | bytes 786440 | tf_op jit(solution)/shard_map/ppermute | solution.py:48
  70.7 10.0 %collective-permute-start.27 = (bf16[64,2048]{1,0:T(8,128)(2,1)S(1)}, bf16[64,2048]{1,0:T(8,128)(2,1)S(1)}, u32[]{:S(2)}, u32[]{:S(2)}) collective-permute-start(bf16[64,2048]{1,0:T(8,128)(2,1)S(1)} %get-tuple-element.51), channel_id=1, source_target_pairs={{0,2},{1,3},{2,0},{3,1},{4,6},{5,7},{6,4},{7,5},{8,10},{9,11},{10,... | collective-permute-start | bytes 786440 | tf_op jit(solution)/shard_map/ppermute | solution.py:48
  71.3 14.9 %collective-permute-start.28 = (bf16[64,2048]{1,0:T(8,128)(2,1)S(1)}, bf16[64,2048]{1,0:T(8,128)(2,1)S(1)}, u32[]{:S(2)}, u32[]{:S(2)}) collective-permute-start(bf16[64,2048]{1,0:T(8,128)(2,1)S(1)} %get-tuple-element.51), channel_id=1, source_target_pairs={{0,1},{1,2},{2,3},{3,0},{4,5},{5,6},{6,7},{7,4},{8,9},{9,10},{10,1... | collective-permute-start | bytes 786440 | tf_op jit(solution)/shard_map/ppermute | solution.py:48
  74.9 15.9 %collective-permute-start.6 = (bf16[64,2176]{1,0:T(8,128)(2,1)S(1)}, bf16[64,2176]{1,0:T(8,128)(2,1)S(1)}, u32[]{:S(2)}, u32[]{:S(2)}) collective-permute-start(bf16[64,2176]{1,0:T(8,128)(2,1)S(1)} %get-tuple-element.18), channel_id=1, source_target_pairs={{0,12},{1,13},{2,14},{3,15},{4,0},{5,1},{6,2},{7,3},{8,4},{9,5},{1... | collective-permute-start | bytes 835592 | tf_op jit(solution)/shard_map/ppermute | solution.py:41
  75.0 17.3 %collective-permute-start.7 = (bf16[64,2176]{1,0:T(8,128)(2,1)S(1)}, bf16[64,2176]{1,0:T(8,128)(2,1)S(1)}, u32[]{:S(2)}, u32[]{:S(2)}) collective-permute-start(bf16[64,2176]{1,0:T(8,128)(2,1)S(1)} %get-tuple-element.18), channel_id=1, source_target_pairs={{0,8},{1,9},{2,10},{3,11},{4,12},{5,13},{6,14},{7,15},{8,0},{9,1},... | collective-permute-start | bytes 835592 | tf_op jit(solution)/shard_map/ppermute | solution.py:41
  77.2 15.2 %collective-permute-start.8 = (bf16[64,2176]{1,0:T(8,128)(2,1)S(1)}, bf16[64,2176]{1,0:T(8,128)(2,1)S(1)}, u32[]{:S(2)}, u32[]{:S(2)}) collective-permute-start(bf16[64,2176]{1,0:T(8,128)(2,1)S(1)} %get-tuple-element.18), channel_id=1, source_target_pairs={{0,4},{1,5},{2,6},{3,7},{4,8},{5,9},{6,10},{7,11},{8,12},{9,13},{1... | collective-permute-start | bytes 835592 | tf_op jit(solution)/shard_map/ppermute | solution.py:41
  86.5 13.0 %collective-permute-start.29 = (bf16[64,2176]{1,0:T(8,128)(2,1)S(1)}, bf16[64,2176]{1,0:T(8,128)(2,1)S(1)}, u32[]{:S(2)}, u32[]{:S(2)}) collective-permute-start(bf16[64,2176]{1,0:T(8,128)(2,1)S(1)} %get-tuple-element.24), channel_id=1, source_target_pairs={{0,12},{1,13},{2,14},{3,15},{4,0},{5,1},{6,2},{7,3},{8,4},{9,5},{1... | collective-permute-start | bytes 835592 | tf_op jit(solution)/shard_map/ppermute | solution.py:41
  88.3 11.3 %collective-permute-start.30 = (bf16[64,2176]{1,0:T(8,128)(2,1)S(1)}, bf16[64,2176]{1,0:T(8,128)(2,1)S(1)}, u32[]{:S(2)}, u32[]{:S(2)}) collective-permute-start(bf16[64,2176]{1,0:T(8,128)(2,1)S(1)} %get-tuple-element.24), channel_id=1, source_target_pairs={{0,8},{1,9},{2,10},{3,11},{4,12},{5,13},{6,14},{7,15},{8,0},{9,1},... | collective-permute-start | bytes 835592 | tf_op jit(solution)/shard_map/ppermute | solution.py:41
  90.8 9.0 %collective-permute-start.31 = (bf16[64,2176]{1,0:T(8,128)(2,1)S(1)}, bf16[64,2176]{1,0:T(8,128)(2,1)S(1)}, u32[]{:S(2)}, u32[]{:S(2)}) collective-permute-start(bf16[64,2176]{1,0:T(8,128)(2,1)S(1)} %get-tuple-element.24), channel_id=1, source_target_pairs={{0,4},{1,5},{2,6},{3,7},{4,8},{5,9},{6,10},{7,11},{8,12},{9,13},{1... | collective-permute-start | bytes 835592 | tf_op jit(solution)/shard_map/ppermute | solution.py:41
  92.4 2.2 %slice-start.2 = ((s8[7340032]{0:T(1024)(128)(4,1)}), s8[4194304]{0:T(1024)(128)(4,1)S(1)}, s32[]{:S(2)}) async-start(s8[7340032]{0:T(1024)(128)(4,1)} %bitcast.86), calls=%async_computation.4 | async-start | bytes 8388608
  92.8 2.9 %slice-start.3 = ((s8[7340032]{0:T(1024)(128)(4,1)}), s8[3145728]{0:T(1024)(128)(4,1)S(1)}, s32[]{:S(2)}) async-start(s8[7340032]{0:T(1024)(128)(4,1)} %bitcast.86), calls=%async_computation.5 | async-start | bytes 6291456
  102.8 2.6 %collective-permute-start.9 = (bf16[128,3712]{1,0:T(8,128)(2,1)S(1)}, bf16[128,3712]{1,0:T(8,128)(2,1)S(1)}, u32[]{:S(2)}, u32[]{:S(2)}) collective-permute-start(bf16[128,3712]{1,0:T(8,128)(2,1)S(1)} %shard_map.128), channel_id=1, source_target_pairs={{0,16},{1,17},{2,18},{3,19},{4,20},{5,21},{6,22},{7,23},{8,24},{9,... | collective-permute-start | bytes 2850824 | tf_op jit(solution)/shard_map/ppermute | solution.py:56
  102.9 22.5 %collective-permute-start.32 = (bf16[128,3712]{1,0:T(8,128)(2,1)S(1)}, bf16[128,3712]{1,0:T(8,128)(2,1)S(1)}, u32[]{:S(2)}, u32[]{:S(2)}) collective-permute-start(bf16[128,3712]{1,0:T(8,128)(2,1)S(1)} %shard_map.132), channel_id=1, source_target_pairs={{0,16},{1,17},{2,18},{3,19},{4,20},{5,21},{6,22},{7,23},{8,24},{9,... | collective-permute-start | bytes 2850824 | tf_op jit(solution)/shard_map/ppermute | solution.py:56
  105.4 50.1 %slice-start = ((s8[7340032]{0:T(1024)(128)(4,1)}), s8[4194304]{0:T(1024)(128)(4,1)S(1)}, s32[]{:S(2)}) async-start(s8[7340032]{0:T(1024)(128)(4,1)} %bitcast.84), calls=%async_computation.2 | async-start | bytes 8388608
  105.7 49.8 %slice-start.1 = ((s8[7340032]{0:T(1024)(128)(4,1)}), s8[3145728]{0:T(1024)(128)(4,1)S(1)}, s32[]{:S(2)}) async-start(s8[7340032]{0:T(1024)(128)(4,1)} %bitcast.84), calls=%async_computation.3 | async-start | bytes 6291456
  105.7 23.9 %collective-permute-start.10 = (bf16[32,3712]{1,0:T(8,128)(2,1)S(1)}, bf16[32,3712]{1,0:T(8,128)(2,1)S(1)}, u32[]{:S(2)}, u32[]{:S(2)}) collective-permute-start(bf16[32,3712]{1,0:T(8,128)(2,1)S(1)} %get-tuple-element.20), channel_id=1, source_target_pairs={{0,64},{1,65},{2,66},{3,67},{4,68},{5,69},{6,70},{7,71},{8,72},{9,... | collective-permute-start | bytes 712712 | tf_op jit(solution)/shard_map/ppermute | solution.py:52
  121.9 12.9 %collective-permute-start.11 = (bf16[32,3712]{1,0:T(8,128)(2,1)S(1)}, bf16[32,3712]{1,0:T(8,128)(2,1)S(1)}, u32[]{:S(2)}, u32[]{:S(2)}) collective-permute-start(bf16[32,3712]{1,0:T(8,128)(2,1)S(1)} %get-tuple-element.21), channel_id=1, source_target_pairs={{0,32},{1,33},{2,34},{3,35},{4,36},{5,37},{6,38},{7,39},{8,40},{9,... | collective-permute-start | bytes 712712 | tf_op jit(solution)/shard_map/ppermute | solution.py:52
  122.6 13.4 %collective-permute-start.12 = (bf16[32,3712]{1,0:T(8,128)(2,1)S(1)}, bf16[32,3712]{1,0:T(8,128)(2,1)S(1)}, u32[]{:S(2)}, u32[]{:S(2)}) collective-permute-start(bf16[32,3712]{1,0:T(8,128)(2,1)S(1)} %get-tuple-element.22), channel_id=1, source_target_pairs={{0,96},{1,97},{2,98},{3,99},{4,100},{5,101},{6,102},{7,103},{8,104... | collective-permute-start | bytes 712712 | tf_op jit(solution)/shard_map/ppermute | solution.py:52
  125.8 14.8 %collective-permute-start.33 = (bf16[32,3712]{1,0:T(8,128)(2,1)S(1)}, bf16[32,3712]{1,0:T(8,128)(2,1)S(1)}, u32[]{:S(2)}, u32[]{:S(2)}) collective-permute-start(bf16[32,3712]{1,0:T(8,128)(2,1)S(1)} %get-tuple-element.26), channel_id=1, source_target_pairs={{0,64},{1,65},{2,66},{3,67},{4,68},{5,69},{6,70},{7,71},{8,72},{9,... | collective-permute-start | bytes 712712 | tf_op jit(solution)/shard_map/ppermute | solution.py:52
  126.9 18.1 %collective-permute-start.34 = (bf16[32,3712]{1,0:T(8,128)(2,1)S(1)}, bf16[32,3712]{1,0:T(8,128)(2,1)S(1)}, u32[]{:S(2)}, u32[]{:S(2)}) collective-permute-start(bf16[32,3712]{1,0:T(8,128)(2,1)S(1)} %get-tuple-element.27), channel_id=1, source_target_pairs={{0,32},{1,33},{2,34},{3,35},{4,36},{5,37},{6,38},{7,39},{8,40},{9,... | collective-permute-start | bytes 712712 | tf_op jit(solution)/shard_map/ppermute | solution.py:52
  129.6 15.3 %collective-permute-start.35 = (bf16[32,3712]{1,0:T(8,128)(2,1)S(1)}, bf16[32,3712]{1,0:T(8,128)(2,1)S(1)}, u32[]{:S(2)}, u32[]{:S(2)}) collective-permute-start(bf16[32,3712]{1,0:T(8,128)(2,1)S(1)} %get-tuple-element.28), channel_id=1, source_target_pairs={{0,96},{1,97},{2,98},{3,99},{4,100},{5,101},{6,102},{7,103},{8,104... | collective-permute-start | bytes 712712 | tf_op jit(solution)/shard_map/ppermute | solution.py:52
  136.3 11.5 %collective-permute-start.13 = (bf16[32,1792]{1,0:T(8,128)(2,1)S(1)}, bf16[32,1792]{1,0:T(8,128)(2,1)S(1)}, u32[]{:S(2)}, u32[]{:S(2)}) collective-permute-start(bf16[32,1792]{1,0:T(8,128)(2,1)S(1)} %shard_map.130), channel_id=1, source_target_pairs={{0,96},{1,97},{2,98},{3,99},{4,100},{5,101},{6,102},{7,103},{8,104... | collective-permute-start | bytes 344072 | tf_op jit(solution)/shard_map/ppermute | solution.py:52
  140.6 8.1 %collective-permute-start.14 = (bf16[32,1792]{1,0:T(8,128)(2,1)S(1)}, bf16[32,1792]{1,0:T(8,128)(2,1)S(1)}, u32[]{:S(2)}, u32[]{:S(2)}) collective-permute-start(bf16[32,1792]{1,0:T(8,128)(2,1)S(1)} %shard_map.130), channel_id=1, source_target_pairs={{0,64},{1,65},{2,66},{3,67},{4,68},{5,69},{6,70},{7,71},{8,72},{9,... | collective-permute-start | bytes 344072 | tf_op jit(solution)/shard_map/ppermute | solution.py:52
  140.6 8.3 %collective-permute-start.15 = (bf16[32,1792]{1,0:T(8,128)(2,1)S(1)}, bf16[32,1792]{1,0:T(8,128)(2,1)S(1)}, u32[]{:S(2)}, u32[]{:S(2)}) collective-permute-start(bf16[32,1792]{1,0:T(8,128)(2,1)S(1)} %shard_map.130), channel_id=1, source_target_pairs={{0,32},{1,33},{2,34},{3,35},{4,36},{5,37},{6,38},{7,39},{8,40},{9,... | collective-permute-start | bytes 344072 | tf_op jit(solution)/shard_map/ppermute | solution.py:52
  145.3 6.1 %collective-permute-start.36 = (bf16[32,1792]{1,0:T(8,128)(2,1)S(1)}, bf16[32,1792]{1,0:T(8,128)(2,1)S(1)}, u32[]{:S(2)}, u32[]{:S(2)}) collective-permute-start(bf16[32,1792]{1,0:T(8,128)(2,1)S(1)} %shard_map.134), channel_id=1, source_target_pairs={{0,96},{1,97},{2,98},{3,99},{4,100},{5,101},{6,102},{7,103},{8,104... | collective-permute-start | bytes 344072 | tf_op jit(solution)/shard_map/ppermute | solution.py:52
  146.0 7.3 %collective-permute-start.37 = (bf16[32,1792]{1,0:T(8,128)(2,1)S(1)}, bf16[32,1792]{1,0:T(8,128)(2,1)S(1)}, u32[]{:S(2)}, u32[]{:S(2)}) collective-permute-start(bf16[32,1792]{1,0:T(8,128)(2,1)S(1)} %shard_map.134), channel_id=1, source_target_pairs={{0,64},{1,65},{2,66},{3,67},{4,68},{5,69},{6,70},{7,71},{8,72},{9,... | collective-permute-start | bytes 344072 | tf_op jit(solution)/shard_map/ppermute | solution.py:52
  147.8 6.9 %collective-permute-start.38 = (bf16[32,1792]{1,0:T(8,128)(2,1)S(1)}, bf16[32,1792]{1,0:T(8,128)(2,1)S(1)}, u32[]{:S(2)}, u32[]{:S(2)}) collective-permute-start(bf16[32,1792]{1,0:T(8,128)(2,1)S(1)} %shard_map.134), channel_id=1, source_target_pairs={{0,32},{1,33},{2,34},{3,35},{4,36},{5,37},{6,38},{7,39},{8,40},{9,... | collective-permute-start | bytes 344072 | tf_op jit(solution)/shard_map/ppermute | solution.py:52
  149.0 6.0 %collective-permute-start.16 = (bf16[128,1792]{1,0:T(8,128)(2,1)S(1)}, bf16[128,1792]{1,0:T(8,128)(2,1)S(1)}, u32[]{:S(2)}, u32[]{:S(2)}) collective-permute-start(bf16[128,1792]{1,0:T(8,128)(2,1)S(1)} %pad_maximum_fusion), channel_id=1, source_target_pairs={{0,16},{1,17},{2,18},{3,19},{4,20},{5,21},{6,22},{7,23},{8,24},{9,... | collective-permute-start | bytes 1376264 | tf_op jit(solution)/shard_map/ppermute | solution.py:56
  154.8 5.1 %collective-permute-start.39 = (bf16[128,1792]{1,0:T(8,128)(2,1)S(1)}, bf16[128,1792]{1,0:T(8,128)(2,1)S(1)}, u32[]{:S(2)}, u32[]{:S(2)}) collective-permute-start(bf16[128,1792]{1,0:T(8,128)(2,1)S(1)} %pad_maximum_fusion.1), channel_id=1, source_target_pairs={{0,16},{1,17},{2,18},{3,19},{4,20},{5,21},{6,22},{7,23},{8,24},{9,... | collective-permute-start | bytes 1376264 | tf_op jit(solution)/shard_map/ppermute | solution.py:56
  163.2 8.0 %collective-permute-start.17 = (bf16[64,2048]{1,0:T(8,128)(2,1)S(1)}, bf16[64,2048]{1,0:T(8,128)(2,1)S(1)}, u32[]{:S(2)}, u32[]{:S(2)}) collective-permute-start(bf16[64,2048]{1,0:T(8,128)(2,1)S(1)} %convolution_convert_fusion.19), channel_id=1, source_target_pairs={{0,8},{1,9},{2,10},{3,11},{4,12},{5,13},{6,14},{7,15},{8,0},{9,1},... | collective-permute-start | bytes 786440 | tf_op jit(solution)/shard_map/ppermute | solution.py:41
  164.7 7.7 %collective-permute-start.18 = (bf16[64,2048]{1,0:T(8,128)(2,1)S(1)}, bf16[64,2048]{1,0:T(8,128)(2,1)S(1)}, u32[]{:S(2)}, u32[]{:S(2)}) collective-permute-start(bf16[64,2048]{1,0:T(8,128)(2,1)S(1)} %convolution_convert_fusion.18), channel_id=1, source_target_pairs={{0,4},{1,5},{2,6},{3,7},{4,8},{5,9},{6,10},{7,11},{8,12},{9,13},{1... | collective-permute-start | bytes 786440 | tf_op jit(solution)/shard_map/ppermute | solution.py:41
  166.4 7.6 %collective-permute-start.19 = (bf16[64,2048]{1,0:T(8,128)(2,1)S(1)}, bf16[64,2048]{1,0:T(8,128)(2,1)S(1)}, u32[]{:S(2)}, u32[]{:S(2)}) collective-permute-start(bf16[64,2048]{1,0:T(8,128)(2,1)S(1)} %convolution_convert_fusion.17), channel_id=1, source_target_pairs={{0,12},{1,13},{2,14},{3,15},{4,0},{5,1},{6,2},{7,3},{8,4},{9,5},{1... | collective-permute-start | bytes 786440 | tf_op jit(solution)/shard_map/ppermute | solution.py:41
  166.8 13.5 %collective-permute-start.40 = (bf16[64,2048]{1,0:T(8,128)(2,1)S(1)}, bf16[64,2048]{1,0:T(8,128)(2,1)S(1)}, u32[]{:S(2)}, u32[]{:S(2)}) collective-permute-start(bf16[64,2048]{1,0:T(8,128)(2,1)S(1)} %convolution_convert_fusion.12), channel_id=1, source_target_pairs={{0,8},{1,9},{2,10},{3,11},{4,12},{5,13},{6,14},{7,15},{8,0},{9,1},... | collective-permute-start | bytes 786440 | tf_op jit(solution)/shard_map/ppermute | solution.py:41
  168.9 14.7 %collective-permute-start.41 = (bf16[64,2048]{1,0:T(8,128)(2,1)S(1)}, bf16[64,2048]{1,0:T(8,128)(2,1)S(1)}, u32[]{:S(2)}, u32[]{:S(2)}) collective-permute-start(bf16[64,2048]{1,0:T(8,128)(2,1)S(1)} %convolution_convert_fusion.11), channel_id=1, source_target_pairs={{0,4},{1,5},{2,6},{3,7},{4,8},{5,9},{6,10},{7,11},{8,12},{9,13},{1... | collective-permute-start | bytes 786440 | tf_op jit(solution)/shard_map/ppermute | solution.py:41
  171.2 12.3 %collective-permute-start.42 = (bf16[64,2048]{1,0:T(8,128)(2,1)S(1)}, bf16[64,2048]{1,0:T(8,128)(2,1)S(1)}, u32[]{:S(2)}, u32[]{:S(2)}) collective-permute-start(bf16[64,2048]{1,0:T(8,128)(2,1)S(1)} %convolution_convert_fusion.10), channel_id=1, source_target_pairs={{0,12},{1,13},{2,14},{3,15},{4,0},{5,1},{6,2},{7,3},{8,4},{9,5},{1... | collective-permute-start | bytes 786440 | tf_op jit(solution)/shard_map/ppermute | solution.py:41
  175.5 10.6 %collective-permute-start.20 = (bf16[16,2048]{1,0:T(8,128)(2,1)S(1)}, bf16[16,2048]{1,0:T(8,128)(2,1)S(1)}, u32[]{:S(2)}, u32[]{:S(2)}) collective-permute-start(bf16[16,2048]{1,0:T(8,128)(2,1)S(1)} %get-tuple-element.35), channel_id=1, source_target_pairs={{0,2},{1,3},{2,0},{3,1},{4,6},{5,7},{6,4},{7,5},{8,10},{9,11},{10,... | collective-permute-start | bytes 196616 | tf_op jit(solution)/shard_map/ppermute | solution.py:48
  180.3 8.2 %collective-permute-start.21 = (bf16[16,2048]{1,0:T(8,128)(2,1)S(1)}, bf16[16,2048]{1,0:T(8,128)(2,1)S(1)}, u32[]{:S(2)}, u32[]{:S(2)}) collective-permute-start(bf16[16,2048]{1,0:T(8,128)(2,1)S(1)} %get-tuple-element.37), channel_id=1, source_target_pairs={{0,1},{1,2},{2,3},{3,0},{4,5},{5,6},{6,7},{7,4},{8,9},{9,10},{10,1... | collective-permute-start | bytes 196616 | tf_op jit(solution)/shard_map/ppermute | solution.py:48
  180.3 8.2 %collective-permute-start.22 = (bf16[16,2048]{1,0:T(8,128)(2,1)S(1)}, bf16[16,2048]{1,0:T(8,128)(2,1)S(1)}, u32[]{:S(2)}, u32[]{:S(2)}) collective-permute-start(bf16[16,2048]{1,0:T(8,128)(2,1)S(1)} %get-tuple-element.36), channel_id=1, source_target_pairs={{0,3},{1,0},{2,1},{3,2},{4,7},{5,4},{6,5},{7,6},{8,11},{9,8},{10,9... | collective-permute-start | bytes 196616 | tf_op jit(solution)/shard_map/ppermute | solution.py:48
  183.5 8.6 %copy-start.1 = (bf16[512,2048]{1,0:T(8,128)(2,1)S(1)}, bf16[512,2048]{1,0:T(8,128)(2,1)}, u32[]{:S(2)}) copy-start(bf16[512,2048]{1,0:T(8,128)(2,1)} %param.21) | copy-start | bytes 6291460
  185.1 6.0 %collective-permute-start.43 = (bf16[16,2048]{1,0:T(8,128)(2,1)S(1)}, bf16[16,2048]{1,0:T(8,128)(2,1)S(1)}, u32[]{:S(2)}, u32[]{:S(2)}) collective-permute-start(bf16[16,2048]{1,0:T(8,128)(2,1)S(1)} %get-tuple-element.38), channel_id=1, source_target_pairs={{0,2},{1,3},{2,0},{3,1},{4,6},{5,7},{6,4},{7,5},{8,10},{9,11},{10,... | collective-permute-start | bytes 196616 | tf_op jit(solution)/shard_map/ppermute | solution.py:48
  185.2 6.2 %collective-permute-start.44 = (bf16[16,2048]{1,0:T(8,128)(2,1)S(1)}, bf16[16,2048]{1,0:T(8,128)(2,1)S(1)}, u32[]{:S(2)}, u32[]{:S(2)}) collective-permute-start(bf16[16,2048]{1,0:T(8,128)(2,1)S(1)} %get-tuple-element.40), channel_id=1, source_target_pairs={{0,1},{1,2},{2,3},{3,0},{4,5},{5,6},{6,7},{7,4},{8,9},{9,10},{10,1... | collective-permute-start | bytes 196616 | tf_op jit(solution)/shard_map/ppermute | solution.py:48
  186.1 5.3 %collective-permute-start.45 = (bf16[16,2048]{1,0:T(8,128)(2,1)S(1)}, bf16[16,2048]{1,0:T(8,128)(2,1)S(1)}, u32[]{:S(2)}, u32[]{:S(2)}) collective-permute-start(bf16[16,2048]{1,0:T(8,128)(2,1)S(1)} %get-tuple-element.39), channel_id=1, source_target_pairs={{0,3},{1,0},{2,1},{3,2},{4,7},{5,4},{6,5},{7,6},{8,11},{9,8},{10,9... | collective-permute-start | bytes 196616 | tf_op jit(solution)/shard_map/ppermute | solution.py:48

commit v3 on v2

--- a/solution.py
+++ b/solution.py
@@ -123,21 +123,23 @@
 
 def gift_kernel(gate, upper, ends, gift):
     width = gate.shape[1]
-    gift[:, :width] = gate[...]
-    gift[:, width : 2 * width] = upper[...]
-    gift[:, 2 * width :] = ends[...]
+    here = pl.ds(0, gift.shape[0])
+    gift[:, :width] = gate[here, :]
+    gift[:, width : 2 * width] = upper[here, :]
+    gift[:, 2 * width :] = ends[here, :]
 
 
 def pair_kernel(gate, upper, ends, other, *payloads):
-    half = gate.shape[0] // RING
+    half = other.shape[0] // RING
     width = gate.shape[1]
     for i, payload in enumerate(payloads):
-        here = pl.ds(i * half, half)
-        payload[:, :width] = (gate[here, :] + other[here, :width].astype(F32)).astype(BF16)
-        payload[:, width : 2 * width] = (
-            upper[here, :] + other[here, width : 2 * width].astype(F32)
-        ).astype(BF16)
-        both = ends[here, :].astype(F32) + other[here, 2 * width :].astype(F32)
+        here, there = pl.ds((RING + i) * half, half), pl.ds(i * half, half)
+        for k, ref in enumerate((gate, upper)):
+            span = pl.ds(k * width, width)
+            payload[:, span] = (
+                ref[here, :].astype(F32) + other[there, span].astype(F32)
+            ).astype(BF16)
+        both = ends[here, :].astype(F32) + other[there, 2 * width :].astype(F32)
         payload[:, 2 * width :] = ends_of(both[:, :1] + both[:, HD // 2 : HD // 2 + 1])
 
 
@@ -255,23 +257,28 @@
     far, near, inner = positions // chunk, (positions // piece) % RING, positions % piece
 
     def sum_first(values, weight):
-        parts = {}
-        for j in FAR_FIRST:
-            part = jnp.dot(values[j * chunk : (j + 1) * chunk], weight, preferred_element_type=F32)
-            parts[j] = part if j == 0 else part.astype(BF16)
+        total = pick(values, weight)
+        parts = {j: total[j * chunk : (j + 1) * chunk] for j in range(RING)}
         return add_up(parts[0], spread(send_first, parts))
 
-    def project(number):
+    def rows_here(number):
         row_x = jnp.where(core == 0, x + far, x + near) % RING
         row_y = jnp.where(core == 0, y + near, y + far) % RING
-        row_here = (row_x * RING + row_y) * block + number * piece + inner
-        slot_of = jnp.sum(
-            jnp.where(row_here[:, None] == jnp.arange(rows)[None, :], cache_slot[None, :], 0), axis=1
-        )
-        context_rows = pick(one_hot_rows(slot_of, rows), all_columns)
+        return (row_x * RING + row_y) * block + number * piece + inner
+
+    every_row = jnp.concatenate([rows_here(number) for number in range(TURNS)])
+    slot_of = jnp.sum(
+        jnp.where(every_row[:, None] == jnp.arange(rows)[None, :], cache_slot[None, :], 0), axis=1
+    )
+    every_context = pick(one_hot_rows(slot_of, rows), all_columns)
+    first_rows = jnp.concatenate([rows_here(number)[:chunk] for number in range(TURNS)])
+    every_resid = pick(one_hot_rows(first_rows, rows), resid)
+
+    def project(number):
+        context_rows = every_context[number * RING * chunk : (number + 1) * RING * chunk]
+        resid_rows = every_resid[number * chunk : (number + 1) * chunk]
         part = sum_first(context_rows, out_weight)
         others = collect(send_second, part.astype(BF16))[1:]
-        resid_rows = pick(one_hot_rows(row_here[:chunk], rows), resid)
         payload, middle = local_kernel(
             middle_kernel,
             [
@@ -296,25 +303,27 @@
         def half_rows(part_core):
             part_y = part_core * (RING // CORES) + inner_half // piece
             source = jnp.where(core == 0, part_x * RING + part_y, part_y * RING + part_x)
-            matrix = one_hot_rows(source * piece + inner_half % piece, rows // TURNS)
-            return pick(matrix, blocks[:, :width]), pick(matrix, blocks[:, width:])
-
-        other_rows, other_ends = half_rows(1 - core)
-        own_rows, own_ends = half_rows(core)
+            return source * piece + inner_half % piece
+
+        source = jnp.concatenate([half_rows(1 - core), half_rows(core)])
+        sorted_rows = pick(one_hot_rows(source, rows // TURNS), blocks)
+        gate = pick(sorted_rows[:, :width], gate_weight)
+        upper = pick(sorted_rows[:, :width], up_weight)
+        ends = sorted_rows[:, width:]
         sums_width = 2 * hidden_width + HD
         (gift,) = local_kernel(
             gift_kernel,
             [jax.ShapeDtypeStruct((RING * half, sums_width), BF16)],
-            pick(other_rows, gate_weight),
-            pick(other_rows, up_weight),
-            other_ends,
+            gate,
+            upper,
+            ends,
         )
         payloads = local_kernel(
             pair_kernel,
             [jax.ShapeDtypeStruct((half, sums_width), BF16)] * RING,
-            jnp.dot(own_rows, gate_weight, preferred_element_type=F32),
-            jnp.dot(own_rows, up_weight, preferred_element_type=F32),
-            own_ends,
+            gate,
+            upper,
+            ends,
             send_core(gift),
         )
         return dict(zip(FAR_FIRST, payloads))

time: 195 us -> 181 us (0.928)
  starting transfers between devices: 92.2 us -> 74.3 us
  waiting for transfers between devices: 47.7 us -> 52.7 us
  matrix products: 41.3 us -> 36.5 us
  other arithmetic: 2.55 us -> 5.84 us
    dot_general x20 -> x0, matrix products: 20.1 us -> none  [the longest x16 15.6 us: sum_first(): jnp.dot(values[j * chunk:(j + 1) * chunk], weight, preferred_element_type...]
    dot_general x21 -> x15, matrix products: 17 us -> 32.4 us  [pick(): return jnp.dot(matrix, values, preferred_element_type=F32).astype(BF16)]
    ppermute x12, starting transfers between devices: 30.3 us -> 15.5 us  [send_z(): lax.ppermute(value, AXES, pairs(lambda x, y, z, core: (x, y, z + step, co...]
    ppermute x12, waiting for transfers between devices: 16.2 us -> 18.5 us  [send_z(): lax.ppermute(value, AXES, pairs(lambda x, y, z, core: (x, y, z + step, co...]
    all_to_all x1, waiting for transfers between devices: 2.39 us -> 4.56 us  [on_device(): lax.all_to_all(outgoing, 'yz', split_axis=0, concat_axis=0, tiled=True)]
  transfers between devices with their start and end apart: 48 -> 48, of which waited for: 21 -> 21; matrix products, arithmetic and copies ran while one was open for 13% -> 18% of each run, Pallas kernels for 1% -> 1%
where the time goes in v3:
time: 181 us; the launch traced here: 179 us
  starting transfers between devices  74.3 us (41%)
  waiting for transfers between devices  52.7 us (29%)
  matrix products  36.5 us (20%)
  local copies, waits for them, and re-layouts  6.3 us (3%)
  other arithmetic  5.84 us (3%)
  Pallas kernels  2.11 us (1%)
    dot_general x15, matrix products, pick(): return jnp.dot(matrix, values, preferred_element_type=F32).astype(BF16)  32.4 us
    ppermute x18, starting transfers between devices, send_first(): return lax.ppermute(value, AXES, pairs(move))  26.2 us
    ppermute x12, waiting for transfers between devices, send_z(): lax.ppermute(value, AXES, pairs(lambda x, y, z, core: (x, y, z + step, co...  18.5 us
    ppermute x12, starting transfers between devices, send_second(): return lax.ppermute(value, AXES, pairs(move))  15.8 us
    ppermute x12, starting transfers between devices, send_z(): lax.ppermute(value, AXES, pairs(lambda x, y, z, core: (x, y, z + step, co...  15.5 us
    ppermute x12, waiting for transfers between devices, send_second(): return lax.ppermute(value, AXES, pairs(move))  11.7 us
    all_to_all x1, waiting for transfers between devices, on_device(): lax.all_to_all(outgoing.reshape(count_gx * count_yz, per_device, head_wid...  9.53 us
    all_to_all x1, starting transfers between devices, on_device(): lax.all_to_all(outgoing.reshape(count_gx * count_yz, per_device, head_wid...  8.57 us
  transfers between devices with their start and end apart: 48, of which 21 were waited for; matrix products, arithmetic and copies ran while one was open for 18% of the time, Pallas kernels for 1%

profile of v3, /device:TPU:6, one launch (start us, length us, event | category | flops | bytes accessed | tf_op | source)
XLA Modules:
  0.0 178.5 jit_solution(12249011836940599761)
XLA Ops:
  0.0 1.4 convolution_convert_fusion.14
  1.5 1.0 convolution_convert_fusion.16
  2.6 1.0 convolution_convert_fusion.15
  4.4 7.4 %all-to-all-start = ((bf16[16,4,576]{2,1,0:T(4,128)(2,1)}), bf16[16,4,576]{2,1,0:T(4,128)(2,1)S(1)}, u32[]{:S(2)}, u32[]{:S(2)}) async-start(bf16[16,4,576]{2,1,0:T(4,128)(2,1)} %all_to_all.9), calls=%async_computation | async-start | bytes 163840 | tf_op jit(solution)/shard_map/all_to_all | solution.py:224
  12.9 4.6 %all-to-all-done = bf16[16,4,576]{2,1,0:T(4,128)(2,1)S(1)} async-done(((bf16[16,4,576]{2,1,0:T(4,128)(2,1)}), bf16[16,4,576]{2,1,0:T(4,128)(2,1)S(1)}, u32[]{:S(2)}, u32[]{:S(2)}) %all-to-all-start) | async-done | bytes 73760 | tf_op jit(solution)/shard_map/all_to_all | solution.py:224
  17.9 2.1 %fusion.104 = (f32[4,4,16]{2,1,0:T(4,128)S(1)}, f32[4,4,16,384]{3,2,1,0:T(8,128)S(1)}) fusion(bf16[4,4,16,128]{3,2,1,0:T(8,128)(2,1)S(1)} %bitcast.59, pred[4,384]{1,0:T(4,128)(4,1)S(1)} %iota_compare_fusion.13, bf16[4,384,512]{2,1,0:T(8,128)(2,1)} %param.17), kind=kOutput, calls=%fused_computation.199 | convolution fusion | flops 25460480 | bytes 2034176 | tf_op jit(solution)/shard_map/bkgd,bckd->bkgc/dot_general | solution.py:168
  20.4 1.9 %fusion.15 = bf16[4,4,16,128]{3,2,1,0:T(8,128)(2,1)S(1)} fusion(f32[4,4,16,384]{3,2,1,0:T(8,128)S(1)} %get-tuple-element.66, f32[4,4,16]{2,1,0:T(4,128)S(1)} %get-tuple-element.64, f32[4,4,16]{2,1,0:T(4,128)S(1)} %multiply_maximum_fusion, f32[4,4,128]{2,1,0:T(4,128)S(1)} %reshape.172, f32[4,4,16]{2,1,0:T(4,128)S(1)} %get-tuple-element.63, ...), kind=kOutput, calls=%fused_computation.23 | convolution fusion | flops 25559040 | bytes 2042880 | tf_op jit(solution)/shard_map/bkgc,bckd->bkgd/dot_general | solution.py:181
  22.4 0.9 broadcast_in_dim.55
  23.4 8.6 %all-to-all-start.1 = ((bf16[128,4,512]{2,1,0:T(4,128)(2,1)}), bf16[128,4,512]{2,1,0:T(4,128)(2,1)S(1)}, u32[]{:S(2)}, u32[]{:S(2)}) async-start(bf16[128,4,512]{2,1,0:T(4,128)(2,1)} %bitcast.8), calls=%async_computation.1 | async-start | bytes 1048576 | tf_op jit(solution)/shard_map/all_to_all | solution.py:244
  32.3 2.1 %convolution_convert_fusion.12 = bf16[128,2048]{1,0:T(8,128)(2,1)S(1)} fusion(bf16[512,2048]{1,0:T(8,128)(2,1)} %param.13, s32[128]{0:T(128)S(1)} %pad_add_fusion.2), kind=kOutput, calls=%fused_computation.12 | convolution fusion | flops 268763136 | bytes 2621952 | tf_op jit(solution)/shard_map/dot_general | solution.py:86
  34.4 9.5 %all-to-all-done.1 = bf16[128,4,512]{2,1,0:T(4,128)(2,1)S(1)} async-done(((bf16[128,4,512]{2,1,0:T(4,128)(2,1)}), bf16[128,4,512]{2,1,0:T(4,128)(2,1)S(1)}, u32[]{:S(2)}, u32[]{:S(2)}) %all-to-all-start.1) | async-done | bytes 524320 | tf_op jit(solution)/shard_map/all_to_all | solution.py:244
  44.8 1.5 convolution_convert_fusion.13
  47.9 2.8 %collective-permute-start = (bf16[64,2048]{1,0:T(8,128)(2,1)S(1)}, bf16[64,2048]{1,0:T(8,128)(2,1)S(1)}, u32[]{:S(2)}, u32[]{:S(2)}) collective-permute-start(bf16[64,2048]{1,0:T(8,128)(2,1)S(1)} %get-tuple-element.44), channel_id=1, source_target_pairs={{0,8},{1,9},{2,10},{3,11},{4,12},{5,13},{6,14},{7,15},{8,0},{9,1},... | collective-permute-start | bytes 786440 | tf_op jit(solution)/shard_map/ppermute | solution.py:41
  51.6 1.1 collective-permute-start.2
  52.8 1.0 collective-permute-start.23
  53.7 2.6 %collective-permute-start.24 = (bf16[64,2048]{1,0:T(8,128)(2,1)S(1)}, bf16[64,2048]{1,0:T(8,128)(2,1)S(1)}, u32[]{:S(2)}, u32[]{:S(2)}) collective-permute-start(bf16[64,2048]{1,0:T(8,128)(2,1)S(1)} %get-tuple-element.52), channel_id=1, source_target_pairs={{0,4},{1,5},{2,6},{3,7},{4,8},{5,9},{6,10},{7,11},{8,12},{9,13},{1... | collective-permute-start | bytes 786440 | tf_op jit(solution)/shard_map/ppermute | solution.py:41
  56.9 1.8 %collective-permute-done.1 = bf16[64,2048]{1,0:T(8,128)(2,1)S(1)} collective-permute-done((bf16[64,2048]{1,0:T(8,128)(2,1)S(1)}, bf16[64,2048]{1,0:T(8,128)(2,1)S(1)}, u32[]{:S(2)}, u32[]{:S(2)}) %collective-permute-start.1) | collective-permute-done | bytes 262176 | tf_op jit(solution)/shard_map/ppermute | solution.py:41
  58.7 3.2 %collective-permute-done.2 = bf16[64,2048]{1,0:T(8,128)(2,1)S(1)} collective-permute-done((bf16[64,2048]{1,0:T(8,128)(2,1)S(1)}, bf16[64,2048]{1,0:T(8,128)(2,1)S(1)}, u32[]{:S(2)}, u32[]{:S(2)}) %collective-permute-start.2) | collective-permute-done | bytes 262176 | tf_op jit(solution)/shard_map/ppermute | solution.py:41
  62.8 2.7 %collective-permute-start.4 = (bf16[64,2048]{1,0:T(8,128)(2,1)}, bf16[64,2048]{1,0:T(8,128)(2,1)S(1)}, u32[]{:S(2)}, u32[]{:S(2)}) collective-permute-start(bf16[64,2048]{1,0:T(8,128)(2,1)} %get-tuple-element.31), channel_id=1, source_target_pairs={{0,2},{1,3},{2,0},{3,1},{4,6},{5,7},{6,4},{7,5},{8,10},{9,11},{10,... | collective-permute-start | bytes 786440 | tf_op jit(solution)/shard_map/ppermute | solution.py:48
  65.5 1.0 collective-permute-done.25
  67.4 2.2 %collective-permute-start.26 = (bf16[64,2048]{1,0:T(8,128)(2,1)}, bf16[64,2048]{1,0:T(8,128)(2,1)S(1)}, u32[]{:S(2)}, u32[]{:S(2)}) collective-permute-start(bf16[64,2048]{1,0:T(8,128)(2,1)} %get-tuple-element.39), channel_id=1, source_target_pairs={{0,3},{1,0},{2,1},{3,2},{4,7},{5,4},{6,5},{7,6},{8,11},{9,8},{10,9... | collective-permute-start | bytes 786440 | tf_op jit(solution)/shard_map/ppermute | solution.py:48
  70.1 1.4 collective-permute-start.28
  71.4 2.3 %collective-permute-done.5.far_three = bf16[64,2048]{1,0:T(8,128)(2,1)S(1)} collective-permute-done((bf16[64,2048]{1,0:T(8,128)(2,1)}, bf16[64,2048]{1,0:T(8,128)(2,1)S(1)}, u32[]{:S(2)}, u32[]{:S(2)}) %collective-permute-start.5) | collective-permute-done | bytes 262176 | tf_op jit(solution)/shard_map/ppermute | solution.py:48
  74.1 1.7 collective-permute-start.7
  76.5 3.3 %collective-permute-start.8 = (bf16[64,2176]{1,0:T(8,128)(2,1)S(1)}, bf16[64,2176]{1,0:T(8,128)(2,1)S(1)}, u32[]{:S(2)}, u32[]{:S(2)}) collective-permute-start(bf16[64,2176]{1,0:T(8,128)(2,1)S(1)} %get-tuple-element.18), channel_id=1, source_target_pairs={{0,4},{1,5},{2,6},{3,7},{4,8},{5,9},{6,10},{7,11},{8,12},{9,13},{1... | collective-permute-start | bytes 835592 | tf_op jit(solution)/shard_map/ppermute | solution.py:41
  79.9 6.4 %collective-permute-done.28.far_three = bf16[64,2048]{1,0:T(8,128)(2,1)S(1)} collective-permute-done((bf16[64,2048]{1,0:T(8,128)(2,1)}, bf16[64,2048]{1,0:T(8,128)(2,1)S(1)}, u32[]{:S(2)}, u32[]{:S(2)}) %collective-permute-start.28) | collective-permute-done | bytes 262176 | tf_op jit(solution)/shard_map/ppermute | solution.py:48
  87.3 2.5 %collective-permute-start.30 = (bf16[64,2176]{1,0:T(8,128)(2,1)S(1)}, bf16[64,2176]{1,0:T(8,128)(2,1)S(1)}, u32[]{:S(2)}, u32[]{:S(2)}) collective-permute-start(bf16[64,2176]{1,0:T(8,128)(2,1)S(1)} %get-tuple-element.24), channel_id=1, source_target_pairs={{0,8},{1,9},{2,10},{3,11},{4,12},{5,13},{6,14},{7,15},{8,0},{9,1},... | collective-permute-start | bytes 835592 | tf_op jit(solution)/shard_map/ppermute | solution.py:41
  89.8 1.4 collective-permute-start.31
  91.8 5.5 %convolution_convert_fusion.7.upper = bf16[256,1792]{1,0:T(8,128)(2,1)S(1)} fusion(bf16[2048,1792]{1,0:T(8,128)(2,1)} %param.24, bf16[256,2176]{1,0:T(8,128)(2,1)S(1)} %convolution_convert_fusion.1), kind=kOutput, calls=%fused_computation.7 | convolution fusion | flops 1879506944 | bytes 9306112 | tf_op jit(solution)/shard_map/dot_general | solution.py:86
  97.3 2.1 %convolution_convert_fusion.8.gate = bf16[256,1792]{1,0:T(8,128)(2,1)S(1)} fusion(bf16[2048,1792]{1,0:T(8,128)(2,1)S(1)} %bitcast.66, bf16[256,2176]{1,0:T(8,128)(2,1)S(1)} %convolution_convert_fusion.1), kind=kOutput, calls=%fused_computation.8 | convolution fusion | flops 1879506944 | bytes 9306112 | tf_op jit(solution)/shard_map/dot_general | solution.py:86
  100.2 2.1 %convolution_convert_fusion.3.upper = bf16[256,1792]{1,0:T(8,128)(2,1)S(1)} fusion(bf16[2048,1792]{1,0:T(8,128)(2,1)S(1)} %bitcast.64, bf16[256,2176]{1,0:T(8,128)(2,1)S(1)} %convolution_convert_fusion), kind=kOutput, calls=%fused_computation.3 | convolution fusion | flops 1879506944 | bytes 9306112 | tf_op jit(solution)/shard_map/dot_general | solution.py:86
  102.3 2.1 %convolution_convert_fusion.4.gate = bf16[256,1792]{1,0:T(8,128)(2,1)S(1)} fusion(bf16[2048,1792]{1,0:T(8,128)(2,1)S(1)} %bitcast.66, bf16[256,2176]{1,0:T(8,128)(2,1)S(1)} %convolution_convert_fusion), kind=kOutput, calls=%fused_computation.4 | convolution fusion | flops 1879506944 | bytes 9306112 | tf_op jit(solution)/shard_map/dot_general | solution.py:86
  105.4 1.4 collective-permute-start.10
  107.4 2.6 %collective-permute-start.12 = (bf16[32,3712]{1,0:T(8,128)(2,1)S(1)}, bf16[32,3712]{1,0:T(8,128)(2,1)S(1)}, u32[]{:S(2)}, u32[]{:S(2)}) collective-permute-start(bf16[32,3712]{1,0:T(8,128)(2,1)S(1)} %get-tuple-element.22), channel_id=1, source_target_pairs={{0,96},{1,97},{2,98},{3,99},{4,100},{5,101},{6,102},{7,103},{8,104... | collective-permute-start | bytes 712712 | tf_op jit(solution)/shard_map/ppermute | solution.py:52
  110.4 1.1 collective-permute-start.33
  111.5 1.1 collective-permute-start.34
  112.6 3.0 %collective-permute-done.10.one = bf16[32,3712]{1,0:T(8,128)(2,1)S(1)} collective-permute-done((bf16[32,3712]{1,0:T(8,128)(2,1)S(1)}, bf16[32,3712]{1,0:T(8,128)(2,1)S(1)}, u32[]{:S(2)}, u32[]{:S(2)}) %collective-permute-start.10) | collective-permute-done | bytes 237600 | tf_op jit(solution)/shard_map/ppermute | solution.py:52
  115.7 1.0 collective-permute-start.35
  116.7 4.1 %collective-permute-done.11.two = bf16[32,3712]{1,0:T(8,128)(2,1)S(1)} collective-permute-done((bf16[32,3712]{1,0:T(8,128)(2,1)S(1)}, bf16[32,3712]{1,0:T(8,128)(2,1)S(1)}, u32[]{:S(2)}, u32[]{:S(2)}) %collective-permute-start.11) | collective-permute-done | bytes 237600 | tf_op jit(solution)/shard_map/ppermute | solution.py:52
  121.1 1.1 collective-permute-start.13
  122.3 2.1 %collective-permute-start.14 = (bf16[32,1792]{1,0:T(8,128)(2,1)S(1)}, bf16[32,1792]{1,0:T(8,128)(2,1)S(1)}, u32[]{:S(2)}, u32[]{:S(2)}) collective-permute-start(bf16[32,1792]{1,0:T(8,128)(2,1)S(1)} %shard_map.130), channel_id=1, source_target_pairs={{0,64},{1,65},{2,66},{3,67},{4,68},{5,69},{6,70},{7,71},{8,72},{9,... | collective-permute-start | bytes 344072 | tf_op jit(solution)/shard_map/ppermute | solution.py:52
  124.4 1.5 collective-permute-done.33.one
  125.9 1.1 collective-permute-start.15
  127.0 4.0 %collective-permute-done.34.two = bf16[32,3712]{1,0:T(8,128)(2,1)S(1)} collective-permute-done((bf16[32,3712]{1,0:T(8,128)(2,1)S(1)}, bf16[32,3712]{1,0:T(8,128)(2,1)S(1)}, u32[]{:S(2)}, u32[]{:S(2)}) %collective-permute-start.34) | collective-permute-done | bytes 237600 | tf_op jit(solution)/shard_map/ppermute | solution.py:52
  131.9 1.7 collective-permute-start.37
  135.0 2.4 %collective-permute-done.36 = bf16[32,1792]{1,0:T(8,128)(2,1)S(1)} collective-permute-done((bf16[32,1792]{1,0:T(8,128)(2,1)S(1)}, bf16[32,1792]{1,0:T(8,128)(2,1)S(1)}, u32[]{:S(2)}, u32[]{:S(2)}) %collective-permute-start.36) | collective-permute-done | bytes 114720 | tf_op jit(solution)/shard_map/ppermute | solution.py:52
  137.4 1.8 collective-permute-done.37
  139.2 1.4 collective-permute-done.38
  141.8 5.4 %convolution_convert_fusion.6 = bf16[256,2048]{1,0:T(8,128)(2,1)S(1)} fusion(bf16[1792,2048]{1,0:T(8,128)(2,1)} %param.25, bf16[256,1792]{1,0:T(8,128)(2,1)S(1)} %constant_dynamic-update-slice_fusion, s32[256]{0:T(256)S(1)} %fusion.76), kind=kOutput, calls=%fused_computation.6 | convolution fusion | flops 2114977792 | bytes 9307136 | tf_op jit(solution)/shard_map/dot_general | solution.py:86
  147.2 1.0 fusion.97
  148.2 1.3 collective-permute-start.17
  149.5 1.9 %collective-permute-start.18 = (bf16[64,2048]{1,0:T(8,128)(2,1)}, bf16[64,2048]{1,0:T(8,128)(2,1)}, u32[]{:S(2)}, u32[]{:S(2)}) collective-permute-start(bf16[64,2048]{1,0:T(8,128)(2,1)} %get-tuple-element.43), channel_id=1, source_target_pairs={{0,4},{1,5},{2,6},{3,7},{4,8},{5,9},{6,10},{7,11},{8,12},{9,13},{1... | collective-permute-start | bytes 786440 | tf_op jit(solution)/shard_map/ppermute | solution.py:41
  152.4 5.7 %convolution_convert_fusion.2 = bf16[256,2048]{1,0:T(8,128)(2,1)S(1)} fusion(bf16[1792,2048]{1,0:T(8,128)(2,1)} %param.25, bf16[256,1792]{1,0:T(8,128)(2,1)} %constant_dynamic-update-slice_fusion.5, s32[256]{0:T(256)S(1)} %fusion.76), kind=kOutput, calls=%fused_computation.2 | convolution fusion | flops 2114977792 | bytes 9307136 | tf_op jit(solution)/shard_map/dot_general | solution.py:86
  158.2 2.3 %collective-permute-start.40 = (bf16[64,2048]{1,0:T(8,128)(2,1)S(1)}, bf16[64,2048]{1,0:T(8,128)(2,1)S(1)}, u32[]{:S(2)}, u32[]{:S(2)}) collective-permute-start(bf16[64,2048]{1,0:T(8,128)(2,1)S(1)} %get-tuple-element.47), channel_id=1, source_target_pairs={{0,8},{1,9},{2,10},{3,11},{4,12},{5,13},{6,14},{7,15},{8,0},{9,1},... | collective-permute-start | bytes 786440 | tf_op jit(solution)/shard_map/ppermute | solution.py:41
  160.5 1.0 collective-permute-start.41
  161.5 1.0 collective-permute-start.42
  162.5 1.4 fusion.93
  163.9 1.8 collective-permute-start.20
  166.1 2.8 %collective-permute-start.22 = (bf16[16,2048]{1,0:T(8,128)(2,1)S(1)}, bf16[16,2048]{1,0:T(8,128)(2,1)S(1)}, u32[]{:S(2)}, u32[]{:S(2)}) collective-permute-start(bf16[16,2048]{1,0:T(8,128)(2,1)S(1)} %get-tuple-element.56), channel_id=1, source_target_pairs={{0,3},{1,0},{2,1},{3,2},{4,7},{5,4},{6,5},{7,6},{8,11},{9,8},{10,9... | collective-permute-start | bytes 196616 | tf_op jit(solution)/shard_map/ppermute | solution.py:48
  169.0 1.9 %collective-permute-done.41 = bf16[64,2048]{1,0:T(8,128)(2,1)S(1)} collective-permute-done((bf16[64,2048]{1,0:T(8,128)(2,1)S(1)}, bf16[64,2048]{1,0:T(8,128)(2,1)S(1)}, u32[]{:S(2)}, u32[]{:S(2)}) %collective-permute-start.41) | collective-permute-done | bytes 262176 | tf_op jit(solution)/shard_map/ppermute | solution.py:41
  171.0 1.3 collective-permute-start.43
  172.7 2.8 %collective-permute-start.45 = (bf16[16,2048]{1,0:T(8,128)(2,1)S(1)}, bf16[16,2048]{1,0:T(8,128)(2,1)S(1)}, u32[]{:S(2)}, u32[]{:S(2)}) collective-permute-start(bf16[16,2048]{1,0:T(8,128)(2,1)S(1)} %get-tuple-element.59), channel_id=1, source_target_pairs={{0,3},{1,0},{2,1},{3,2},{4,7},{5,4},{6,5},{7,6},{8,11},{9,8},{10,9... | collective-permute-start | bytes 196616 | tf_op jit(solution)/shard_map/ppermute | solution.py:48
  175.6 1.2 collective-permute-done.43
  176.8 0.9 collective-permute-done.44
  (142 shorter events, 21.2 us)
Async XLA Ops:
  0.0 46.4 %copy-start = (bf16[512,2048]{1,0:T(8,128)(2,1)S(1)}, bf16[512,2048]{1,0:T(8,128)(2,1)}, u32[]{:S(2)}) copy-start(bf16[512,2048]{1,0:T(8,128)(2,1)} %param.21) | copy-start | bytes 6291460
  4.4 13.1 %all-to-all-start = ((bf16[16,4,576]{2,1,0:T(4,128)(2,1)}), bf16[16,4,576]{2,1,0:T(4,128)(2,1)S(1)}, u32[]{:S(2)}, u32[]{:S(2)}) async-start(bf16[16,4,576]{2,1,0:T(4,128)(2,1)} %all_to_all.9), calls=%async_computation | async-start | bytes 163840 | tf_op jit(solution)/shard_map/all_to_all | solution.py:224
  20.4 11.6 %copy-start.4 = (s32[512]{0:T(512)S(1)}, s32[512]{0:T(512)}, u32[]{:S(2)}) copy-start(s32[512]{0:T(512)} %param.20) | copy-start | bytes 6148
  23.4 20.5 %all-to-all-start.1 = ((bf16[128,4,512]{2,1,0:T(4,128)(2,1)}), bf16[128,4,512]{2,1,0:T(4,128)(2,1)S(1)}, u32[]{:S(2)}, u32[]{:S(2)}) async-start(bf16[128,4,512]{2,1,0:T(4,128)(2,1)} %bitcast.8), calls=%async_computation.1 | async-start | bytes 1048576 | tf_op jit(solution)/shard_map/all_to_all | solution.py:244
  47.9 8.5 %collective-permute-start = (bf16[64,2048]{1,0:T(8,128)(2,1)S(1)}, bf16[64,2048]{1,0:T(8,128)(2,1)S(1)}, u32[]{:S(2)}, u32[]{:S(2)}) collective-permute-start(bf16[64,2048]{1,0:T(8,128)(2,1)S(1)} %get-tuple-element.44), channel_id=1, source_target_pairs={{0,8},{1,9},{2,10},{3,11},{4,12},{5,13},{6,14},{7,15},{8,0},{9,1},... | collective-permute-start | bytes 786440 | tf_op jit(solution)/shard_map/ppermute | solution.py:41
  50.7 8.0 %collective-permute-start.1 = (bf16[64,2048]{1,0:T(8,128)(2,1)S(1)}, bf16[64,2048]{1,0:T(8,128)(2,1)S(1)}, u32[]{:S(2)}, u32[]{:S(2)}) collective-permute-start(bf16[64,2048]{1,0:T(8,128)(2,1)S(1)} %get-tuple-element.46), channel_id=1, source_target_pairs={{0,4},{1,5},{2,6},{3,7},{4,8},{5,9},{6,10},{7,11},{8,12},{9,13},{1... | collective-permute-start | bytes 786440 | tf_op jit(solution)/shard_map/ppermute | solution.py:41
  51.6 10.4 %collective-permute-start.2 = (bf16[64,2048]{1,0:T(8,128)(2,1)S(1)}, bf16[64,2048]{1,0:T(8,128)(2,1)S(1)}, u32[]{:S(2)}, u32[]{:S(2)}) collective-permute-start(bf16[64,2048]{1,0:T(8,128)(2,1)S(1)} %get-tuple-element.45), channel_id=1, source_target_pairs={{0,12},{1,13},{2,14},{3,15},{4,0},{5,1},{6,2},{7,3},{8,4},{9,5},{1... | collective-permute-start | bytes 786440 | tf_op jit(solution)/shard_map/ppermute | solution.py:41
  52.8 12.7 %collective-permute-start.23 = (bf16[64,2048]{1,0:T(8,128)(2,1)S(1)}, bf16[64,2048]{1,0:T(8,128)(2,1)S(1)}, u32[]{:S(2)}, u32[]{:S(2)}) collective-permute-start(bf16[64,2048]{1,0:T(8,128)(2,1)S(1)} %get-tuple-element.50), channel_id=1, source_target_pairs={{0,8},{1,9},{2,10},{3,11},{4,12},{5,13},{6,14},{7,15},{8,0},{9,1},... | collective-permute-start | bytes 786440 | tf_op jit(solution)/shard_map/ppermute | solution.py:41
  53.7 11.8 %collective-permute-start.24 = (bf16[64,2048]{1,0:T(8,128)(2,1)S(1)}, bf16[64,2048]{1,0:T(8,128)(2,1)S(1)}, u32[]{:S(2)}, u32[]{:S(2)}) collective-permute-start(bf16[64,2048]{1,0:T(8,128)(2,1)S(1)} %get-tuple-element.52), channel_id=1, source_target_pairs={{0,4},{1,5},{2,6},{3,7},{4,8},{5,9},{6,10},{7,11},{8,12},{9,13},{1... | collective-permute-start | bytes 786440 | tf_op jit(solution)/shard_map/ppermute | solution.py:41
  56.4 17.3 %copy-start.2 = (f32[2048]{0:T(1024)S(1)}, f32[2048]{0:T(1024)}, u32[]{:S(2)}) copy-start(f32[2048]{0:T(1024)} %param.22) | copy-start | bytes 24580
  56.4 10.1 %collective-permute-start.25 = (bf16[64,2048]{1,0:T(8,128)(2,1)S(1)}, bf16[64,2048]{1,0:T(8,128)(2,1)S(1)}, u32[]{:S(2)}, u32[]{:S(2)}) collective-permute-start(bf16[64,2048]{1,0:T(8,128)(2,1)S(1)} %get-tuple-element.51), channel_id=1, source_target_pairs={{0,12},{1,13},{2,14},{3,15},{4,0},{5,1},{6,2},{7,3},{8,4},{9,5},{1... | collective-permute-start | bytes 786440 | tf_op jit(solution)/shard_map/ppermute | solution.py:41
  62.8 7.3 %collective-permute-start.3 = (bf16[64,2048]{1,0:T(8,128)(2,1)}, bf16[64,2048]{1,0:T(8,128)(2,1)S(1)}, u32[]{:S(2)}, u32[]{:S(2)}) collective-permute-start(bf16[64,2048]{1,0:T(8,128)(2,1)} %get-tuple-element.31), channel_id=1, source_target_pairs={{0,3},{1,0},{2,1},{3,2},{4,7},{5,4},{6,5},{7,6},{8,11},{9,8},{10,9... | collective-permute-start | bytes 786440 | tf_op jit(solution)/shard_map/ppermute | solution.py:48
  62.8 8.6 %collective-permute-start.4 = (bf16[64,2048]{1,0:T(8,128)(2,1)}, bf16[64,2048]{1,0:T(8,128)(2,1)S(1)}, u32[]{:S(2)}, u32[]{:S(2)}) collective-permute-start(bf16[64,2048]{1,0:T(8,128)(2,1)} %get-tuple-element.31), channel_id=1, source_target_pairs={{0,2},{1,3},{2,0},{3,1},{4,6},{5,7},{6,4},{7,5},{8,10},{9,11},{10,... | collective-permute-start | bytes 786440 | tf_op jit(solution)/shard_map/ppermute | solution.py:48
  65.5 8.2 %collective-permute-start.5 = (bf16[64,2048]{1,0:T(8,128)(2,1)}, bf16[64,2048]{1,0:T(8,128)(2,1)S(1)}, u32[]{:S(2)}, u32[]{:S(2)}) collective-permute-start(bf16[64,2048]{1,0:T(8,128)(2,1)} %get-tuple-element.31), channel_id=1, source_target_pairs={{0,1},{1,2},{2,3},{3,0},{4,5},{5,6},{6,7},{7,4},{8,9},{9,10},{10,1... | collective-permute-start | bytes 786440 | tf_op jit(solution)/shard_map/ppermute | solution.py:48
  67.4 9.1 %collective-permute-start.26 = (bf16[64,2048]{1,0:T(8,128)(2,1)}, bf16[64,2048]{1,0:T(8,128)(2,1)S(1)}, u32[]{:S(2)}, u32[]{:S(2)}) collective-permute-start(bf16[64,2048]{1,0:T(8,128)(2,1)} %get-tuple-element.39), channel_id=1, source_target_pairs={{0,3},{1,0},{2,1},{3,2},{4,7},{5,4},{6,5},{7,6},{8,11},{9,8},{10,9... | collective-permute-start | bytes 786440 | tf_op jit(solution)/shard_map/ppermute | solution.py:48
  69.7 10.3 %collective-permute-start.27 = (bf16[64,2048]{1,0:T(8,128)(2,1)}, bf16[64,2048]{1,0:T(8,128)(2,1)S(1)}, u32[]{:S(2)}, u32[]{:S(2)}) collective-permute-start(bf16[64,2048]{1,0:T(8,128)(2,1)} %get-tuple-element.39), channel_id=1, source_target_pairs={{0,2},{1,3},{2,0},{3,1},{4,6},{5,7},{6,4},{7,5},{8,10},{9,11},{10,... | collective-permute-start | bytes 786440 | tf_op jit(solution)/shard_map/ppermute | solution.py:48
  70.1 16.3 %collective-permute-start.28 = (bf16[64,2048]{1,0:T(8,128)(2,1)}, bf16[64,2048]{1,0:T(8,128)(2,1)S(1)}, u32[]{:S(2)}, u32[]{:S(2)}) collective-permute-start(bf16[64,2048]{1,0:T(8,128)(2,1)} %get-tuple-element.39), channel_id=1, source_target_pairs={{0,1},{1,2},{2,3},{3,0},{4,5},{5,6},{6,7},{7,4},{8,9},{9,10},{10,1... | collective-permute-start | bytes 786440 | tf_op jit(solution)/shard_map/ppermute | solution.py:48
  74.0 15.8 %collective-permute-start.6 = (bf16[64,2176]{1,0:T(8,128)(2,1)S(1)}, bf16[64,2176]{1,0:T(8,128)(2,1)S(1)}, u32[]{:S(2)}, u32[]{:S(2)}) collective-permute-start(bf16[64,2176]{1,0:T(8,128)(2,1)S(1)} %get-tuple-element.18), channel_id=1, source_target_pairs={{0,12},{1,13},{2,14},{3,15},{4,0},{5,1},{6,2},{7,3},{8,4},{9,5},{1... | collective-permute-start | bytes 835592 | tf_op jit(solution)/shard_map/ppermute | solution.py:41
  74.1 17.1 %collective-permute-start.7 = (bf16[64,2176]{1,0:T(8,128)(2,1)S(1)}, bf16[64,2176]{1,0:T(8,128)(2,1)S(1)}, u32[]{:S(2)}, u32[]{:S(2)}) collective-permute-start(bf16[64,2176]{1,0:T(8,128)(2,1)S(1)} %get-tuple-element.18), channel_id=1, source_target_pairs={{0,8},{1,9},{2,10},{3,11},{4,12},{5,13},{6,14},{7,15},{8,0},{9,1},... | collective-permute-start | bytes 835592 | tf_op jit(solution)/shard_map/ppermute | solution.py:41
  76.5 14.7 %collective-permute-start.8 = (bf16[64,2176]{1,0:T(8,128)(2,1)S(1)}, bf16[64,2176]{1,0:T(8,128)(2,1)S(1)}, u32[]{:S(2)}, u32[]{:S(2)}) collective-permute-start(bf16[64,2176]{1,0:T(8,128)(2,1)S(1)} %get-tuple-element.18), channel_id=1, source_target_pairs={{0,4},{1,5},{2,6},{3,7},{4,8},{5,9},{6,10},{7,11},{8,12},{9,13},{1... | collective-permute-start | bytes 835592 | tf_op jit(solution)/shard_map/ppermute | solution.py:41
  86.7 12.9 %collective-permute-start.29 = (bf16[64,2176]{1,0:T(8,128)(2,1)S(1)}, bf16[64,2176]{1,0:T(8,128)(2,1)S(1)}, u32[]{:S(2)}, u32[]{:S(2)}) collective-permute-start(bf16[64,2176]{1,0:T(8,128)(2,1)S(1)} %get-tuple-element.24), channel_id=1, source_target_pairs={{0,12},{1,13},{2,14},{3,15},{4,0},{5,1},{6,2},{7,3},{8,4},{9,5},{1... | collective-permute-start | bytes 835592 | tf_op jit(solution)/shard_map/ppermute | solution.py:41
  87.3 12.3 %collective-permute-start.30 = (bf16[64,2176]{1,0:T(8,128)(2,1)S(1)}, bf16[64,2176]{1,0:T(8,128)(2,1)S(1)}, u32[]{:S(2)}, u32[]{:S(2)}) collective-permute-start(bf16[64,2176]{1,0:T(8,128)(2,1)S(1)} %get-tuple-element.24), channel_id=1, source_target_pairs={{0,8},{1,9},{2,10},{3,11},{4,12},{5,13},{6,14},{7,15},{8,0},{9,1},... | collective-permute-start | bytes 835592 | tf_op jit(solution)/shard_map/ppermute | solution.py:41
  89.8 9.8 %collective-permute-start.31 = (bf16[64,2176]{1,0:T(8,128)(2,1)S(1)}, bf16[64,2176]{1,0:T(8,128)(2,1)S(1)}, u32[]{:S(2)}, u32[]{:S(2)}) collective-permute-start(bf16[64,2176]{1,0:T(8,128)(2,1)S(1)} %get-tuple-element.24), channel_id=1, source_target_pairs={{0,4},{1,5},{2,6},{3,7},{4,8},{5,9},{6,10},{7,11},{8,12},{9,13},{1... | collective-permute-start | bytes 835592 | tf_op jit(solution)/shard_map/ppermute | solution.py:41
  91.2 6.0 %slice-start.2 = ((s8[7340032]{0:T(1024)(128)(4,1)}), s8[4194304]{0:T(1024)(128)(4,1)S(1)}, s32[]{:S(2)}) async-start(s8[7340032]{0:T(1024)(128)(4,1)} %bitcast.65), calls=%async_computation.4 | async-start | bytes 8388608
  91.7 5.5 %slice-start.3 = ((s8[7340032]{0:T(1024)(128)(4,1)}), s8[3145728]{0:T(1024)(128)(4,1)S(1)}, s32[]{:S(2)}) async-start(s8[7340032]{0:T(1024)(128)(4,1)} %bitcast.65), calls=%async_computation.5 | async-start | bytes 6291456
  91.8 8.4 %slice-start = ((s8[7340032]{0:T(1024)(128)(4,1)}), s8[4194304]{0:T(1024)(128)(4,1)S(1)}, s32[]{:S(2)}) async-start(s8[7340032]{0:T(1024)(128)(4,1)} %bitcast.63), calls=%async_computation.2 | async-start | bytes 8388608
  97.3 2.9 %slice-start.1 = ((s8[7340032]{0:T(1024)(128)(4,1)}), s8[3145728]{0:T(1024)(128)(4,1)S(1)}, s32[]{:S(2)}) async-start(s8[7340032]{0:T(1024)(128)(4,1)} %bitcast.63), calls=%async_computation.3 | async-start | bytes 6291456
  99.5 5.5 %collective-permute-start.9 = (bf16[128,3712]{1,0:T(8,128)(2,1)S(1)}, bf16[128,3712]{1,0:T(8,128)(2,1)S(1)}, u32[]{:S(2)}, u32[]{:S(2)}) collective-permute-start(bf16[128,3712]{1,0:T(8,128)(2,1)S(1)} %shard_map.128), channel_id=1, source_target_pairs={{0,16},{1,17},{2,18},{3,19},{4,20},{5,21},{6,22},{7,23},{8,24},{9,... | collective-permute-start | bytes 2850824 | tf_op jit(solution)/shard_map/ppermute | solution.py:56
  104.5 5.6 %collective-permute-start.32 = (bf16[128,3712]{1,0:T(8,128)(2,1)S(1)}, bf16[128,3712]{1,0:T(8,128)(2,1)S(1)}, u32[]{:S(2)}, u32[]{:S(2)}) collective-permute-start(bf16[128,3712]{1,0:T(8,128)(2,1)S(1)} %shard_map.132), channel_id=1, source_target_pairs={{0,16},{1,17},{2,18},{3,19},{4,20},{5,21},{6,22},{7,23},{8,24},{9,... | collective-permute-start | bytes 2850824 | tf_op jit(solution)/shard_map/ppermute | solution.py:56
  105.4 10.3 %collective-permute-start.10 = (bf16[32,3712]{1,0:T(8,128)(2,1)S(1)}, bf16[32,3712]{1,0:T(8,128)(2,1)S(1)}, u32[]{:S(2)}, u32[]{:S(2)}) collective-permute-start(bf16[32,3712]{1,0:T(8,128)(2,1)S(1)} %get-tuple-element.20), channel_id=1, source_target_pairs={{0,64},{1,65},{2,66},{3,67},{4,68},{5,69},{6,70},{7,71},{8,72},{9,... | collective-permute-start | bytes 712712 | tf_op jit(solution)/shard_map/ppermute | solution.py:52
  106.8 14.0 %collective-permute-start.11 = (bf16[32,3712]{1,0:T(8,128)(2,1)S(1)}, bf16[32,3712]{1,0:T(8,128)(2,1)S(1)}, u32[]{:S(2)}, u32[]{:S(2)}) collective-permute-start(bf16[32,3712]{1,0:T(8,128)(2,1)S(1)} %get-tuple-element.21), channel_id=1, source_target_pairs={{0,32},{1,33},{2,34},{3,35},{4,36},{5,37},{6,38},{7,39},{8,40},{9,... | collective-permute-start | bytes 712712 | tf_op jit(solution)/shard_map/ppermute | solution.py:52
  107.4 13.4 %collective-permute-start.12 = (bf16[32,3712]{1,0:T(8,128)(2,1)S(1)}, bf16[32,3712]{1,0:T(8,128)(2,1)S(1)}, u32[]{:S(2)}, u32[]{:S(2)}) collective-permute-start(bf16[32,3712]{1,0:T(8,128)(2,1)S(1)} %get-tuple-element.22), channel_id=1, source_target_pairs={{0,96},{1,97},{2,98},{3,99},{4,100},{5,101},{6,102},{7,103},{8,104... | collective-permute-start | bytes 712712 | tf_op jit(solution)/shard_map/ppermute | solution.py:52
  110.4 15.5 %collective-permute-start.33 = (bf16[32,3712]{1,0:T(8,128)(2,1)S(1)}, bf16[32,3712]{1,0:T(8,128)(2,1)S(1)}, u32[]{:S(2)}, u32[]{:S(2)}) collective-permute-start(bf16[32,3712]{1,0:T(8,128)(2,1)S(1)} %get-tuple-element.26), channel_id=1, source_target_pairs={{0,64},{1,65},{2,66},{3,67},{4,68},{5,69},{6,70},{7,71},{8,72},{9,... | collective-permute-start | bytes 712712 | tf_op jit(solution)/shard_map/ppermute | solution.py:52
  111.5 19.5 %collective-permute-start.34 = (bf16[32,3712]{1,0:T(8,128)(2,1)S(1)}, bf16[32,3712]{1,0:T(8,128)(2,1)S(1)}, u32[]{:S(2)}, u32[]{:S(2)}) collective-permute-start(bf16[32,3712]{1,0:T(8,128)(2,1)S(1)} %get-tuple-element.27), channel_id=1, source_target_pairs={{0,32},{1,33},{2,34},{3,35},{4,36},{5,37},{6,38},{7,39},{8,40},{9,... | collective-permute-start | bytes 712712 | tf_op jit(solution)/shard_map/ppermute | solution.py:52
  115.7 15.3 %collective-permute-start.35 = (bf16[32,3712]{1,0:T(8,128)(2,1)S(1)}, bf16[32,3712]{1,0:T(8,128)(2,1)S(1)}, u32[]{:S(2)}, u32[]{:S(2)}) collective-permute-start(bf16[32,3712]{1,0:T(8,128)(2,1)S(1)} %get-tuple-element.28), channel_id=1, source_target_pairs={{0,96},{1,97},{2,98},{3,99},{4,100},{5,101},{6,102},{7,103},{8,104... | collective-permute-start | bytes 712712 | tf_op jit(solution)/shard_map/ppermute | solution.py:52
  121.1 12.5 %collective-permute-start.13 = (bf16[32,1792]{1,0:T(8,128)(2,1)S(1)}, bf16[32,1792]{1,0:T(8,128)(2,1)S(1)}, u32[]{:S(2)}, u32[]{:S(2)}) collective-permute-start(bf16[32,1792]{1,0:T(8,128)(2,1)S(1)} %shard_map.130), channel_id=1, source_target_pairs={{0,96},{1,97},{2,98},{3,99},{4,100},{5,101},{6,102},{7,103},{8,104... | collective-permute-start | bytes 344072 | tf_op jit(solution)/shard_map/ppermute | solution.py:52
  122.3 12.4 %collective-permute-start.14 = (bf16[32,1792]{1,0:T(8,128)(2,1)S(1)}, bf16[32,1792]{1,0:T(8,128)(2,1)S(1)}, u32[]{:S(2)}, u32[]{:S(2)}) collective-permute-start(bf16[32,1792]{1,0:T(8,128)(2,1)S(1)} %shard_map.130), channel_id=1, source_target_pairs={{0,64},{1,65},{2,66},{3,67},{4,68},{5,69},{6,70},{7,71},{8,72},{9,... | collective-permute-start | bytes 344072 | tf_op jit(solution)/shard_map/ppermute | solution.py:52
  125.9 9.0 %collective-permute-start.15 = (bf16[32,1792]{1,0:T(8,128)(2,1)S(1)}, bf16[32,1792]{1,0:T(8,128)(2,1)S(1)}, u32[]{:S(2)}, u32[]{:S(2)}) collective-permute-start(bf16[32,1792]{1,0:T(8,128)(2,1)S(1)} %shard_map.130), channel_id=1, source_target_pairs={{0,32},{1,33},{2,34},{3,35},{4,36},{5,37},{6,38},{7,39},{8,40},{9,... | collective-permute-start | bytes 344072 | tf_op jit(solution)/shard_map/ppermute | solution.py:52
  131.3 6.1 %collective-permute-start.36 = (bf16[32,1792]{1,0:T(8,128)(2,1)S(1)}, bf16[32,1792]{1,0:T(8,128)(2,1)S(1)}, u32[]{:S(2)}, u32[]{:S(2)}) collective-permute-start(bf16[32,1792]{1,0:T(8,128)(2,1)S(1)} %shard_map.134), channel_id=1, source_target_pairs={{0,96},{1,97},{2,98},{3,99},{4,100},{5,101},{6,102},{7,103},{8,104... | collective-permute-start | bytes 344072 | tf_op jit(solution)/shard_map/ppermute | solution.py:52
  131.9 7.2 %collective-permute-start.37 = (bf16[32,1792]{1,0:T(8,128)(2,1)S(1)}, bf16[32,1792]{1,0:T(8,128)(2,1)S(1)}, u32[]{:S(2)}, u32[]{:S(2)}) collective-permute-start(bf16[32,1792]{1,0:T(8,128)(2,1)S(1)} %shard_map.134), channel_id=1, source_target_pairs={{0,64},{1,65},{2,66},{3,67},{4,68},{5,69},{6,70},{7,71},{8,72},{9,... | collective-permute-start | bytes 344072 | tf_op jit(solution)/shard_map/ppermute | solution.py:52
  133.7 6.9 %collective-permute-start.38 = (bf16[32,1792]{1,0:T(8,128)(2,1)S(1)}, bf16[32,1792]{1,0:T(8,128)(2,1)S(1)}, u32[]{:S(2)}, u32[]{:S(2)}) collective-permute-start(bf16[32,1792]{1,0:T(8,128)(2,1)S(1)} %shard_map.134), channel_id=1, source_target_pairs={{0,32},{1,33},{2,34},{3,35},{4,36},{5,37},{6,38},{7,39},{8,40},{9,... | collective-permute-start | bytes 344072 | tf_op jit(solution)/shard_map/ppermute | solution.py:52
  134.9 5.9 %collective-permute-start.16 = (bf16[128,1792]{1,0:T(8,128)(2,1)S(1)}, bf16[128,1792]{1,0:T(8,128)(2,1)S(1)}, u32[]{:S(2)}, u32[]{:S(2)}) collective-permute-start(bf16[128,1792]{1,0:T(8,128)(2,1)S(1)} %pad_maximum_fusion), channel_id=1, source_target_pairs={{0,16},{1,17},{2,18},{3,19},{4,20},{5,21},{6,22},{7,23},{8,24},{9,... | collective-permute-start | bytes 1376264 | tf_op jit(solution)/shard_map/ppermute | solution.py:56
  140.6 10.9 %collective-permute-start.39 = (bf16[128,1792]{1,0:T(8,128)(2,1)S(1)}, bf16[128,1792]{1,0:T(8,128)(2,1)S(1)}, u32[]{:S(2)}, u32[]{:S(2)}) collective-permute-start(bf16[128,1792]{1,0:T(8,128)(2,1)S(1)} %pad_maximum_fusion.1), channel_id=1, source_target_pairs={{0,16},{1,17},{2,18},{3,19},{4,20},{5,21},{6,22},{7,23},{8,24},{9,... | collective-permute-start | bytes 1376264 | tf_op jit(solution)/shard_map/ppermute | solution.py:56
  140.8 0.9 copy-start.5
  147.2 10.9 %copy-start.3 = (bf16[256,2048]{1,0:T(8,128)(2,1)}, bf16[256,2048]{1,0:T(8,128)(2,1)S(1)}, u32[]{:S(2)}) copy-start(bf16[256,2048]{1,0:T(8,128)(2,1)S(1)} %convolution_convert_fusion.6) | copy-start | bytes 3145732
  148.2 13.2 %collective-permute-start.17 = (bf16[64,2048]{1,0:T(8,128)(2,1)}, bf16[64,2048]{1,0:T(8,128)(2,1)S(1)}, u32[]{:S(2)}, u32[]{:S(2)}) collective-permute-start(bf16[64,2048]{1,0:T(8,128)(2,1)} %get-tuple-element.41), channel_id=1, source_target_pairs={{0,8},{1,9},{2,10},{3,11},{4,12},{5,13},{6,14},{7,15},{8,0},{9,1},... | collective-permute-start | bytes 786440 | tf_op jit(solution)/shard_map/ppermute | solution.py:41
  149.5 13.0 %collective-permute-start.18 = (bf16[64,2048]{1,0:T(8,128)(2,1)}, bf16[64,2048]{1,0:T(8,128)(2,1)}, u32[]{:S(2)}, u32[]{:S(2)}) collective-permute-start(bf16[64,2048]{1,0:T(8,128)(2,1)} %get-tuple-element.43), channel_id=1, source_target_pairs={{0,4},{1,5},{2,6},{3,7},{4,8},{5,9},{6,10},{7,11},{8,12},{9,13},{1... | collective-permute-start | bytes 786440 | tf_op jit(solution)/shard_map/ppermute | solution.py:41
  151.4 11.1 %collective-permute-start.19 = (bf16[64,2048]{1,0:T(8,128)(2,1)}, bf16[64,2048]{1,0:T(8,128)(2,1)}, u32[]{:S(2)}, u32[]{:S(2)}) collective-permute-start(bf16[64,2048]{1,0:T(8,128)(2,1)} %get-tuple-element.42), channel_id=1, source_target_pairs={{0,12},{1,13},{2,14},{3,15},{4,0},{5,1},{6,2},{7,3},{8,4},{9,5},{1... | collective-permute-start | bytes 786440 | tf_op jit(solution)/shard_map/ppermute | solution.py:41
  158.2 8.0 %collective-permute-start.40 = (bf16[64,2048]{1,0:T(8,128)(2,1)S(1)}, bf16[64,2048]{1,0:T(8,128)(2,1)S(1)}, u32[]{:S(2)}, u32[]{:S(2)}) collective-permute-start(bf16[64,2048]{1,0:T(8,128)(2,1)S(1)} %get-tuple-element.47), channel_id=1, source_target_pairs={{0,8},{1,9},{2,10},{3,11},{4,12},{5,13},{6,14},{7,15},{8,0},{9,1},... | collective-permute-start | bytes 786440 | tf_op jit(solution)/shard_map/ppermute | solution.py:41
  160.5 10.4 %collective-permute-start.41 = (bf16[64,2048]{1,0:T(8,128)(2,1)S(1)}, bf16[64,2048]{1,0:T(8,128)(2,1)S(1)}, u32[]{:S(2)}, u32[]{:S(2)}) collective-permute-start(bf16[64,2048]{1,0:T(8,128)(2,1)S(1)} %get-tuple-element.49), channel_id=1, source_target_pairs={{0,4},{1,5},{2,6},{3,7},{4,8},{5,9},{6,10},{7,11},{8,12},{9,13},{1... | collective-permute-start | bytes 786440 | tf_op jit(solution)/shard_map/ppermute | solution.py:41
  161.5 9.4 %collective-permute-start.42 = (bf16[64,2048]{1,0:T(8,128)(2,1)S(1)}, bf16[64,2048]{1,0:T(8,128)(2,1)S(1)}, u32[]{:S(2)}, u32[]{:S(2)}) collective-permute-start(bf16[64,2048]{1,0:T(8,128)(2,1)S(1)} %get-tuple-element.48), channel_id=1, source_target_pairs={{0,12},{1,13},{2,14},{3,15},{4,0},{5,1},{6,2},{7,3},{8,4},{9,5},{1... | collective-permute-start | bytes 786440 | tf_op jit(solution)/shard_map/ppermute | solution.py:41
  162.5 16.0 %copy-start.1 = (bf16[512,2048]{1,0:T(8,128)(2,1)S(1)}, bf16[512,2048]{1,0:T(8,128)(2,1)}, u32[]{:S(2)}) copy-start(bf16[512,2048]{1,0:T(8,128)(2,1)} %param.21) | copy-start | bytes 6291460
  163.9 8.8 %collective-permute-start.20 = (bf16[16,2048]{1,0:T(8,128)(2,1)S(1)}, bf16[16,2048]{1,0:T(8,128)(2,1)S(1)}, u32[]{:S(2)}, u32[]{:S(2)}) collective-permute-start(bf16[16,2048]{1,0:T(8,128)(2,1)S(1)} %get-tuple-element.55), channel_id=1, source_target_pairs={{0,2},{1,3},{2,0},{3,1},{4,6},{5,7},{6,4},{7,5},{8,10},{9,11},{10,... | collective-permute-start | bytes 196616 | tf_op jit(solution)/shard_map/ppermute | solution.py:48
  165.7 9.9 %collective-permute-start.21 = (bf16[16,2048]{1,0:T(8,128)(2,1)S(1)}, bf16[16,2048]{1,0:T(8,128)(2,1)S(1)}, u32[]{:S(2)}, u32[]{:S(2)}) collective-permute-start(bf16[16,2048]{1,0:T(8,128)(2,1)S(1)} %get-tuple-element.57), channel_id=1, source_target_pairs={{0,1},{1,2},{2,3},{3,0},{4,5},{5,6},{6,7},{7,4},{8,9},{9,10},{10,1... | collective-permute-start | bytes 196616 | tf_op jit(solution)/shard_map/ppermute | solution.py:48
  166.1 9.4 %collective-permute-start.22 = (bf16[16,2048]{1,0:T(8,128)(2,1)S(1)}, bf16[16,2048]{1,0:T(8,128)(2,1)S(1)}, u32[]{:S(2)}, u32[]{:S(2)}) collective-permute-start(bf16[16,2048]{1,0:T(8,128)(2,1)S(1)} %get-tuple-element.56), channel_id=1, source_target_pairs={{0,3},{1,0},{2,1},{3,2},{4,7},{5,4},{6,5},{7,6},{8,11},{9,8},{10,9... | collective-permute-start | bytes 196616 | tf_op jit(solution)/shard_map/ppermute | solution.py:48
  171.0 5.8 %collective-permute-start.43 = (bf16[16,2048]{1,0:T(8,128)(2,1)S(1)}, bf16[16,2048]{1,0:T(8,128)(2,1)S(1)}, u32[]{:S(2)}, u32[]{:S(2)}) collective-permute-start(bf16[16,2048]{1,0:T(8,128)(2,1)S(1)} %get-tuple-element.58), channel_id=1, source_target_pairs={{0,2},{1,3},{2,0},{3,1},{4,6},{5,7},{6,4},{7,5},{8,10},{9,11},{10,... | collective-permute-start | bytes 196616 | tf_op jit(solution)/shard_map/ppermute | solution.py:48
  172.3 5.5 %collective-permute-start.44 = (bf16[16,2048]{1,0:T(8,128)(2,1)S(1)}, bf16[16,2048]{1,0:T(8,128)(2,1)S(1)}, u32[]{:S(2)}, u32[]{:S(2)}) collective-permute-start(bf16[16,2048]{1,0:T(8,128)(2,1)S(1)} %get-tuple-element.60), channel_id=1, source_target_pairs={{0,1},{1,2},{2,3},{3,0},{4,5},{5,6},{6,7},{7,4},{8,9},{9,10},{10,1... | collective-permute-start | bytes 196616 | tf_op jit(solution)/shard_map/ppermute | solution.py:48
  172.7 5.1 %collective-permute-start.45 = (bf16[16,2048]{1,0:T(8,128)(2,1)S(1)}, bf16[16,2048]{1,0:T(8,128)(2,1)S(1)}, u32[]{:S(2)}, u32[]{:S(2)}) collective-permute-start(bf16[16,2048]{1,0:T(8,128)(2,1)S(1)} %get-tuple-element.59), channel_id=1, source_target_pairs={{0,3},{1,0},{2,1},{3,2},{4,7},{5,4},{6,5},{7,6},{8,11},{9,8},{10,9... | collective-permute-start | bytes 196616 | tf_op jit(solution)/shard_map/ppermute | solution.py:48

commit v4 on v3

--- a/solution.py
+++ b/solution.py
@@ -108,14 +108,20 @@
 def middle_kernel(part, far_one, far_two, far_three, resid, gain, payload, middle):
     chunk, width = part.shape
     piece = chunk // RING
-    for k in range(RING):
-        here = pl.ds(k * piece, piece)
+
+    @pl.loop(0, RING)
+    def _(k):
+        here = pl.ds(pl.multiple_of(k * piece, piece), piece)
         total = part[here, :] + resid[here, :].astype(F32)
         for d, other in enumerate((far_one, far_two, far_three)):
-            total = total + other[pl.ds((k - d - 1) % RING * piece, piece), :].astype(F32)
+            start = pl.multiple_of(lax.rem(k + RING - d - 1, RING) * piece, piece)
+            total = total + other[pl.ds(start, piece), :].astype(F32)
         rounded = total.astype(BF16)
-        if k == 0:
+
+        @pl.when(k == 0)
+        def _():
             middle[...] = rounded
+
         total = rounded.astype(F32)
         payload[here, :width] = (total * gain[...]).astype(BF16)
         payload[here, width:] = ends_of(jnp.sum(total * total, axis=1, keepdims=True))
@@ -135,10 +141,14 @@
     for i, payload in enumerate(payloads):
         here, there = pl.ds((RING + i) * half, half), pl.ds(i * half, half)
         for k, ref in enumerate((gate, upper)):
-            span = pl.ds(k * width, width)
-            payload[:, span] = (
-                ref[here, :].astype(F32) + other[there, span].astype(F32)
-            ).astype(BF16)
+
+            @pl.loop(0, width // (2 * HD))
+            def _(step):
+                start = pl.multiple_of(step * 2 * HD, 2 * HD)
+                span = pl.ds(k * width + start, 2 * HD)
+                total = ref[here, pl.ds(start, 2 * HD)].astype(F32) + other[there, span].astype(F32)
+                payload[:, span] = total.astype(BF16)
+
         both = ends[here, :].astype(F32) + other[there, 2 * width :].astype(F32)
         payload[:, 2 * width :] = ends_of(both[:, :1] + both[:, HD // 2 : HD // 2 + 1])
 
@@ -153,9 +163,14 @@
     ends = total(pl.ds(2 * width, HD))
     squares = ends[:, :1] + ends[:, HD // 2 : HD // 2 + 1]
     factor = lax.rsqrt(squares / model_width + 1e-05)
-    gate = total(pl.ds(0, width)) * factor
-    upper = total(pl.ds(width, width)) * factor
-    hidden[...] = (gate / (1.0 + jnp.exp(-gate)) * upper).astype(BF16)
+
+    @pl.loop(0, width // (2 * HD))
+    def _(step):
+        start = pl.multiple_of(step * 2 * HD, 2 * HD)
+        gate = total(pl.ds(start, 2 * HD)) * factor
+        upper = total(pl.ds(width + start, 2 * HD)) * factor
+        value = gate / (1.0 + jnp.exp(-gate)) * upper
+        hidden[:, pl.ds(start, 2 * HD)] = value.astype(BF16)
 
 
 def attend_slots(query_heads, key_rows, value_rows, cache_keys, cache_values, valid):
@@ -257,8 +272,14 @@
     far, near, inner = positions // chunk, (positions // piece) % RING, positions % piece
 
     def sum_first(values, weight):
-        total = pick(values, weight)
-        parts = {j: total[j * chunk : (j + 1) * chunk] for j in range(RING)}
+        cuts = 2 if weight is down_weight else 1
+        span = RING // cuts
+        parts = {}
+        for cut in range(cuts):
+            start = cut * span * chunk
+            total = pick(values[start : start + span * chunk], weight)
+            for j in range(span):
+                parts[cut * span + j] = total[j * chunk : (j + 1) * chunk]
         return add_up(parts[0], spread(send_first, parts))
 
     def rows_here(number):

time: 181 us -> 174 us (0.961)
  matrix products: 36.5 us -> 30.8 us
  Pallas kernels: 2.11 us -> 4.85 us
  waiting for transfers between devices: 52.7 us -> 50.1 us
  local copies, waits for them, and re-layouts: 6.3 us -> 3.76 us
  starting transfers between devices: 74.3 us -> 76.8 us
    dot_general x15 -> x19, matrix products: 32.4 us -> 26.6 us  [pick(): return jnp.dot(matrix, values, preferred_element_type=F32).astype(BF16)]
    pallas_call x8, Pallas kernels: 2.11 us -> 4.85 us  [local_kernel(): pl.pallas_call(body, out_shape=shapes, in_specs=[whole] * len(values), ou...]
  transfers between devices with their start and end apart: 48 -> 48, of which waited for: 21 -> 19; matrix products, arithmetic and copies ran while one was open for 18% -> 14% of each run, Pallas kernels for 1% -> 3%
where the time goes in v4:
time: 174 us; the launch traced here: 172 us
  starting transfers between devices  76.8 us (44%)
  waiting for transfers between devices  50.1 us (29%)
  matrix products  30.8 us (18%)
  Pallas kernels  4.85 us (3%)
  other arithmetic  4.59 us (3%)
  local copies, waits for them, and re-layouts  3.76 us (2%)
    ppermute x18, starting transfers between devices, send_first(): return lax.ppermute(value, AXES, pairs(move))  27.5 us
    dot_general x19, matrix products, pick(): return jnp.dot(matrix, values, preferred_element_type=F32).astype(BF16)  26.6 us
    ppermute x12, waiting for transfers between devices, send_z(): lax.ppermute(value, AXES, pairs(lambda x, y, z, core: (x, y, z + step, co...  17.4 us
    ppermute x12, starting transfers between devices, send_second(): return lax.ppermute(value, AXES, pairs(move))  17.1 us
    ppermute x12, starting transfers between devices, send_z(): lax.ppermute(value, AXES, pairs(lambda x, y, z, core: (x, y, z + step, co...  15.4 us
    ppermute x12, waiting for transfers between devices, send_second(): return lax.ppermute(value, AXES, pairs(move))  11.5 us
    all_to_all x1, waiting for transfers between devices, on_device(): lax.all_to_all(outgoing.reshape(count_gx * count_yz, per_device, head_wid...  9.53 us
    all_to_all x1, starting transfers between devices, on_device(): lax.all_to_all(outgoing.reshape(count_gx * count_yz, per_device, head_wid...  8.57 us
  transfers between devices with their start and end apart: 48, of which 19 were waited for; matrix products, arithmetic and copies ran while one was open for 14% of the time, Pallas kernels for 3%

profile of v4, /device:TPU:6, one launch (start us, length us, event | category | flops | bytes accessed | tf_op | source)
XLA Modules:
  0.0 171.6 jit_solution(16961127870721142402)
XLA Ops:
  0.0 1.4 convolution_convert_fusion.16
  1.5 1.0 convolution_convert_fusion.18
  2.6 1.0 convolution_convert_fusion.17
  4.4 7.4 %all-to-all-start = ((bf16[16,4,576]{2,1,0:T(4,128)(2,1)}), bf16[16,4,576]{2,1,0:T(4,128)(2,1)S(1)}, u32[]{:S(2)}, u32[]{:S(2)}) async-start(bf16[16,4,576]{2,1,0:T(4,128)(2,1)} %all_to_all.9), calls=%async_computation | async-start | bytes 163840 | tf_op jit(solution)/shard_map/all_to_all | solution.py:239
  12.9 4.6 %all-to-all-done = bf16[16,4,576]{2,1,0:T(4,128)(2,1)S(1)} async-done(((bf16[16,4,576]{2,1,0:T(4,128)(2,1)}), bf16[16,4,576]{2,1,0:T(4,128)(2,1)S(1)}, u32[]{:S(2)}, u32[]{:S(2)}) %all-to-all-start) | async-done | bytes 73760 | tf_op jit(solution)/shard_map/all_to_all | solution.py:239
  17.9 2.1 %fusion.106 = (f32[4,4,16]{2,1,0:T(4,128)S(1)}, f32[4,4,16,384]{3,2,1,0:T(8,128)S(1)}) fusion(bf16[4,4,16,128]{3,2,1,0:T(8,128)(2,1)S(1)} %bitcast.63, pred[4,384]{1,0:T(4,128)(4,1)S(1)} %iota_compare_fusion.11, bf16[4,384,512]{2,1,0:T(8,128)(2,1)} %param.17), kind=kOutput, calls=%fused_computation.205 | convolution fusion | flops 25460480 | bytes 2034176 | tf_op jit(solution)/shard_map/bkgd,bckd->bkgc/dot_general | solution.py:183
  20.4 1.9 %fusion.15 = bf16[4,4,16,128]{3,2,1,0:T(8,128)(2,1)S(1)} fusion(f32[4,4,16,384]{3,2,1,0:T(8,128)S(1)} %get-tuple-element.64, f32[4,4,16]{2,1,0:T(4,128)S(1)} %get-tuple-element.62, f32[4,4,16]{2,1,0:T(4,128)S(1)} %multiply_maximum_fusion, f32[4,4,128]{2,1,0:T(4,128)S(1)} %reshape.172, f32[4,4,16]{2,1,0:T(4,128)S(1)} %get-tuple-element.61, ...), kind=kOutput, calls=%fused_computation.25 | convolution fusion | flops 25559040 | bytes 2042880 | tf_op jit(solution)/shard_map/bkgc,bckd->bkgd/dot_general | solution.py:196
  22.4 1.0 broadcast_in_dim.55
  23.4 8.6 %all-to-all-start.1 = ((bf16[128,4,512]{2,1,0:T(4,128)(2,1)}), bf16[128,4,512]{2,1,0:T(4,128)(2,1)S(1)}, u32[]{:S(2)}, u32[]{:S(2)}) async-start(bf16[128,4,512]{2,1,0:T(4,128)(2,1)} %bitcast.8), calls=%async_computation.1 | async-start | bytes 1048576 | tf_op jit(solution)/shard_map/all_to_all | solution.py:259
  32.3 2.1 %convolution_convert_fusion.14 = bf16[128,2048]{1,0:T(8,128)(2,1)S(1)} fusion(bf16[512,2048]{1,0:T(8,128)(2,1)} %param.13, s32[128]{0:T(128)S(1)} %pad_add_fusion.2), kind=kOutput, calls=%fused_computation.14 | convolution fusion | flops 268763136 | bytes 2621952 | tf_op jit(solution)/shard_map/dot_general | solution.py:86
  34.4 9.5 %all-to-all-done.1 = bf16[128,4,512]{2,1,0:T(4,128)(2,1)S(1)} async-done(((bf16[128,4,512]{2,1,0:T(4,128)(2,1)}), bf16[128,4,512]{2,1,0:T(4,128)(2,1)S(1)}, u32[]{:S(2)}, u32[]{:S(2)}) %all-to-all-start.1) | async-done | bytes 524320 | tf_op jit(solution)/shard_map/all_to_all | solution.py:259
  43.9 1.0 reshape.171
  44.9 1.5 convolution_convert_fusion.15
  47.9 2.8 %collective-permute-start = (bf16[64,2048]{1,0:T(8,128)(2,1)S(1)}, bf16[64,2048]{1,0:T(8,128)(2,1)S(1)}, u32[]{:S(2)}, u32[]{:S(2)}) collective-permute-start(bf16[64,2048]{1,0:T(8,128)(2,1)S(1)} %get-tuple-element.41), channel_id=1, source_target_pairs={{0,8},{1,9},{2,10},{3,11},{4,12},{5,13},{6,14},{7,15},{8,0},{9,1},... | collective-permute-start | bytes 786440 | tf_op jit(solution)/shard_map/ppermute | solution.py:41
  51.6 1.1 collective-permute-start.2
  52.8 1.0 collective-permute-start.23
  53.8 2.6 %collective-permute-start.24 = (bf16[64,2048]{1,0:T(8,128)(2,1)S(1)}, bf16[64,2048]{1,0:T(8,128)(2,1)S(1)}, u32[]{:S(2)}, u32[]{:S(2)}) collective-permute-start(bf16[64,2048]{1,0:T(8,128)(2,1)S(1)} %get-tuple-element.46), channel_id=1, source_target_pairs={{0,4},{1,5},{2,6},{3,7},{4,8},{5,9},{6,10},{7,11},{8,12},{9,13},{1... | collective-permute-start | bytes 786440 | tf_op jit(solution)/shard_map/ppermute | solution.py:41
  56.9 1.8 %collective-permute-done.1 = bf16[64,2048]{1,0:T(8,128)(2,1)S(1)} collective-permute-done((bf16[64,2048]{1,0:T(8,128)(2,1)S(1)}, bf16[64,2048]{1,0:T(8,128)(2,1)S(1)}, u32[]{:S(2)}, u32[]{:S(2)}) %collective-permute-start.1) | collective-permute-done | bytes 262176 | tf_op jit(solution)/shard_map/ppermute | solution.py:41
  58.8 3.2 %collective-permute-done.2 = bf16[64,2048]{1,0:T(8,128)(2,1)S(1)} collective-permute-done((bf16[64,2048]{1,0:T(8,128)(2,1)S(1)}, bf16[64,2048]{1,0:T(8,128)(2,1)S(1)}, u32[]{:S(2)}, u32[]{:S(2)}) %collective-permute-start.2) | collective-permute-done | bytes 262176 | tf_op jit(solution)/shard_map/ppermute | solution.py:41
  62.9 2.7 %collective-permute-start.4 = (bf16[64,2048]{1,0:T(8,128)(2,1)}, bf16[64,2048]{1,0:T(8,128)(2,1)S(1)}, u32[]{:S(2)}, u32[]{:S(2)}) collective-permute-start(bf16[64,2048]{1,0:T(8,128)(2,1)} %get-tuple-element.31), channel_id=1, source_target_pairs={{0,2},{1,3},{2,0},{3,1},{4,6},{5,7},{6,4},{7,5},{8,10},{9,11},{10,... | collective-permute-start | bytes 786440 | tf_op jit(solution)/shard_map/ppermute | solution.py:48
  65.6 1.0 collective-permute-done.25
  67.4 2.3 %collective-permute-start.26 = (bf16[64,2048]{1,0:T(8,128)(2,1)}, bf16[64,2048]{1,0:T(8,128)(2,1)S(1)}, u32[]{:S(2)}, u32[]{:S(2)}) collective-permute-start(bf16[64,2048]{1,0:T(8,128)(2,1)} %get-tuple-element.39), channel_id=1, source_target_pairs={{0,3},{1,0},{2,1},{3,2},{4,7},{5,4},{6,5},{7,6},{8,11},{9,8},{10,9... | collective-permute-start | bytes 786440 | tf_op jit(solution)/shard_map/ppermute | solution.py:48
  70.1 1.4 collective-permute-start.28
  71.5 2.3 %collective-permute-done.5.far_three = bf16[64,2048]{1,0:T(8,128)(2,1)S(1)} collective-permute-done((bf16[64,2048]{1,0:T(8,128)(2,1)}, bf16[64,2048]{1,0:T(8,128)(2,1)S(1)}, u32[]{:S(2)}, u32[]{:S(2)}) %collective-permute-start.5) | collective-permute-done | bytes 262176 | tf_op jit(solution)/shard_map/ppermute | solution.py:48
  74.3 1.7 collective-permute-start.7
  76.3 3.2 %collective-permute-start.8 = (bf16[64,2176]{1,0:T(8,128)(2,1)S(1)}, bf16[64,2176]{1,0:T(8,128)(2,1)S(1)}, u32[]{:S(2)}, u32[]{:S(2)}) collective-permute-start(bf16[64,2176]{1,0:T(8,128)(2,1)S(1)} %get-tuple-element.18), channel_id=1, source_target_pairs={{0,4},{1,5},{2,6},{3,7},{4,8},{5,9},{6,10},{7,11},{8,12},{9,13},{1... | collective-permute-start | bytes 835592 | tf_op jit(solution)/shard_map/ppermute | solution.py:41
  79.8 6.5 %collective-permute-done.28.far_three = bf16[64,2048]{1,0:T(8,128)(2,1)S(1)} collective-permute-done((bf16[64,2048]{1,0:T(8,128)(2,1)}, bf16[64,2048]{1,0:T(8,128)(2,1)S(1)}, u32[]{:S(2)}, u32[]{:S(2)}) %collective-permute-start.28) | collective-permute-done | bytes 262176 | tf_op jit(solution)/shard_map/ppermute | solution.py:48
  87.5 2.5 %collective-permute-start.30 = (bf16[64,2176]{1,0:T(8,128)(2,1)S(1)}, bf16[64,2176]{1,0:T(8,128)(2,1)S(1)}, u32[]{:S(2)}, u32[]{:S(2)}) collective-permute-start(bf16[64,2176]{1,0:T(8,128)(2,1)S(1)} %get-tuple-element.24), channel_id=1, source_target_pairs={{0,8},{1,9},{2,10},{3,11},{4,12},{5,13},{6,14},{7,15},{8,0},{9,1},... | collective-permute-start | bytes 835592 | tf_op jit(solution)/shard_map/ppermute | solution.py:41
  90.0 1.4 collective-permute-start.31
  92.0 5.5 %convolution_convert_fusion.5.upper = bf16[256,1792]{1,0:T(8,128)(2,1)S(1)} fusion(bf16[2048,1792]{1,0:T(8,128)(2,1)} %param.24, bf16[256,2176]{1,0:T(8,128)(2,1)S(1)} %convolution_convert_fusion.1), kind=kOutput, calls=%fused_computation.5 | convolution fusion | flops 1879506944 | bytes 9306112 | tf_op jit(solution)/shard_map/dot_general | solution.py:86
  97.5 2.1 %convolution_convert_fusion.6.gate = bf16[256,1792]{1,0:T(8,128)(2,1)S(1)} fusion(bf16[2048,1792]{1,0:T(8,128)(2,1)S(1)} %bitcast.70, bf16[256,2176]{1,0:T(8,128)(2,1)S(1)} %convolution_convert_fusion.1), kind=kOutput, calls=%fused_computation.6 | convolution fusion | flops 1879506944 | bytes 9306112 | tf_op jit(solution)/shard_map/dot_general | solution.py:86
  100.4 2.1 %convolution_convert_fusion.2.upper = bf16[256,1792]{1,0:T(8,128)(2,1)S(1)} fusion(bf16[2048,1792]{1,0:T(8,128)(2,1)S(1)} %bitcast.68, bf16[256,2176]{1,0:T(8,128)(2,1)S(1)} %convolution_convert_fusion), kind=kOutput, calls=%fused_computation.2 | convolution fusion | flops 1879506944 | bytes 9306112 | tf_op jit(solution)/shard_map/dot_general | solution.py:86
  102.5 2.1 %convolution_convert_fusion.3.gate = bf16[256,1792]{1,0:T(8,128)(2,1)S(1)} fusion(bf16[2048,1792]{1,0:T(8,128)(2,1)S(1)} %bitcast.70, bf16[256,2176]{1,0:T(8,128)(2,1)S(1)} %convolution_convert_fusion), kind=kOutput, calls=%fused_computation.3 | convolution fusion | flops 1879506944 | bytes 9306112 | tf_op jit(solution)/shard_map/dot_general | solution.py:86
  105.2 1.1 shard_map.129
  106.3 1.3 collective-permute-start.10
  108.3 2.6 %collective-permute-start.12 = (bf16[32,3712]{1,0:T(8,128)(2,1)S(1)}, bf16[32,3712]{1,0:T(8,128)(2,1)S(1)}, u32[]{:S(2)}, u32[]{:S(2)}) collective-permute-start(bf16[32,3712]{1,0:T(8,128)(2,1)S(1)} %get-tuple-element.22), channel_id=1, source_target_pairs={{0,96},{1,97},{2,98},{3,99},{4,100},{5,101},{6,102},{7,103},{8,104... | collective-permute-start | bytes 712712 | tf_op jit(solution)/shard_map/ppermute | solution.py:52
  110.9 1.1 shard_map.133
  112.0 1.0 collective-permute-start.33
  113.0 1.1 collective-permute-start.34
  114.2 2.4 %collective-permute-done.10.one = bf16[32,3712]{1,0:T(8,128)(2,1)S(1)} collective-permute-done((bf16[32,3712]{1,0:T(8,128)(2,1)S(1)}, bf16[32,3712]{1,0:T(8,128)(2,1)S(1)}, u32[]{:S(2)}, u32[]{:S(2)}) %collective-permute-start.10) | collective-permute-done | bytes 237600 | tf_op jit(solution)/shard_map/ppermute | solution.py:52
  116.5 1.0 collective-permute-start.35
  117.6 4.1 %collective-permute-done.11.two = bf16[32,3712]{1,0:T(8,128)(2,1)S(1)} collective-permute-done((bf16[32,3712]{1,0:T(8,128)(2,1)S(1)}, bf16[32,3712]{1,0:T(8,128)(2,1)S(1)}, u32[]{:S(2)}, u32[]{:S(2)}) %collective-permute-start.11) | collective-permute-done | bytes 237600 | tf_op jit(solution)/shard_map/ppermute | solution.py:52
  122.4 1.1 collective-permute-start.13
  123.6 2.1 %collective-permute-start.14 = (bf16[32,1792]{1,0:T(8,128)(2,1)S(1)}, bf16[32,1792]{1,0:T(8,128)(2,1)S(1)}, u32[]{:S(2)}, u32[]{:S(2)}) collective-permute-start(bf16[32,1792]{1,0:T(8,128)(2,1)S(1)} %shard_map.130), channel_id=1, source_target_pairs={{0,64},{1,65},{2,66},{3,67},{4,68},{5,69},{6,70},{7,71},{8,72},{9,... | collective-permute-start | bytes 344072 | tf_op jit(solution)/shard_map/ppermute | solution.py:52
  125.7 1.1 collective-permute-done.33.one
  126.8 1.1 collective-permute-start.15
  127.9 4.0 %collective-permute-done.34.two = bf16[32,3712]{1,0:T(8,128)(2,1)S(1)} collective-permute-done((bf16[32,3712]{1,0:T(8,128)(2,1)S(1)}, bf16[32,3712]{1,0:T(8,128)(2,1)S(1)}, u32[]{:S(2)}, u32[]{:S(2)}) %collective-permute-start.34) | collective-permute-done | bytes 237600 | tf_op jit(solution)/shard_map/ppermute | solution.py:52
  133.2 1.7 collective-permute-start.37
  135.0 0.9 collective-permute-start.38
  136.0 2.7 %collective-permute-done.36 = bf16[32,1792]{1,0:T(8,128)(2,1)S(1)} collective-permute-done((bf16[32,1792]{1,0:T(8,128)(2,1)S(1)}, bf16[32,1792]{1,0:T(8,128)(2,1)S(1)}, u32[]{:S(2)}, u32[]{:S(2)}) %collective-permute-start.36) | collective-permute-done | bytes 114720 | tf_op jit(solution)/shard_map/ppermute | solution.py:52
  138.7 1.8 %collective-permute-done.37 = bf16[32,1792]{1,0:T(8,128)(2,1)S(1)} collective-permute-done((bf16[32,1792]{1,0:T(8,128)(2,1)S(1)}, bf16[32,1792]{1,0:T(8,128)(2,1)S(1)}, u32[]{:S(2)}, u32[]{:S(2)}) %collective-permute-start.37) | collective-permute-done | bytes 114720 | tf_op jit(solution)/shard_map/ppermute | solution.py:52
  140.5 1.4 collective-permute-done.38
  142.7 1.1 convolution_convert_fusion.12
  143.8 1.6 collective-permute-start.17
  145.6 1.1 convolution_convert_fusion.13
  146.8 3.1 %collective-permute-start.18 = (bf16[64,2048]{1,0:T(8,128)(2,1)S(1)}, bf16[64,2048]{1,0:T(8,128)(2,1)S(1)}, u32[]{:S(2)}, u32[]{:S(2)}) collective-permute-start(bf16[64,2048]{1,0:T(8,128)(2,1)S(1)} %slice.202), channel_id=1, source_target_pairs={{0,4},{1,5},{2,6},{3,7},{4,8},{5,9},{6,10},{7,11},{8,12},{9,13},{1... | collective-permute-start | bytes 786440 | tf_op jit(solution)/shard_map/ppermute | solution.py:41
  150.4 1.1 convolution_convert_fusion.10
  153.0 1.1 convolution_convert_fusion.11
  154.2 2.8 %collective-permute-start.41 = (bf16[64,2048]{1,0:T(8,128)(2,1)S(1)}, bf16[64,2048]{1,0:T(8,128)(2,1)S(1)}, u32[]{:S(2)}, u32[]{:S(2)}) collective-permute-start(bf16[64,2048]{1,0:T(8,128)(2,1)S(1)} %slice.220), channel_id=1, source_target_pairs={{0,4},{1,5},{2,6},{3,7},{4,8},{5,9},{6,10},{7,11},{8,12},{9,13},{1... | collective-permute-start | bytes 786440 | tf_op jit(solution)/shard_map/ppermute | solution.py:41
  157.1 1.8 %collective-permute-start.20 = (bf16[16,2048]{1,0:T(8,128)(2,1)S(1)}, bf16[16,2048]{1,0:T(8,128)(2,1)S(1)}, u32[]{:S(2)}, u32[]{:S(2)}) collective-permute-start(bf16[16,2048]{1,0:T(8,128)(2,1)S(1)} %get-tuple-element.53), channel_id=1, source_target_pairs={{0,2},{1,3},{2,0},{3,1},{4,6},{5,7},{6,4},{7,5},{8,10},{9,11},{10,... | collective-permute-start | bytes 196616 | tf_op jit(solution)/shard_map/ppermute | solution.py:48
  159.6 2.6 %collective-permute-start.22 = (bf16[16,2048]{1,0:T(8,128)(2,1)S(1)}, bf16[16,2048]{1,0:T(8,128)(2,1)S(1)}, u32[]{:S(2)}, u32[]{:S(2)}) collective-permute-start(bf16[16,2048]{1,0:T(8,128)(2,1)S(1)} %get-tuple-element.54), channel_id=1, source_target_pairs={{0,3},{1,0},{2,1},{3,2},{4,7},{5,4},{6,5},{7,6},{8,11},{9,8},{10,9... | collective-permute-start | bytes 196616 | tf_op jit(solution)/shard_map/ppermute | solution.py:48
  162.7 2.8 %collective-permute-start.43 = (bf16[16,2048]{1,0:T(8,128)(2,1)S(1)}, bf16[16,2048]{1,0:T(8,128)(2,1)S(1)}, u32[]{:S(2)}, u32[]{:S(2)}) collective-permute-start(bf16[16,2048]{1,0:T(8,128)(2,1)S(1)} %get-tuple-element.56), channel_id=1, source_target_pairs={{0,2},{1,3},{2,0},{3,1},{4,6},{5,7},{6,4},{7,5},{8,10},{9,11},{10,... | collective-permute-start | bytes 196616 | tf_op jit(solution)/shard_map/ppermute | solution.py:48
  165.4 3.2 %collective-permute-start.45 = (bf16[16,2048]{1,0:T(8,128)(2,1)S(1)}, bf16[16,2048]{1,0:T(8,128)(2,1)S(1)}, u32[]{:S(2)}, u32[]{:S(2)}) collective-permute-start(bf16[16,2048]{1,0:T(8,128)(2,1)S(1)} %get-tuple-element.57), channel_id=1, source_target_pairs={{0,3},{1,0},{2,1},{3,2},{4,7},{5,4},{6,5},{7,6},{8,11},{9,8},{10,9... | collective-permute-start | bytes 196616 | tf_op jit(solution)/shard_map/ppermute | solution.py:48
  168.7 2.2 %collective-permute-done.44 = bf16[16,2048]{1,0:T(8,128)(2,1)S(1)} collective-permute-done((bf16[16,2048]{1,0:T(8,128)(2,1)S(1)}, bf16[16,2048]{1,0:T(8,128)(2,1)S(1)}, u32[]{:S(2)}, u32[]{:S(2)}) %collective-permute-start.44) | collective-permute-done | bytes 65568 | tf_op jit(solution)/shard_map/ppermute | solution.py:48
  (149 shorter events, 20.3 us)
Async XLA Ops:
  0.0 46.4 %copy-start = (bf16[512,2048]{1,0:T(8,128)(2,1)S(1)}, bf16[512,2048]{1,0:T(8,128)(2,1)}, u32[]{:S(2)}) copy-start(bf16[512,2048]{1,0:T(8,128)(2,1)} %param.21) | copy-start | bytes 6291460
  4.4 13.1 %all-to-all-start = ((bf16[16,4,576]{2,1,0:T(4,128)(2,1)}), bf16[16,4,576]{2,1,0:T(4,128)(2,1)S(1)}, u32[]{:S(2)}, u32[]{:S(2)}) async-start(bf16[16,4,576]{2,1,0:T(4,128)(2,1)} %all_to_all.9), calls=%async_computation | async-start | bytes 163840 | tf_op jit(solution)/shard_map/all_to_all | solution.py:239
  20.4 11.6 %copy-start.3 = (s32[512]{0:T(512)S(1)}, s32[512]{0:T(512)}, u32[]{:S(2)}) copy-start(s32[512]{0:T(512)} %param.20) | copy-start | bytes 6148
  23.4 20.5 %all-to-all-start.1 = ((bf16[128,4,512]{2,1,0:T(4,128)(2,1)}), bf16[128,4,512]{2,1,0:T(4,128)(2,1)S(1)}, u32[]{:S(2)}, u32[]{:S(2)}) async-start(bf16[128,4,512]{2,1,0:T(4,128)(2,1)} %bitcast.8), calls=%async_computation.1 | async-start | bytes 1048576 | tf_op jit(solution)/shard_map/all_to_all | solution.py:259
  47.9 8.5 %collective-permute-start = (bf16[64,2048]{1,0:T(8,128)(2,1)S(1)}, bf16[64,2048]{1,0:T(8,128)(2,1)S(1)}, u32[]{:S(2)}, u32[]{:S(2)}) collective-permute-start(bf16[64,2048]{1,0:T(8,128)(2,1)S(1)} %get-tuple-element.41), channel_id=1, source_target_pairs={{0,8},{1,9},{2,10},{3,11},{4,12},{5,13},{6,14},{7,15},{8,0},{9,1},... | collective-permute-start | bytes 786440 | tf_op jit(solution)/shard_map/ppermute | solution.py:41
  50.8 8.0 %collective-permute-start.1 = (bf16[64,2048]{1,0:T(8,128)(2,1)S(1)}, bf16[64,2048]{1,0:T(8,128)(2,1)S(1)}, u32[]{:S(2)}, u32[]{:S(2)}) collective-permute-start(bf16[64,2048]{1,0:T(8,128)(2,1)S(1)} %get-tuple-element.43), channel_id=1, source_target_pairs={{0,4},{1,5},{2,6},{3,7},{4,8},{5,9},{6,10},{7,11},{8,12},{9,13},{1... | collective-permute-start | bytes 786440 | tf_op jit(solution)/shard_map/ppermute | solution.py:41
  51.6 10.4 %collective-permute-start.2 = (bf16[64,2048]{1,0:T(8,128)(2,1)S(1)}, bf16[64,2048]{1,0:T(8,128)(2,1)S(1)}, u32[]{:S(2)}, u32[]{:S(2)}) collective-permute-start(bf16[64,2048]{1,0:T(8,128)(2,1)S(1)} %get-tuple-element.42), channel_id=1, source_target_pairs={{0,12},{1,13},{2,14},{3,15},{4,0},{5,1},{6,2},{7,3},{8,4},{9,5},{1... | collective-permute-start | bytes 786440 | tf_op jit(solution)/shard_map/ppermute | solution.py:41
  52.8 12.7 %collective-permute-start.23 = (bf16[64,2048]{1,0:T(8,128)(2,1)S(1)}, bf16[64,2048]{1,0:T(8,128)(2,1)S(1)}, u32[]{:S(2)}, u32[]{:S(2)}) collective-permute-start(bf16[64,2048]{1,0:T(8,128)(2,1)S(1)} %get-tuple-element.44), channel_id=1, source_target_pairs={{0,8},{1,9},{2,10},{3,11},{4,12},{5,13},{6,14},{7,15},{8,0},{9,1},... | collective-permute-start | bytes 786440 | tf_op jit(solution)/shard_map/ppermute | solution.py:41
  53.8 11.8 %collective-permute-start.24 = (bf16[64,2048]{1,0:T(8,128)(2,1)S(1)}, bf16[64,2048]{1,0:T(8,128)(2,1)S(1)}, u32[]{:S(2)}, u32[]{:S(2)}) collective-permute-start(bf16[64,2048]{1,0:T(8,128)(2,1)S(1)} %get-tuple-element.46), channel_id=1, source_target_pairs={{0,4},{1,5},{2,6},{3,7},{4,8},{5,9},{6,10},{7,11},{8,12},{9,13},{1... | collective-permute-start | bytes 786440 | tf_op jit(solution)/shard_map/ppermute | solution.py:41
  56.4 17.3 %copy-start.2 = (f32[2048]{0:T(1024)S(1)}, f32[2048]{0:T(1024)}, u32[]{:S(2)}) copy-start(f32[2048]{0:T(1024)} %param.22) | copy-start | bytes 24580
  56.4 10.1 %collective-permute-start.25 = (bf16[64,2048]{1,0:T(8,128)(2,1)S(1)}, bf16[64,2048]{1,0:T(8,128)(2,1)S(1)}, u32[]{:S(2)}, u32[]{:S(2)}) collective-permute-start(bf16[64,2048]{1,0:T(8,128)(2,1)S(1)} %get-tuple-element.45), channel_id=1, source_target_pairs={{0,12},{1,13},{2,14},{3,15},{4,0},{5,1},{6,2},{7,3},{8,4},{9,5},{1... | collective-permute-start | bytes 786440 | tf_op jit(solution)/shard_map/ppermute | solution.py:41
  62.9 7.2 %collective-permute-start.3 = (bf16[64,2048]{1,0:T(8,128)(2,1)}, bf16[64,2048]{1,0:T(8,128)(2,1)S(1)}, u32[]{:S(2)}, u32[]{:S(2)}) collective-permute-start(bf16[64,2048]{1,0:T(8,128)(2,1)} %get-tuple-element.31), channel_id=1, source_target_pairs={{0,3},{1,0},{2,1},{3,2},{4,7},{5,4},{6,5},{7,6},{8,11},{9,8},{10,9... | collective-permute-start | bytes 786440 | tf_op jit(solution)/shard_map/ppermute | solution.py:48
  62.9 8.6 %collective-permute-start.4 = (bf16[64,2048]{1,0:T(8,128)(2,1)}, bf16[64,2048]{1,0:T(8,128)(2,1)S(1)}, u32[]{:S(2)}, u32[]{:S(2)}) collective-permute-start(bf16[64,2048]{1,0:T(8,128)(2,1)} %get-tuple-element.31), channel_id=1, source_target_pairs={{0,2},{1,3},{2,0},{3,1},{4,6},{5,7},{6,4},{7,5},{8,10},{9,11},{10,... | collective-permute-start | bytes 786440 | tf_op jit(solution)/shard_map/ppermute | solution.py:48
  65.6 8.2 %collective-permute-start.5 = (bf16[64,2048]{1,0:T(8,128)(2,1)}, bf16[64,2048]{1,0:T(8,128)(2,1)S(1)}, u32[]{:S(2)}, u32[]{:S(2)}) collective-permute-start(bf16[64,2048]{1,0:T(8,128)(2,1)} %get-tuple-element.31), channel_id=1, source_target_pairs={{0,1},{1,2},{2,3},{3,0},{4,5},{5,6},{6,7},{7,4},{8,9},{9,10},{10,1... | collective-permute-start | bytes 786440 | tf_op jit(solution)/shard_map/ppermute | solution.py:48
  67.4 8.9 %collective-permute-start.26 = (bf16[64,2048]{1,0:T(8,128)(2,1)}, bf16[64,2048]{1,0:T(8,128)(2,1)S(1)}, u32[]{:S(2)}, u32[]{:S(2)}) collective-permute-start(bf16[64,2048]{1,0:T(8,128)(2,1)} %get-tuple-element.39), channel_id=1, source_target_pairs={{0,3},{1,0},{2,1},{3,2},{4,7},{5,4},{6,5},{7,6},{8,11},{9,8},{10,9... | collective-permute-start | bytes 786440 | tf_op jit(solution)/shard_map/ppermute | solution.py:48
  69.8 10.1 %collective-permute-start.27 = (bf16[64,2048]{1,0:T(8,128)(2,1)}, bf16[64,2048]{1,0:T(8,128)(2,1)S(1)}, u32[]{:S(2)}, u32[]{:S(2)}) collective-permute-start(bf16[64,2048]{1,0:T(8,128)(2,1)} %get-tuple-element.39), channel_id=1, source_target_pairs={{0,2},{1,3},{2,0},{3,1},{4,6},{5,7},{6,4},{7,5},{8,10},{9,11},{10,... | collective-permute-start | bytes 786440 | tf_op jit(solution)/shard_map/ppermute | solution.py:48
  70.1 16.2 %collective-permute-start.28 = (bf16[64,2048]{1,0:T(8,128)(2,1)}, bf16[64,2048]{1,0:T(8,128)(2,1)S(1)}, u32[]{:S(2)}, u32[]{:S(2)}) collective-permute-start(bf16[64,2048]{1,0:T(8,128)(2,1)} %get-tuple-element.39), channel_id=1, source_target_pairs={{0,1},{1,2},{2,3},{3,0},{4,5},{5,6},{6,7},{7,4},{8,9},{9,10},{10,1... | collective-permute-start | bytes 786440 | tf_op jit(solution)/shard_map/ppermute | solution.py:48
  74.3 15.7 %collective-permute-start.6 = (bf16[64,2176]{1,0:T(8,128)(2,1)S(1)}, bf16[64,2176]{1,0:T(8,128)(2,1)S(1)}, u32[]{:S(2)}, u32[]{:S(2)}) collective-permute-start(bf16[64,2176]{1,0:T(8,128)(2,1)S(1)} %get-tuple-element.18), channel_id=1, source_target_pairs={{0,12},{1,13},{2,14},{3,15},{4,0},{5,1},{6,2},{7,3},{8,4},{9,5},{1... | collective-permute-start | bytes 835592 | tf_op jit(solution)/shard_map/ppermute | solution.py:41
  74.3 17.1 %collective-permute-start.7 = (bf16[64,2176]{1,0:T(8,128)(2,1)S(1)}, bf16[64,2176]{1,0:T(8,128)(2,1)S(1)}, u32[]{:S(2)}, u32[]{:S(2)}) collective-permute-start(bf16[64,2176]{1,0:T(8,128)(2,1)S(1)} %get-tuple-element.18), channel_id=1, source_target_pairs={{0,8},{1,9},{2,10},{3,11},{4,12},{5,13},{6,14},{7,15},{8,0},{9,1},... | collective-permute-start | bytes 835592 | tf_op jit(solution)/shard_map/ppermute | solution.py:41
  76.3 15.1 %collective-permute-start.8 = (bf16[64,2176]{1,0:T(8,128)(2,1)S(1)}, bf16[64,2176]{1,0:T(8,128)(2,1)S(1)}, u32[]{:S(2)}, u32[]{:S(2)}) collective-permute-start(bf16[64,2176]{1,0:T(8,128)(2,1)S(1)} %get-tuple-element.18), channel_id=1, source_target_pairs={{0,4},{1,5},{2,6},{3,7},{4,8},{5,9},{6,10},{7,11},{8,12},{9,13},{1... | collective-permute-start | bytes 835592 | tf_op jit(solution)/shard_map/ppermute | solution.py:41
  86.9 12.9 %collective-permute-start.29 = (bf16[64,2176]{1,0:T(8,128)(2,1)S(1)}, bf16[64,2176]{1,0:T(8,128)(2,1)S(1)}, u32[]{:S(2)}, u32[]{:S(2)}) collective-permute-start(bf16[64,2176]{1,0:T(8,128)(2,1)S(1)} %get-tuple-element.24), channel_id=1, source_target_pairs={{0,12},{1,13},{2,14},{3,15},{4,0},{5,1},{6,2},{7,3},{8,4},{9,5},{1... | collective-permute-start | bytes 835592 | tf_op jit(solution)/shard_map/ppermute | solution.py:41
  87.5 12.3 %collective-permute-start.30 = (bf16[64,2176]{1,0:T(8,128)(2,1)S(1)}, bf16[64,2176]{1,0:T(8,128)(2,1)S(1)}, u32[]{:S(2)}, u32[]{:S(2)}) collective-permute-start(bf16[64,2176]{1,0:T(8,128)(2,1)S(1)} %get-tuple-element.24), channel_id=1, source_target_pairs={{0,8},{1,9},{2,10},{3,11},{4,12},{5,13},{6,14},{7,15},{8,0},{9,1},... | collective-permute-start | bytes 835592 | tf_op jit(solution)/shard_map/ppermute | solution.py:41
  90.0 9.8 %collective-permute-start.31 = (bf16[64,2176]{1,0:T(8,128)(2,1)S(1)}, bf16[64,2176]{1,0:T(8,128)(2,1)S(1)}, u32[]{:S(2)}, u32[]{:S(2)}) collective-permute-start(bf16[64,2176]{1,0:T(8,128)(2,1)S(1)} %get-tuple-element.24), channel_id=1, source_target_pairs={{0,4},{1,5},{2,6},{3,7},{4,8},{5,9},{6,10},{7,11},{8,12},{9,13},{1... | collective-permute-start | bytes 835592 | tf_op jit(solution)/shard_map/ppermute | solution.py:41
  91.4 6.0 %slice-start.4 = ((s8[7340032]{0:T(1024)(128)(4,1)}), s8[4194304]{0:T(1024)(128)(4,1)S(1)}, s32[]{:S(2)}) async-start(s8[7340032]{0:T(1024)(128)(4,1)} %bitcast.69), calls=%async_computation.6 | async-start | bytes 8388608
  92.0 5.5 %slice-start.5 = ((s8[7340032]{0:T(1024)(128)(4,1)}), s8[3145728]{0:T(1024)(128)(4,1)S(1)}, s32[]{:S(2)}) async-start(s8[7340032]{0:T(1024)(128)(4,1)} %bitcast.69), calls=%async_computation.7 | async-start | bytes 6291456
  92.0 8.4 %slice-start.2 = ((s8[7340032]{0:T(1024)(128)(4,1)}), s8[4194304]{0:T(1024)(128)(4,1)S(1)}, s32[]{:S(2)}) async-start(s8[7340032]{0:T(1024)(128)(4,1)} %bitcast.67), calls=%async_computation.4 | async-start | bytes 8388608
  97.5 2.9 %slice-start.3 = ((s8[7340032]{0:T(1024)(128)(4,1)}), s8[3145728]{0:T(1024)(128)(4,1)S(1)}, s32[]{:S(2)}) async-start(s8[7340032]{0:T(1024)(128)(4,1)} %bitcast.67), calls=%async_computation.5 | async-start | bytes 6291456
  99.7 5.6 %collective-permute-start.9 = (bf16[128,3712]{1,0:T(8,128)(2,1)S(1)}, bf16[128,3712]{1,0:T(8,128)(2,1)S(1)}, u32[]{:S(2)}, u32[]{:S(2)}) collective-permute-start(bf16[128,3712]{1,0:T(8,128)(2,1)S(1)} %shard_map.128), channel_id=1, source_target_pairs={{0,16},{1,17},{2,18},{3,19},{4,20},{5,21},{6,22},{7,23},{8,24},{9,... | collective-permute-start | bytes 2850824 | tf_op jit(solution)/shard_map/ppermute | solution.py:56
  104.6 38.0 %slice-start = ((s8[7340032]{0:T(1024)(128)(4,1)}), s8[4194304]{0:T(1024)(128)(4,1)S(1)}, s32[]{:S(2)}) async-start(s8[7340032]{0:T(1024)(128)(4,1)} %bitcast.60), calls=%async_computation.2 | async-start | bytes 8388608
  104.7 6.2 %collective-permute-start.32 = (bf16[128,3712]{1,0:T(8,128)(2,1)S(1)}, bf16[128,3712]{1,0:T(8,128)(2,1)S(1)}, u32[]{:S(2)}, u32[]{:S(2)}) collective-permute-start(bf16[128,3712]{1,0:T(8,128)(2,1)S(1)} %shard_map.132), channel_id=1, source_target_pairs={{0,16},{1,17},{2,18},{3,19},{4,20},{5,21},{6,22},{7,23},{8,24},{9,... | collective-permute-start | bytes 2850824 | tf_op jit(solution)/shard_map/ppermute | solution.py:56
  106.3 10.2 %collective-permute-start.10 = (bf16[32,3712]{1,0:T(8,128)(2,1)S(1)}, bf16[32,3712]{1,0:T(8,128)(2,1)S(1)}, u32[]{:S(2)}, u32[]{:S(2)}) collective-permute-start(bf16[32,3712]{1,0:T(8,128)(2,1)S(1)} %get-tuple-element.20), channel_id=1, source_target_pairs={{0,64},{1,65},{2,66},{3,67},{4,68},{5,69},{6,70},{7,71},{8,72},{9,... | collective-permute-start | bytes 712712 | tf_op jit(solution)/shard_map/ppermute | solution.py:52
  107.7 14.0 %collective-permute-start.11 = (bf16[32,3712]{1,0:T(8,128)(2,1)S(1)}, bf16[32,3712]{1,0:T(8,128)(2,1)S(1)}, u32[]{:S(2)}, u32[]{:S(2)}) collective-permute-start(bf16[32,3712]{1,0:T(8,128)(2,1)S(1)} %get-tuple-element.21), channel_id=1, source_target_pairs={{0,32},{1,33},{2,34},{3,35},{4,36},{5,37},{6,38},{7,39},{8,40},{9,... | collective-permute-start | bytes 712712 | tf_op jit(solution)/shard_map/ppermute | solution.py:52
  108.3 13.4 %collective-permute-start.12 = (bf16[32,3712]{1,0:T(8,128)(2,1)S(1)}, bf16[32,3712]{1,0:T(8,128)(2,1)S(1)}, u32[]{:S(2)}, u32[]{:S(2)}) collective-permute-start(bf16[32,3712]{1,0:T(8,128)(2,1)S(1)} %get-tuple-element.22), channel_id=1, source_target_pairs={{0,96},{1,97},{2,98},{3,99},{4,100},{5,101},{6,102},{7,103},{8,104... | collective-permute-start | bytes 712712 | tf_op jit(solution)/shard_map/ppermute | solution.py:52
  112.0 30.6 %slice-start.1 = ((s8[7340032]{0:T(1024)(128)(4,1)}), s8[3145728]{0:T(1024)(128)(4,1)S(1)}, s32[]{:S(2)}) async-start(s8[7340032]{0:T(1024)(128)(4,1)} %bitcast.60), calls=%async_computation.3 | async-start | bytes 6291456
  112.0 14.8 %collective-permute-start.33 = (bf16[32,3712]{1,0:T(8,128)(2,1)S(1)}, bf16[32,3712]{1,0:T(8,128)(2,1)S(1)}, u32[]{:S(2)}, u32[]{:S(2)}) collective-permute-start(bf16[32,3712]{1,0:T(8,128)(2,1)S(1)} %get-tuple-element.26), channel_id=1, source_target_pairs={{0,64},{1,65},{2,66},{3,67},{4,68},{5,69},{6,70},{7,71},{8,72},{9,... | collective-permute-start | bytes 712712 | tf_op jit(solution)/shard_map/ppermute | solution.py:52
  113.0 18.8 %collective-permute-start.34 = (bf16[32,3712]{1,0:T(8,128)(2,1)S(1)}, bf16[32,3712]{1,0:T(8,128)(2,1)S(1)}, u32[]{:S(2)}, u32[]{:S(2)}) collective-permute-start(bf16[32,3712]{1,0:T(8,128)(2,1)S(1)} %get-tuple-element.27), channel_id=1, source_target_pairs={{0,32},{1,33},{2,34},{3,35},{4,36},{5,37},{6,38},{7,39},{8,40},{9,... | collective-permute-start | bytes 712712 | tf_op jit(solution)/shard_map/ppermute | solution.py:52
  116.5 15.3 %collective-permute-start.35 = (bf16[32,3712]{1,0:T(8,128)(2,1)S(1)}, bf16[32,3712]{1,0:T(8,128)(2,1)S(1)}, u32[]{:S(2)}, u32[]{:S(2)}) collective-permute-start(bf16[32,3712]{1,0:T(8,128)(2,1)S(1)} %get-tuple-element.28), channel_id=1, source_target_pairs={{0,96},{1,97},{2,98},{3,99},{4,100},{5,101},{6,102},{7,103},{8,104... | collective-permute-start | bytes 712712 | tf_op jit(solution)/shard_map/ppermute | solution.py:52
  122.4 12.5 %collective-permute-start.13 = (bf16[32,1792]{1,0:T(8,128)(2,1)S(1)}, bf16[32,1792]{1,0:T(8,128)(2,1)S(1)}, u32[]{:S(2)}, u32[]{:S(2)}) collective-permute-start(bf16[32,1792]{1,0:T(8,128)(2,1)S(1)} %shard_map.130), channel_id=1, source_target_pairs={{0,96},{1,97},{2,98},{3,99},{4,100},{5,101},{6,102},{7,103},{8,104... | collective-permute-start | bytes 344072 | tf_op jit(solution)/shard_map/ppermute | solution.py:52
  123.6 12.3 %collective-permute-start.14 = (bf16[32,1792]{1,0:T(8,128)(2,1)S(1)}, bf16[32,1792]{1,0:T(8,128)(2,1)S(1)}, u32[]{:S(2)}, u32[]{:S(2)}) collective-permute-start(bf16[32,1792]{1,0:T(8,128)(2,1)S(1)} %shard_map.130), channel_id=1, source_target_pairs={{0,64},{1,65},{2,66},{3,67},{4,68},{5,69},{6,70},{7,71},{8,72},{9,... | collective-permute-start | bytes 344072 | tf_op jit(solution)/shard_map/ppermute | solution.py:52
  126.8 9.1 %collective-permute-start.15 = (bf16[32,1792]{1,0:T(8,128)(2,1)S(1)}, bf16[32,1792]{1,0:T(8,128)(2,1)S(1)}, u32[]{:S(2)}, u32[]{:S(2)}) collective-permute-start(bf16[32,1792]{1,0:T(8,128)(2,1)S(1)} %shard_map.130), channel_id=1, source_target_pairs={{0,32},{1,33},{2,34},{3,35},{4,36},{5,37},{6,38},{7,39},{8,40},{9,... | collective-permute-start | bytes 344072 | tf_op jit(solution)/shard_map/ppermute | solution.py:52
  132.6 6.1 %collective-permute-start.36 = (bf16[32,1792]{1,0:T(8,128)(2,1)S(1)}, bf16[32,1792]{1,0:T(8,128)(2,1)S(1)}, u32[]{:S(2)}, u32[]{:S(2)}) collective-permute-start(bf16[32,1792]{1,0:T(8,128)(2,1)S(1)} %shard_map.134), channel_id=1, source_target_pairs={{0,96},{1,97},{2,98},{3,99},{4,100},{5,101},{6,102},{7,103},{8,104... | collective-permute-start | bytes 344072 | tf_op jit(solution)/shard_map/ppermute | solution.py:52
  133.2 7.2 %collective-permute-start.37 = (bf16[32,1792]{1,0:T(8,128)(2,1)S(1)}, bf16[32,1792]{1,0:T(8,128)(2,1)S(1)}, u32[]{:S(2)}, u32[]{:S(2)}) collective-permute-start(bf16[32,1792]{1,0:T(8,128)(2,1)S(1)} %shard_map.134), channel_id=1, source_target_pairs={{0,64},{1,65},{2,66},{3,67},{4,68},{5,69},{6,70},{7,71},{8,72},{9,... | collective-permute-start | bytes 344072 | tf_op jit(solution)/shard_map/ppermute | solution.py:52
  135.0 6.9 %collective-permute-start.38 = (bf16[32,1792]{1,0:T(8,128)(2,1)S(1)}, bf16[32,1792]{1,0:T(8,128)(2,1)S(1)}, u32[]{:S(2)}, u32[]{:S(2)}) collective-permute-start(bf16[32,1792]{1,0:T(8,128)(2,1)S(1)} %shard_map.134), channel_id=1, source_target_pairs={{0,32},{1,33},{2,34},{3,35},{4,36},{5,37},{6,38},{7,39},{8,40},{9,... | collective-permute-start | bytes 344072 | tf_op jit(solution)/shard_map/ppermute | solution.py:52
  135.9 6.2 %collective-permute-start.16 = (bf16[128,1792]{1,0:T(8,128)(2,1)S(1)}, bf16[128,1792]{1,0:T(8,128)(2,1)S(1)}, u32[]{:S(2)}, u32[]{:S(2)}) collective-permute-start(bf16[128,1792]{1,0:T(8,128)(2,1)S(1)} %pad_maximum_fusion), channel_id=1, source_target_pairs={{0,16},{1,17},{2,18},{3,19},{4,20},{5,21},{6,22},{7,23},{8,24},{9,... | collective-permute-start | bytes 1376264 | tf_op jit(solution)/shard_map/ppermute | solution.py:56
  141.9 8.0 %collective-permute-start.39 = (bf16[128,1792]{1,0:T(8,128)(2,1)S(1)}, bf16[128,1792]{1,0:T(8,128)(2,1)S(1)}, u32[]{:S(2)}, u32[]{:S(2)}) collective-permute-start(bf16[128,1792]{1,0:T(8,128)(2,1)S(1)} %pad_maximum_fusion.1), channel_id=1, source_target_pairs={{0,16},{1,17},{2,18},{3,19},{4,20},{5,21},{6,22},{7,23},{8,24},{9,... | collective-permute-start | bytes 1376264 | tf_op jit(solution)/shard_map/ppermute | solution.py:56
  143.8 10.3 %collective-permute-start.17 = (bf16[64,2048]{1,0:T(8,128)(2,1)S(1)}, bf16[64,2048]{1,0:T(8,128)(2,1)S(1)}, u32[]{:S(2)}, u32[]{:S(2)}) collective-permute-start(bf16[64,2048]{1,0:T(8,128)(2,1)S(1)} %get-tuple-element.47), channel_id=1, source_target_pairs={{0,8},{1,9},{2,10},{3,11},{4,12},{5,13},{6,14},{7,15},{8,0},{9,1},... | collective-permute-start | bytes 786440 | tf_op jit(solution)/shard_map/ppermute | solution.py:41
  145.4 11.5 %collective-permute-start.19 = (bf16[64,2048]{1,0:T(8,128)(2,1)S(1)}, bf16[64,2048]{1,0:T(8,128)(2,1)S(1)}, u32[]{:S(2)}, u32[]{:S(2)}) collective-permute-start(bf16[64,2048]{1,0:T(8,128)(2,1)S(1)} %get-tuple-element.48), channel_id=1, source_target_pairs={{0,12},{1,13},{2,14},{3,15},{4,0},{5,1},{6,2},{7,3},{8,4},{9,5},{1... | collective-permute-start | bytes 786440 | tf_op jit(solution)/shard_map/ppermute | solution.py:41
  146.8 10.1 %collective-permute-start.18 = (bf16[64,2048]{1,0:T(8,128)(2,1)S(1)}, bf16[64,2048]{1,0:T(8,128)(2,1)S(1)}, u32[]{:S(2)}, u32[]{:S(2)}) collective-permute-start(bf16[64,2048]{1,0:T(8,128)(2,1)S(1)} %slice.202), channel_id=1, source_target_pairs={{0,4},{1,5},{2,6},{3,7},{4,8},{5,9},{6,10},{7,11},{8,12},{9,13},{1... | collective-permute-start | bytes 786440 | tf_op jit(solution)/shard_map/ppermute | solution.py:41
  151.5 8.1 %collective-permute-start.40 = (bf16[64,2048]{1,0:T(8,128)(2,1)S(1)}, bf16[64,2048]{1,0:T(8,128)(2,1)S(1)}, u32[]{:S(2)}, u32[]{:S(2)}) collective-permute-start(bf16[64,2048]{1,0:T(8,128)(2,1)S(1)} %get-tuple-element.51), channel_id=1, source_target_pairs={{0,8},{1,9},{2,10},{3,11},{4,12},{5,13},{6,14},{7,15},{8,0},{9,1},... | collective-permute-start | bytes 786440 | tf_op jit(solution)/shard_map/ppermute | solution.py:41
  152.4 10.0 %collective-permute-start.42 = (bf16[64,2048]{1,0:T(8,128)(2,1)S(1)}, bf16[64,2048]{1,0:T(8,128)(2,1)S(1)}, u32[]{:S(2)}, u32[]{:S(2)}) collective-permute-start(bf16[64,2048]{1,0:T(8,128)(2,1)S(1)} %get-tuple-element.52), channel_id=1, source_target_pairs={{0,12},{1,13},{2,14},{3,15},{4,0},{5,1},{6,2},{7,3},{8,4},{9,5},{1... | collective-permute-start | bytes 786440 | tf_op jit(solution)/shard_map/ppermute | solution.py:41
  154.2 8.3 %collective-permute-start.41 = (bf16[64,2048]{1,0:T(8,128)(2,1)S(1)}, bf16[64,2048]{1,0:T(8,128)(2,1)S(1)}, u32[]{:S(2)}, u32[]{:S(2)}) collective-permute-start(bf16[64,2048]{1,0:T(8,128)(2,1)S(1)} %slice.220), channel_id=1, source_target_pairs={{0,4},{1,5},{2,6},{3,7},{4,8},{5,9},{6,10},{7,11},{8,12},{9,13},{1... | collective-permute-start | bytes 786440 | tf_op jit(solution)/shard_map/ppermute | solution.py:41
  156.9 14.7 %copy-start.1 = (bf16[512,2048]{1,0:T(8,128)(2,1)S(1)}, bf16[512,2048]{1,0:T(8,128)(2,1)}, u32[]{:S(2)}) copy-start(bf16[512,2048]{1,0:T(8,128)(2,1)} %param.21) | copy-start | bytes 6291460
  157.1 8.3 %collective-permute-start.20 = (bf16[16,2048]{1,0:T(8,128)(2,1)S(1)}, bf16[16,2048]{1,0:T(8,128)(2,1)S(1)}, u32[]{:S(2)}, u32[]{:S(2)}) collective-permute-start(bf16[16,2048]{1,0:T(8,128)(2,1)S(1)} %get-tuple-element.53), channel_id=1, source_target_pairs={{0,2},{1,3},{2,0},{3,1},{4,6},{5,7},{6,4},{7,5},{8,10},{9,11},{10,... | collective-permute-start | bytes 196616 | tf_op jit(solution)/shard_map/ppermute | solution.py:48
  158.9 9.7 %collective-permute-start.21 = (bf16[16,2048]{1,0:T(8,128)(2,1)S(1)}, bf16[16,2048]{1,0:T(8,128)(2,1)S(1)}, u32[]{:S(2)}, u32[]{:S(2)}) collective-permute-start(bf16[16,2048]{1,0:T(8,128)(2,1)S(1)} %get-tuple-element.55), channel_id=1, source_target_pairs={{0,1},{1,2},{2,3},{3,0},{4,5},{5,6},{6,7},{7,4},{8,9},{9,10},{10,1... | collective-permute-start | bytes 196616 | tf_op jit(solution)/shard_map/ppermute | solution.py:48
  159.6 9.1 %collective-permute-start.22 = (bf16[16,2048]{1,0:T(8,128)(2,1)S(1)}, bf16[16,2048]{1,0:T(8,128)(2,1)S(1)}, u32[]{:S(2)}, u32[]{:S(2)}) collective-permute-start(bf16[16,2048]{1,0:T(8,128)(2,1)S(1)} %get-tuple-element.54), channel_id=1, source_target_pairs={{0,3},{1,0},{2,1},{3,2},{4,7},{5,4},{6,5},{7,6},{8,11},{9,8},{10,9... | collective-permute-start | bytes 196616 | tf_op jit(solution)/shard_map/ppermute | solution.py:48
  162.7 6.1 %collective-permute-start.43 = (bf16[16,2048]{1,0:T(8,128)(2,1)S(1)}, bf16[16,2048]{1,0:T(8,128)(2,1)S(1)}, u32[]{:S(2)}, u32[]{:S(2)}) collective-permute-start(bf16[16,2048]{1,0:T(8,128)(2,1)S(1)} %get-tuple-element.56), channel_id=1, source_target_pairs={{0,2},{1,3},{2,0},{3,1},{4,6},{5,7},{6,4},{7,5},{8,10},{9,11},{10,... | collective-permute-start | bytes 196616 | tf_op jit(solution)/shard_map/ppermute | solution.py:48
  165.4 5.5 %collective-permute-start.44 = (bf16[16,2048]{1,0:T(8,128)(2,1)S(1)}, bf16[16,2048]{1,0:T(8,128)(2,1)S(1)}, u32[]{:S(2)}, u32[]{:S(2)}) collective-permute-start(bf16[16,2048]{1,0:T(8,128)(2,1)S(1)} %get-tuple-element.58), channel_id=1, source_target_pairs={{0,1},{1,2},{2,3},{3,0},{4,5},{5,6},{6,7},{7,4},{8,9},{9,10},{10,1... | collective-permute-start | bytes 196616 | tf_op jit(solution)/shard_map/ppermute | solution.py:48
  165.4 5.5 %collective-permute-start.45 = (bf16[16,2048]{1,0:T(8,128)(2,1)S(1)}, bf16[16,2048]{1,0:T(8,128)(2,1)S(1)}, u32[]{:S(2)}, u32[]{:S(2)}) collective-permute-start(bf16[16,2048]{1,0:T(8,128)(2,1)S(1)} %get-tuple-element.57), channel_id=1, source_target_pairs={{0,3},{1,0},{2,1},{3,2},{4,7},{5,4},{6,5},{7,6},{8,11},{9,8},{10,9... | collective-permute-start | bytes 196616 | tf_op jit(solution)/shard_map/ppermute | solution.py:48
